TPU v7x, 256 devices: a whole 4x4x8 slice. The times are simulated.
256 devices in a mesh: tile: 128 (over y, x, z_lo, core), mp: 2 (over z_hi).
Axes of the slice: x: 4, y: 4, z: 8 (z_hi: 2, z_lo: 4; z = z_hi * 4 + z_lo), core: 2. Of those that a mesh axis runs over, the one named last changes fastest.
Arguments:
- feat_cot: bfloat16 [512, 1024, 128], P(None, 'tile'), may hold values from -6 to 6
- latent: bfloat16 [16, 1024, 128], P(None, 'tile'), may hold values from -6 to 6
- dec_w1: bfloat16 [9, 512, 16], replicated, may hold values from -0.5 to 0.5
- dec_w2: bfloat16 [9, 512, 512], replicated, may hold values from -0.09375 to 0.09375
- hidden: bfloat16 [32768, 3072], P('tile', 'mp'), may hold values from -840 to 840
- modulation: bfloat16 [16, 2, 3072], P(None, None, 'mp'), may hold values from -3 to 3
- prompt_ids: int32 [8], replicated, may hold values from 0 to 15
- step_size: float32 [8], replicated, may hold values from 0.1 to 1
- proj_w: bfloat16 [3072, 64], P('mp'), may hold values from -0.75 to 0.75
Outputs:
- grad_hidden: bfloat16 [32768, 3072], P('tile', 'mp')
- grad_proj: float32 [3072, 64], P('mp')
- grad_mod: float32 [8, 2, 3072], P(None, None, 'mp')
All inputs are finite; a program needn't handle non-finite values.
Results may differ from a plain program's by a relative error of at most 0.008.
Values may be sent and summed in bfloat16 or wider, within the bound.
No kernel may reach another device: no remote copies, remote signals or barrier semaphores. Data moves between devices by JAX's collectives and lax.ppermute only.
A program may use at most 128 MiB of HBM per device.

v0:
```python
import jax
import jax.numpy as jnp
from jax import lax
from jax.sharding import PartitionSpec as P


def padded_2(block, sides, width):
    for axis, dim in sides:
        count = lax.axis_size(axis)
        forward = [(i, i + 1) for i in range(count - 1)]
        forward.append((count - 1, 0))
        backward = [(target, source) for source, target in forward]
        low = lax.ppermute(
            lax.slice_in_dim(block, block.shape[dim] - width, None, axis=dim), axis, forward
        )
        high = lax.ppermute(lax.slice_in_dim(block, 0, width, axis=dim), axis, backward)
        block = jnp.concatenate([low, block, high], axis=dim)
    return block


def silu_grad(values):
    sigm = jax.nn.sigmoid(values)
    return sigm * (1.0 + values * (1.0 - sigm))


def conv_forward(padded, weight):
    out_rows = padded.shape[1] - 2
    width = padded.shape[2]
    widened = jnp.pad(padded, ((0, 0), (0, 0), (1, 1)))
    result = jnp.zeros((weight.shape[1], out_rows, width), jnp.float32)
    for kernel_tap in range(9):
        row_off, col_off = (kernel_tap // 3, kernel_tap % 3)
        result = result + jnp.einsum(
            "oc,crw->orw",
            weight[kernel_tap],
            widened[:, row_off : row_off + out_rows, col_off : col_off + width],
            preferred_element_type=jnp.float32,
        )
    return result


def conv_backward(padded, weight):
    out_rows = padded.shape[1] - 2
    width = padded.shape[2]
    widened = jnp.pad(padded, ((0, 0), (0, 0), (1, 1)))
    result = jnp.zeros((weight.shape[2], out_rows, width), jnp.float32)
    for kernel_tap in range(9):
        row_off, col_off = (kernel_tap // 3, kernel_tap % 3)
        result = result + jnp.einsum(
            "oc,orw->crw",
            weight[kernel_tap],
            widened[:, 2 - row_off : 2 - row_off + out_rows, 2 - col_off : 2 - col_off + width],
            preferred_element_type=jnp.float32,
        )
    return result


def keep_rows(values, extent, own_rows, image_side):
    row_start = (lax.axis_index("tile") * own_rows + image_side // 2) % image_side
    position = row_start - extent + jnp.arange(values.shape[1])
    inside = (position >= 0) & (position < image_side)
    return jnp.where(inside[None, :, None], values, jnp.zeros((), values.dtype))


def body(feat_cot, latent, dec_w1, dec_w2, hidden, modulation, prompt_ids, step_size, proj_w):
    own_rows = latent.shape[1]
    image_side = latent.shape[2]
    channels = latent.shape[0]
    latent_pad = keep_rows(padded_2(latent, (("tile", 1),), 1), 1, own_rows, image_side)
    pre_one = conv_forward(latent_pad, dec_w1)
    act_one = jax.nn.silu(pre_one).astype(jnp.bfloat16)
    act_pad = keep_rows(padded_2(act_one, (("tile", 1),), 1), 1, own_rows, image_side)
    pre_two = conv_forward(act_pad, dec_w2)
    grad_two = (feat_cot * silu_grad(pre_two)).astype(jnp.bfloat16)
    grad_pad = keep_rows(padded_2(grad_two, (("tile", 1),), 1), 1, own_rows, image_side)
    grad_one = (conv_backward(grad_pad, dec_w2) * silu_grad(pre_one)).astype(jnp.bfloat16)
    inner_pad = keep_rows(padded_2(grad_one, (("tile", 1),), 1), 1, own_rows, image_side)
    grad_latent = conv_backward(inner_pad, dec_w1)
    token_rows = own_rows // 2
    half_side = image_side // 2
    tokens_grad = (
        grad_latent.reshape(channels, token_rows, 2, half_side, 2)
        .transpose(1, 3, 0, 2, 4)
        .reshape(token_rows * half_side, 4 * channels)
    )
    image_count = prompt_ids.shape[0]
    image_index = (lax.axis_index("tile") * own_rows + image_side // 2) // image_side % image_count
    image_hit = jnp.arange(image_count) == image_index
    image_pick = image_hit.astype(jnp.float32)
    step_now = jnp.sum(image_pick * step_size)
    prompt_now = jnp.sum(jnp.where(image_hit, prompt_ids, 0))
    prompt_pick = (jnp.arange(modulation.shape[0]) == prompt_now).astype(jnp.float32)
    mod_now = jnp.einsum("p,pkd->kd", prompt_pick, modulation.astype(jnp.float32))
    grad_velocity = (tokens_grad * -step_now).astype(jnp.bfloat16)
    width_all = lax.axis_size("mp") * hidden.shape[1]
    states = hidden.astype(jnp.float32)
    sum_first, sum_second = lax.psum(
        (jnp.sum(states, axis=1), jnp.sum(states * states, axis=1)), "mp"
    )
    mean_val = sum_first / width_all
    spread = sum_second / width_all - mean_val * mean_val
    sigma = jnp.sqrt(spread + 1e-06)
    normed = (states - mean_val[:, None]) / sigma[:, None]
    modulated = (normed * (1.0 + mod_now[1]) + mod_now[0]).astype(jnp.bfloat16)
    proj_part = jnp.einsum(
        "td,tp->dp", modulated, grad_velocity, preferred_element_type=jnp.float32
    )
    grad_modulated = jnp.einsum(
        "tp,dp->td", grad_velocity, proj_w, preferred_element_type=jnp.float32
    )
    mod_part = jnp.stack(
        [jnp.sum(grad_modulated, axis=0), jnp.sum(grad_modulated * normed, axis=0)]
    )
    mod_spread = image_pick[:, None, None] * mod_part[None, :, :]
    grad_proj, grad_mod = lax.psum((proj_part, mod_spread), "tile")
    grad_normed = grad_modulated * (1.0 + mod_now[1])
    back_first, back_second = lax.psum(
        (jnp.sum(grad_normed, axis=1), jnp.sum(grad_normed * normed, axis=1)), "mp"
    )
    first_mean = back_first / width_all
    second_mean = back_second / width_all
    grad_hidden = (
        (grad_normed - first_mean[:, None] - normed * second_mean[:, None]) / sigma[:, None]
    ).astype(jnp.bfloat16)
    return (grad_hidden, grad_proj, grad_mod)


def solution(mesh):
    return jax.shard_map(
        body,
        mesh=mesh,
        in_specs=(
            P(None, "tile", None),
            P(None, "tile", None),
            P(),
            P(),
            P("tile", "mp"),
            P(None, None, "mp"),
            P(),
            P(),
            P("mp", None),
        ),
        out_specs=(P("tile", "mp"), P("mp", None), P(None, None, "mp")),
        check_vma=False,
    )
```

profile of v0, /device:TPU:1, one launch (start us, length us, event | category | flops | bytes accessed | tf_op | source)
XLA Modules:
  0.0 1313.5 jit_solution(3819517730603394169)
XLA Ops:
  7.2 0.8 copy.26
  8.1 3.1 collective-permute-start
  11.5 1.5 convert_reduce_fusion
  13.0 1.3 select_reduce_fusion
  14.3 1.6 copy.25
  15.9 8.0 all-reduce.6
  28.3 1.4 fusion.11
  29.7 2.7 collective-permute-start.2
  32.4 6.2 collective-permute-start.3
  38.6 0.8 fusion.146
  39.8 0.7 fusion.116
  40.6 0.7 fusion.124
  41.3 0.7 fusion.73
  42.1 0.7 fusion.75
  42.8 0.7 fusion.77
  43.6 0.7 fusion.79
  44.3 0.7 fusion.81
  45.1 0.7 fusion.83
  45.8 1.8 fusion.7
  47.8 9.5 collective-permute-start.5
  60.6 0.7 fusion.63
  62.0 0.7 fusion.67
  64.2 1.6 fusion
  65.9 10.4 collective-permute-start.7
  81.5 0.8 multiply_reduce_fusion
  82.4 1.3 fusion.85
  83.7 0.7 broadcast_multiply_fusion
  84.4 7.7 all-reduce.5
  92.1 1.4 divide_convert_fusion
  93.5 1209.8 %all-reduce.9.cloned.1.call-done = (f32[1536,64]{0,1:T(8,128)}, f32[8,2,1536]{2,1,0:T(2,128)}) async-done(((f32[1536,64]{0,1:T(8,128)}, f32[8,2,1536]{2,1,0:T(2,128)}), (f32[1536,64]{0,1:T(8,128)}, f32[8,2,1536]{2,1,0:T(2,128)})) %all-reduce.9.cloned.1.call-update) | async-done | bytes 491536 | tf_op jit(solution)/shard_map/psum | solution.py:115
  1303.3 1.8 copy.57
  1305.1 1.5 copy.58
  (72 shorter events, 15.5 us)
Async XLA Ops:
  7.2 74.4 %copy-start = (bf16[1536,64]{0,1:T(8,128)(2,1)S(1)}, bf16[1536,64]{0,1:T(8,128)(2,1)}, u32[]{:S(2)}) copy-start(bf16[1536,64]{0,1:T(8,128)(2,1)} %param.17) | copy-start | bytes 589828
  7.2 16.8 %copy-start.2 = (bf16[9,512,16]{1,2,0:T(8,128)(2,1)S(1)}, bf16[9,512,16]{1,2,0:T(8,128)(2,1)}, u32[]{:S(2)}) copy-start(bf16[9,512,16]{1,2,0:T(8,128)(2,1)} %param.11) | copy-start | bytes 442372
  7.2 1296.1 %all-reduce.9.cloned.1.call-start = ((), (), s32[]{:S(2)}) async-start(), calls=%async_computation | async-start | bytes 983040 | tf_op jit(solution)/shard_map/psum | solution.py:115
  8.1 15.9 %collective-permute-start = (bf16[16,1,128]{2,0,1:T(8,128)(2,1)S(1)}, bf16[16,1,128]{2,0,1:T(8,128)(2,1)S(1)}, u32[]{:S(2)}, u32[]{:S(2)}) collective-permute-start(bf16[16,1,128]{2,0,1:T(8,128)(2,1)S(1)} %get-tuple-element.23), channel_id=1, source_target_pairs={{0,2},{2,4},{4,6},{6,8},{8,10},{10,12},{12,14},{14,16},{16,18},{18... | collective-permute-start | bytes 12296 | tf_op jit(solution)/shard_map/ppermute | solution.py:13
  11.2 12.8 collective-permute-start.1
  27.8 12.0 slice-start
  28.3 10.3 copy-start.3
  28.3 11.5 slice-start.1
  29.7 9.6 collective-permute-start.2
  32.4 7.1 collective-permute-start.3
  45.8 11.4 copy-start.4
  47.7 10.2 collective-permute-start.4
  47.8 10.4 collective-permute-start.5
  65.8 11.2 collective-permute-start.6
  65.9 11.4 collective-permute-start.7
  80.2 1.3 copy-start.1
Sparse Core Ops, SparseCore 0:
  84.6 1218.7 all-reduce.8
where the time goes:
time: 1320 us; the launch traced here: 1310 us
  waiting for transfers between devices  1210 us (92%)
  starting transfers between devices  32.3 us (2%)
  matrix products  27.1 us (2%)
  blocking collectives  15.7 us (1%)
  between operations  15 us (1%)
    psum x1, waiting for transfers between devices, body(): grad_proj, grad_mod = lax.psum((proj_part, mod_spread), 'tile')  1210 us
  transfers between devices with their start and end apart: 9, of which 4 were waited for; matrix products, arithmetic and copies ran while one was open for 1% of the time, Pallas kernels for 0%

commit v1 on v0

v1 whole, which is shorter than its diff:
```python
import jax
import jax.numpy as jnp
from jax import lax
from jax.sharding import Mesh, PartitionSpec as P

BF = jnp.bfloat16
F32 = jnp.float32
TILE = ("y", "x", "zl", "core")


def padded_2(block, sides, width):
    for axis, dim in sides:
        count = lax.axis_size(axis)
        forward = [(i, i + 1) for i in range(count - 1)]
        forward.append((count - 1, 0))
        backward = [(target, source) for source, target in forward]
        low = lax.ppermute(
            lax.slice_in_dim(block, block.shape[dim] - width, None, axis=dim), axis, forward
        )
        high = lax.ppermute(lax.slice_in_dim(block, 0, width, axis=dim), axis, backward)
        block = jnp.concatenate([low, block, high], axis=dim)
    return block


def silu_grad(values):
    sigm = jax.nn.sigmoid(values)
    return sigm * (1.0 + values * (1.0 - sigm))


def conv_forward(padded, weight):
    out_rows = padded.shape[1] - 2
    width = padded.shape[2]
    widened = jnp.pad(padded, ((0, 0), (0, 0), (1, 1)))
    result = jnp.zeros((weight.shape[1], out_rows, width), F32)
    for kernel_tap in range(9):
        row_off, col_off = (kernel_tap // 3, kernel_tap % 3)
        result = result + jnp.einsum(
            "oc,crw->orw",
            weight[kernel_tap],
            widened[:, row_off : row_off + out_rows, col_off : col_off + width],
            preferred_element_type=F32,
        )
    return result


def conv_backward(padded, weight):
    out_rows = padded.shape[1] - 2
    width = padded.shape[2]
    widened = jnp.pad(padded, ((0, 0), (0, 0), (1, 1)))
    result = jnp.zeros((weight.shape[2], out_rows, width), F32)
    for kernel_tap in range(9):
        row_off, col_off = (kernel_tap // 3, kernel_tap % 3)
        result = result + jnp.einsum(
            "oc,orw->crw",
            weight[kernel_tap],
            widened[:, 2 - row_off : 2 - row_off + out_rows, 2 - col_off : 2 - col_off + width],
            preferred_element_type=F32,
        )
    return result


def keep_rows(values, extent, own_rows, image_side):
    row_start = (lax.axis_index(TILE) * own_rows + image_side // 2) % image_side
    position = row_start - extent + jnp.arange(values.shape[1])
    inside = (position >= 0) & (position < image_side)
    return jnp.where(inside[None, :, None], values, jnp.zeros((), values.dtype))


def sum_over_tile(part):
    half = part.shape[1] // 2
    core = lax.axis_index("core")
    swap = [(0, 1), (1, 0)]
    keep = lax.dynamic_slice_in_dim(part, core * half, half, 1)
    send = lax.dynamic_slice_in_dim(part, (1 - core) * half, half, 1)
    total = keep + lax.ppermute(send.astype(BF), "core", swap).astype(F32)
    for axis in ("zl", "x", "y"):
        count = lax.axis_size(axis)
        out = total.astype(BF)
        came = [
            lax.ppermute(out, axis, [(i, (i + d) % count) for i in range(count)])
            for d in range(1, count)
        ]
        for block in came:
            total = total + block.astype(F32)
    mine = total.astype(BF)
    other = lax.ppermute(mine, "core", swap)
    return jnp.where(
        core == 0,
        jnp.concatenate([mine, other], axis=1),
        jnp.concatenate([other, mine], axis=1),
    )


def body(feat_cot, latent, dec_w1, dec_w2, hidden, modulation, prompt_ids, step_size, proj_w):
    own_rows = latent.shape[1]
    image_side = latent.shape[2]
    channels = latent.shape[0]
    image_count = prompt_ids.shape[0]
    features = hidden.shape[1]
    image_index = (lax.axis_index(TILE) * own_rows + image_side // 2) // image_side % image_count
    image_hit = jnp.arange(image_count) == image_index
    image_pick = image_hit.astype(F32)
    step_now = jnp.sum(image_pick * step_size)
    prompt_now = jnp.sum(jnp.where(image_hit, prompt_ids, 0))
    mod_now = lax.dynamic_index_in_dim(modulation, prompt_now, 0, False).astype(F32)
    gain = 1.0 + mod_now[1]

    states = hidden.astype(F32)
    w_gain = (gain[:, None] * proj_w.astype(F32)).astype(BF)
    cross = jnp.dot(hidden, w_gain, preferred_element_type=F32)
    w_sum = jnp.sum(w_gain.astype(F32), axis=0)
    stats = jnp.concatenate(
        [
            jnp.concatenate(
                [cross, jnp.sum(states, axis=1)[:, None], jnp.sum(states * states, axis=1)[:, None]], 1
            ),
            jnp.pad(w_sum, (0, 2))[None],
        ],
        0,
    )
    stats = stats + lax.ppermute(stats, "mp", [(0, 1), (1, 0)])
    width_all = lax.axis_size("mp") * features
    patch = proj_w.shape[1]
    mean_val = stats[:-1, patch] / width_all
    spread = stats[:-1, patch + 1] / width_all - mean_val * mean_val
    sigma = jnp.sqrt(spread + 1e-06)
    w_sum = stats[-1, :patch]
    cross = (stats[:-1, :patch] - mean_val[:, None] * w_sum[None]) / sigma[:, None]

    latent_pad = keep_rows(padded_2(latent, ((TILE, 1),), 1), 1, own_rows, image_side)
    pre_one = conv_forward(latent_pad, dec_w1)
    act_one = jax.nn.silu(pre_one).astype(BF)
    act_pad = keep_rows(padded_2(act_one, ((TILE, 1),), 1), 1, own_rows, image_side)
    pre_two = conv_forward(act_pad, dec_w2)
    grad_two = (feat_cot * silu_grad(pre_two)).astype(BF)
    grad_pad = keep_rows(padded_2(grad_two, ((TILE, 1),), 1), 1, own_rows, image_side)
    grad_one = (conv_backward(grad_pad, dec_w2) * silu_grad(pre_one)).astype(BF)
    inner_pad = keep_rows(padded_2(grad_one, ((TILE, 1),), 1), 1, own_rows, image_side)
    grad_latent = conv_backward(inner_pad, dec_w1)
    token_rows = own_rows // 2
    half_side = image_side // 2
    tokens_grad = (
        grad_latent.reshape(channels, token_rows, 2, half_side, 2)
        .transpose(1, 3, 0, 2, 4)
        .reshape(token_rows * half_side, 4 * channels)
    )
    grad_velocity = (tokens_grad * -step_now).astype(BF)

    normed = (states - mean_val[:, None]) / sigma[:, None]
    cross_grad = jnp.einsum("tp,td->pd", grad_velocity, normed.astype(BF), preferred_element_type=F32)
    gv_sum = jnp.sum(grad_velocity.astype(F32), axis=0)
    w_t = proj_w.T
    proj_part = cross_grad * gain + mod_now[0] * gv_sum[:, None]
    mod_part = image_pick[:, None] * jnp.sum(cross_grad * w_t.astype(F32), axis=0)
    sums = image_pick[:, None] * gv_sum[None]
    high = sums.astype(BF).astype(F32)
    sums = jnp.pad(
        jnp.stack([high, sums - high]).reshape(2, image_count * patch),
        ((0, 6), (0, features - image_count * patch)),
    )
    total = sum_over_tile(jnp.concatenate([proj_part, mod_part, sums], 0)).astype(F32)
    grad_proj = total[:patch].T
    sums = (total[patch + 8] + total[patch + 9])[: image_count * patch].reshape(image_count, patch)
    first = jnp.dot(sums, w_t.astype(F32), precision=lax.Precision.HIGHEST)
    grad_mod = jnp.stack([first, total[patch : patch + 8]], axis=1)

    wide = grad_velocity.astype(F32)
    first_mean = jnp.sum(wide * w_sum[None], axis=1) / width_all
    second_mean = jnp.sum(wide * cross, axis=1) / width_all
    grad_normed = jnp.dot(grad_velocity, w_t, preferred_element_type=F32) * gain
    grad_hidden = (
        (grad_normed - first_mean[:, None] - normed * second_mean[:, None]) / sigma[:, None]
    ).astype(BF)
    return (grad_hidden, grad_proj, grad_mod)


def solution(mesh):
    fine = Mesh(
        mesh.devices.reshape(4, 4, 4, 2, 2), ("y", "x", "zl", "core", "mp")
    )
    return jax.shard_map(
        body,
        mesh=fine,
        in_specs=(
            P(None, TILE, None),
            P(None, TILE, None),
            P(),
            P(),
            P(TILE, "mp"),
            P(None, None, "mp"),
            P(),
            P(),
            P("mp", None),
        ),
        out_specs=(P(TILE, "mp"), P("mp", None), P(None, None, "mp")),
        check_vma=False,
    )
```

time: 1320 us -> 138 us (0.10)
  waiting for transfers between devices: 1210 us -> 34.4 us
  starting transfers between devices: 32.3 us -> 48.2 us
  blocking collectives: 15.7 us -> 0 us
    psum x1 -> x0, waiting for transfers between devices: 1210 us -> none  [body(): grad_proj, grad_mod = lax.psum((proj_part, mod_spread), 'tile')]
    ppermute x0 -> x12, waiting for transfers between devices: none -> 25.6 us  [the longest x9 24.6 us: sum_over_tile(): lax.ppermute(out, axis, [(i, (i + d) % count) for i in range(count)])]
    ppermute x0 -> x12, starting transfers between devices: none -> 20.9 us  [the longest x1 8.51 us: sum_over_tile(): total = keep + lax.ppermute(send.astype(BF), 'core', swap).astype(F32)]
    psum x2 -> x0, blocking collectives: 15.7 us -> none  [the longest x1 8.02 us: body(): lax.psum((jnp.sum(states, axis=1), jnp.sum(states * states, axis=1)), 'mp')]
  transfers between devices with their start and end apart: 9 -> 20, of which waited for: 4 -> 14; matrix products, arithmetic and copies ran while one was open for 1% -> 23% of each run, Pallas kernels for 0% -> 0%
where the time goes in v1:
time: 138 us
  starting transfers between devices  48.2 us (35%)
  waiting for transfers between devices  34.4 us (25%)
  matrix products  32 us (23%)
  other arithmetic  11.4 us (8%)
  local copies, waits for them, and re-layouts  8.23 us (6%)
  between operations  3.66 us (3%)
    ppermute x4, starting transfers between devices, padded_2(): lax.ppermute(lax.slice_in_dim(block, 0, width, axis=dim), axis, backward)  27.3 us
    ppermute x9, waiting for transfers between devices, sum_over_tile(): lax.ppermute(out, axis, [(i, (i + d) % count) for i in range(count)])  24.6 us
    dot_general x18, matrix products, conv_forward(): jnp.einsum('oc,crw->orw', weight[kernel_tap], widened[:, row_off:row_off...  15.2 us
    dot_general x18, matrix products, conv_backward(): jnp.einsum('oc,orw->crw', weight[kernel_tap], widened[:, 2 - row_off:2 -...  13.1 us
    ppermute x1, starting transfers between devices, sum_over_tile(): total = keep + lax.ppermute(send.astype(BF), 'core', swap).astype(F32)  8.51 us
    ppermute x4, waiting for transfers between devices, padded_2(): lax.ppermute(lax.slice_in_dim(block, block.shape[dim] - width, None, axis...  7.77 us
    ppermute x1, starting transfers between devices, body(): stats = stats + lax.ppermute(stats, 'mp', [(0, 1), (1, 0)])  6.24 us
    ppermute x9, starting transfers between devices, sum_over_tile(): lax.ppermute(out, axis, [(i, (i + d) % count) for i in range(count)])  5.21 us
  transfers between devices with their start and end apart: 20, of which 14 were waited for; matrix products, arithmetic and copies ran while one was open for 23% of the time, Pallas kernels for 0%

profile of v1, /device:TPU:1, one launch (start us, length us, event | category | flops | bytes accessed | tf_op | source)
XLA Modules:
  0.0 137.9 jit_solution(10732445569698356653)
XLA Ops:
  1.4 3.3 %collective-permute-start.1 = (bf16[16,1,128]{2,0,1:T(8,128)(2,1)S(1)}, bf16[16,1,128]{2,0,1:T(8,128)(2,1)S(1)}, u32[]{:S(2)}, u32[]{:S(2)}) collective-permute-start(bf16[16,1,128]{2,0,1:T(8,128)(2,1)S(1)} %get-tuple-element.33), channel_id=1, source_target_pairs={{2,0},{4,2},{6,4},{8,6},{10,8},{12,10},{14,12},{16,14},{18,16},{20... | collective-permute-start | bytes 12296 | tf_op jit(solution)/shard_map/ppermute | solution.py:20
  4.8 1.3 select_reduce_fusion
  8.7 1.5 %convert_reduce_fusion = (f32[256]{0:T(256)S(1)}, f32[256]{0:T(256)S(1)}) fusion(bf16[256,1536]{1,0:T(8,128)(2,1)} %param.13), kind=kLoop, calls=%fused_computation.7 | loop fusion | flops 1572352 | bytes 788480 | tf_op jit(solution)/shard_map/reduce_sum | solution.py:115
  11.3 1.6 %convolution_bitcast_fusion.1 = f32[256,64]{0,1:T(8,128)S(1)} fusion(bf16[256,1536]{1,0:T(8,128)(2,1)} %param.13, bf16[1536,64]{0,1:T(8,128)(2,1)} %param.17, f32[1536]{0:T(1024)S(1)} %get-tuple-element.17), kind=kOutput, calls=%fused_computation.36 | convolution fusion | flops 50626560 | bytes 1054720 | tf_op jit(solution)/shard_map/dot_general | solution.py:110
  13.7 6.2 %collective-permute-start.8 = (f32[257,66]{0,1:T(8,128)}, f32[257,66]{0,1:T(8,128)}, u32[]{:S(2)}, u32[]{:S(2)}) collective-permute-start(f32[257,66]{0,1:T(8,128)} %pad_maximum_fusion.1), channel_id=1, source_target_pairs={{0,1},{1,0},{2,3},{3,2},{4,5},{5,4},{6,7},{7,6},{8,9},{9,8},{10,11... | collective-permute-start | bytes 203552 | tf_op jit(solution)/shard_map/ppermute | solution.py:121
  26.2 5.2 %collective-permute-start.3 = (bf16[512,1,128]{0,2,1:T(8,128)(2,1)}, bf16[512,1,128]{0,2,1:T(8,128)(2,1)}, u32[]{:S(2)}, u32[]{:S(2)}) collective-permute-start(bf16[512,1,128]{0,2,1:T(8,128)(2,1)} %get-tuple-element.25), channel_id=1, source_target_pairs={{2,0},{4,2},{6,4},{8,6},{10,8},{12,10},{14,12},{16,14},{18,16},{20... | collective-permute-start | bytes 393224 | tf_op jit(solution)/shard_map/ppermute | solution.py:20
  32.1 2.4 %copy.47 = bf16[512,8,128]{0,2,1:T(8,128)(2,1)} copy(bf16[512,8,128]{2,1,0:T(8,128)(2,1)} %param.9) | data formatting | bytes 2097152 | tf_op args[0]
  35.3 4.8 %collective-permute-done.2 = bf16[512,1,128]{0,2,1:T(8,128)(2,1)} collective-permute-done((bf16[512,1,128]{0,2,1:T(8,128)(2,1)}, bf16[512,1,128]{0,2,1:T(8,128)(2,1)}, u32[]{:S(2)}, u32[]{:S(2)}) %collective-permute-start.2) | collective-permute-done | bytes 131104 | tf_op jit(solution)/shard_map/ppermute | solution.py:17
  40.1 1.3 maximum_select_fusion
  41.5 1.9 %fusion.77 = f32[8,128,512]{2,1,0:T(8,128)S(1)} fusion(bf16[512,10,128]{0,2,1:T(8,128)(2,1)S(1)} %maximum_select_fusion, bf16[9,512,512]{2,1,0:T(8,128)(2,1)} %param.12), kind=kOutput, calls=%fused_computation.72 | convolution fusion | flops 536870912 | bytes 3932160 | tf_op jit(solution)/shard_map/oc,crw->orw/dot_general | solution.py:37
  43.3 1.8 %fusion.79 = f32[8,128,512]{2,1,0:T(8,128)S(1)} fusion(bf16[512,10,128]{0,2,1:T(8,128)(2,1)S(1)} %maximum_select_fusion, bf16[9,512,512]{2,1,0:T(8,128)(2,1)} %param.12), kind=kOutput, calls=%fused_computation.74 | convolution fusion | flops 536870912 | bytes 3932160 | tf_op jit(solution)/shard_map/oc,crw->orw/dot_general | solution.py:37
  50.1 1.7 %fusion.11 = bf16[512,8,128]{0,2,1:T(8,128)(2,1)S(1)} fusion(f32[8,128,512]{2,1,0:T(8,128)S(1)} %fusion.77, f32[8,128,512]{2,1,0:T(8,128)S(1)} %fusion.79, f32[8,128,512]{2,1,0:T(8,128)S(1)} %fusion.81, f32[8,128,512]{2,1,0:T(8,128)S(1)} %fusion.121, f32[8,128,512]{2,1,0:T(8,128)S(1)} %fusion.83, f32[8,128,512]{2,1,0:T(8,128)S(1)} %fusion.85, ...), kind=kOutput, calls=%fused_computation.19 | convolution fusion | flops 546308096 | bytes 20709376 | tf_op jit(solution)/shard_map/oc,crw->orw/dot_general | solution.py:37
  52.6 9.5 %collective-permute-start.5 = (bf16[512,1,128]{0,2,1:T(8,128)(2,1)}, bf16[512,1,128]{0,2,1:T(8,128)(2,1)}, u32[]{:S(2)}, u32[]{:S(2)}) collective-permute-start(bf16[512,1,128]{0,2,1:T(8,128)(2,1)} %get-tuple-element.23), channel_id=1, source_target_pairs={{2,0},{4,2},{6,4},{8,6},{10,8},{12,10},{14,12},{16,14},{18,16},{20... | collective-permute-start | bytes 393224 | tf_op jit(solution)/shard_map/ppermute | solution.py:20
  64.6 1.3 maximum_select_fusion.1
  66.0 1.8 %fusion.65 = f32[8,128,512]{2,1,0:T(8,128)S(1)} fusion(bf16[512,10,128]{0,2,1:T(8,128)(2,1)S(1)} %maximum_select_fusion.1, bf16[9,512,512]{2,1,0:T(8,128)(2,1)} %param.12), kind=kOutput, calls=%fused_computation.60 | convolution fusion | flops 536870912 | bytes 3932160 | tf_op jit(solution)/shard_map/oc,orw->crw/dot_general | solution.py:53
  67.8 1.8 %fusion.67 = f32[8,128,512]{2,1,0:T(8,128)S(1)} fusion(bf16[512,10,128]{0,2,1:T(8,128)(2,1)S(1)} %maximum_select_fusion.1, bf16[9,512,512]{2,1,0:T(8,128)(2,1)} %param.12), kind=kOutput, calls=%fused_computation.62 | convolution fusion | flops 536870912 | bytes 3932160 | tf_op jit(solution)/shard_map/oc,orw->crw/dot_general | solution.py:53
  73.9 1.7 %fusion.4 = bf16[512,8,128]{0,2,1:T(8,128)(2,1)S(1)} fusion(f32[8,128,512]{2,1,0:T(8,128)S(1)} %get-tuple-element.37, f32[8,128,512]{2,1,0:T(8,128)S(1)} %fusion.65, f32[8,128,512]{2,1,0:T(8,128)S(1)} %fusion.67, f32[8,128,512]{2,1,0:T(8,128)S(1)} %fusion.69, f32[8,128,512]{2,1,0:T(8,128)S(1)} %fusion.119, f32[8,128,512]{2,1,0:T(8,128)S(1)} %fusion.71, ...), kind=kOutput, calls=%fused_computation.10 | convolution fusion | flops 545783808 | bytes 21757952 | tf_op jit(solution)/shard_map/oc,orw->crw/dot_general | solution.py:53
  75.7 9.2 %collective-permute-start.7 = (bf16[512,1,128]{0,2,1:T(8,128)(2,1)S(1)}, bf16[512,1,128]{0,2,1:T(8,128)(2,1)S(1)}, u32[]{:S(2)}, u32[]{:S(2)}) collective-permute-start(bf16[512,1,128]{0,2,1:T(8,128)(2,1)S(1)} %get-tuple-element.21), channel_id=1, source_target_pairs={{2,0},{4,2},{6,4},{8,6},{10,8},{12,10},{14,12},{16,14},{18,16},{20... | collective-permute-start | bytes 393224 | tf_op jit(solution)/shard_map/ppermute | solution.py:20
  85.8 1.8 %collective-permute-done.6 = bf16[512,1,128]{0,2,1:T(8,128)(2,1)S(1)} collective-permute-done((bf16[512,1,128]{0,2,1:T(8,128)(2,1)S(1)}, bf16[512,1,128]{0,2,1:T(8,128)(2,1)S(1)}, u32[]{:S(2)}, u32[]{:S(2)}) %collective-permute-start.6) | collective-permute-done | bytes 131104 | tf_op jit(solution)/shard_map/ppermute | solution.py:17
  93.8 8.5 %collective-permute-start.9 = (bf16[80,768]{1,0:T(8,128)(2,1)S(1)}, bf16[80,768]{1,0:T(8,128)(2,1)S(1)}, u32[]{:S(2)}, u32[]{:S(2)}) collective-permute-start(bf16[80,768]{1,0:T(8,128)(2,1)S(1)} %dynamic-slice_convert_fusion), channel_id=1, source_target_pairs={{0,2},{2,0},{1,3},{3,1},{4,6},{6,4},{5,7},{7,5},{8,10},{10,8},{9,1... | collective-permute-start | bytes 368648 | tf_op jit(solution)/shard_map/ppermute | solution.py:75
  103.5 1.4 collective-permute-start.10
  104.9 4.1 %collective-permute-done.12 = bf16[80,768]{1,0:T(8,128)(2,1)S(1)} collective-permute-done((bf16[80,768]{1,0:T(8,128)(2,1)S(1)}, bf16[80,768]{1,0:T(8,128)(2,1)S(1)}, u32[]{:S(2)}, u32[]{:S(2)}) %collective-permute-start.12) | collective-permute-done | bytes 122912 | tf_op jit(solution)/shard_map/ppermute | solution.py:80
  109.1 5.2 %collective-permute-done.11 = bf16[80,768]{1,0:T(8,128)(2,1)S(1)} collective-permute-done((bf16[80,768]{1,0:T(8,128)(2,1)S(1)}, bf16[80,768]{1,0:T(8,128)(2,1)S(1)}, u32[]{:S(2)}, u32[]{:S(2)}) %collective-permute-start.11) | collective-permute-done | bytes 122912 | tf_op jit(solution)/shard_map/ppermute | solution.py:80
  114.5 1.4 collective-permute-start.13
  116.0 2.2 %collective-permute-done.15 = bf16[80,768]{1,0:T(8,128)(2,1)S(1)} collective-permute-done((bf16[80,768]{1,0:T(8,128)(2,1)S(1)}, bf16[80,768]{1,0:T(8,128)(2,1)S(1)}, u32[]{:S(2)}, u32[]{:S(2)}) %collective-permute-start.15) | collective-permute-done | bytes 122912 | tf_op jit(solution)/shard_map/ppermute | solution.py:80
  118.1 1.7 %collective-permute-done.14 = bf16[80,768]{1,0:T(8,128)(2,1)S(1)} collective-permute-done((bf16[80,768]{1,0:T(8,128)(2,1)S(1)}, bf16[80,768]{1,0:T(8,128)(2,1)S(1)}, u32[]{:S(2)}, u32[]{:S(2)}) %collective-permute-start.14) | collective-permute-done | bytes 122912 | tf_op jit(solution)/shard_map/ppermute | solution.py:80
  119.8 3.4 %collective-permute-done.13 = bf16[80,768]{1,0:T(8,128)(2,1)S(1)} collective-permute-done((bf16[80,768]{1,0:T(8,128)(2,1)S(1)}, bf16[80,768]{1,0:T(8,128)(2,1)S(1)}, u32[]{:S(2)}, u32[]{:S(2)}) %collective-permute-start.13) | collective-permute-done | bytes 122912 | tf_op jit(solution)/shard_map/ppermute | solution.py:80
  123.3 1.5 %collective-permute-start.18 = (bf16[80,768]{1,0:T(8,128)(2,1)S(1)}, bf16[80,768]{1,0:T(8,128)(2,1)S(1)}, u32[]{:S(2)}, u32[]{:S(2)}) collective-permute-start(bf16[80,768]{1,0:T(8,128)(2,1)S(1)} %fusion.166), channel_id=1, source_target_pairs={{0,192},{64,0},{128,64},{192,128},{1,193},{65,1},{129,65},{193,129... | collective-permute-start | bytes 368648 | tf_op jit(solution)/shard_map/ppermute | solution.py:80
  125.4 1.7 %collective-permute-done.18 = bf16[80,768]{1,0:T(8,128)(2,1)S(1)} collective-permute-done((bf16[80,768]{1,0:T(8,128)(2,1)S(1)}, bf16[80,768]{1,0:T(8,128)(2,1)S(1)}, u32[]{:S(2)}, u32[]{:S(2)}) %collective-permute-start.18) | collective-permute-done | bytes 122912 | tf_op jit(solution)/shard_map/ppermute | solution.py:80
  127.1 3.0 %collective-permute-done.17 = bf16[80,768]{1,0:T(8,128)(2,1)S(1)} collective-permute-done((bf16[80,768]{1,0:T(8,128)(2,1)S(1)}, bf16[80,768]{1,0:T(8,128)(2,1)S(1)}, u32[]{:S(2)}, u32[]{:S(2)}) %collective-permute-start.17) | collective-permute-done | bytes 122912 | tf_op jit(solution)/shard_map/ppermute | solution.py:80
  130.1 3.4 %collective-permute-done.16 = bf16[80,768]{1,0:T(8,128)(2,1)S(1)} collective-permute-done((bf16[80,768]{1,0:T(8,128)(2,1)S(1)}, bf16[80,768]{1,0:T(8,128)(2,1)S(1)}, u32[]{:S(2)}, u32[]{:S(2)}) %collective-permute-start.16) | collective-permute-done | bytes 122912 | tf_op jit(solution)/shard_map/ppermute | solution.py:80
  134.5 1.5 %fusion.3 = bf16[256,1536]{1,0:T(8,128)(2,1)} fusion(bf16[256,64]{0,1:T(8,128)(2,1)S(1)} %convert_element_type.170, bf16[1536,64]{0,1:T(8,128)(2,1)S(1)} %copy-done.2, bf16[256,1536]{1,0:T(8,128)(2,1)S(1)} %copy-done.1, f32[256]{0:T(256)S(1)} %broadcast_multiply_fusion.2, f32[256]{0:T(256)S(1)} %bitcast.217, f32[256]{0:T(256)S(1)} %bitcast.214, ...), kind=kOutput, calls=%fused_computation.4 | convolution fusion | flops 53870592 | bytes 1812480 | tf_op jit(solution)/shard_map/dot_general | solution.py:170
  (124 shorter events, 35.2 us)
Async XLA Ops:
  0.6 19.4 %copy-start.3 = (bf16[9,512,16]{1,2,0:T(8,128)(2,1)S(1)}, bf16[9,512,16]{1,2,0:T(8,128)(2,1)}, u32[]{:S(2)}) copy-start(bf16[9,512,16]{1,2,0:T(8,128)(2,1)} %param.11) | copy-start | bytes 442372
  1.4 18.5 %collective-permute-start.1 = (bf16[16,1,128]{2,0,1:T(8,128)(2,1)S(1)}, bf16[16,1,128]{2,0,1:T(8,128)(2,1)S(1)}, u32[]{:S(2)}, u32[]{:S(2)}) collective-permute-start(bf16[16,1,128]{2,0,1:T(8,128)(2,1)S(1)} %get-tuple-element.33), channel_id=1, source_target_pairs={{2,0},{4,2},{6,4},{8,6},{10,8},{12,10},{14,12},{16,14},{18,16},{20... | collective-permute-start | bytes 12296 | tf_op jit(solution)/shard_map/ppermute | solution.py:20
  4.8 15.2 %collective-permute-start = (bf16[16,1,128]{2,0,1:T(8,128)(2,1)S(1)}, bf16[16,1,128]{2,0,1:T(8,128)(2,1)S(1)}, u32[]{:S(2)}, u32[]{:S(2)}) collective-permute-start(bf16[16,1,128]{2,0,1:T(8,128)(2,1)S(1)} %get-tuple-element.32), channel_id=1, source_target_pairs={{0,2},{2,4},{4,6},{6,8},{8,10},{10,12},{12,14},{14,16},{16,18},{18... | collective-permute-start | bytes 12296 | tf_op jit(solution)/shard_map/ppermute | solution.py:17
  13.7 48.4 %collective-permute-start.8 = (f32[257,66]{0,1:T(8,128)}, f32[257,66]{0,1:T(8,128)}, u32[]{:S(2)}, u32[]{:S(2)}) collective-permute-start(f32[257,66]{0,1:T(8,128)} %pad_maximum_fusion.1), channel_id=1, source_target_pairs={{0,1},{1,0},{2,3},{3,2},{4,5},{5,4},{6,7},{7,6},{8,9},{9,8},{10,11... | collective-permute-start | bytes 203552 | tf_op jit(solution)/shard_map/ppermute | solution.py:121
  24.3 7.1 %copy-start.4 = (f32[8]{0:T(128)S(1)}, f32[8]{0:T(128)}, u32[]{:S(2)}) copy-start(f32[8]{0:T(128)} %param.16) | copy-start | bytes 100
  26.2 9.1 %collective-permute-start.3 = (bf16[512,1,128]{0,2,1:T(8,128)(2,1)}, bf16[512,1,128]{0,2,1:T(8,128)(2,1)}, u32[]{:S(2)}, u32[]{:S(2)}) collective-permute-start(bf16[512,1,128]{0,2,1:T(8,128)(2,1)} %get-tuple-element.25), channel_id=1, source_target_pairs={{2,0},{4,2},{6,4},{8,6},{10,8},{12,10},{14,12},{16,14},{18,16},{20... | collective-permute-start | bytes 393224 | tf_op jit(solution)/shard_map/ppermute | solution.py:20
  31.4 8.7 %collective-permute-start.2 = (bf16[512,1,128]{0,2,1:T(8,128)(2,1)}, bf16[512,1,128]{0,2,1:T(8,128)(2,1)}, u32[]{:S(2)}, u32[]{:S(2)}) collective-permute-start(bf16[512,1,128]{0,2,1:T(8,128)(2,1)} %get-tuple-element.24), channel_id=1, source_target_pairs={{0,2},{2,4},{4,6},{6,8},{8,10},{10,12},{12,14},{14,16},{16,18},{18... | collective-permute-start | bytes 393224 | tf_op jit(solution)/shard_map/ppermute | solution.py:17
  40.1 5.0 %slice-start = ((s8[4718592]{0:T(1024)(128)(4,1)}), s8[4194304]{0:T(1024)(128)(4,1)S(1)}, s32[]{:S(2)}) async-start(s8[4718592]{0:T(1024)(128)(4,1)} %bitcast.202), calls=%async_computation | async-start | bytes 8388608
  41.4 3.7 %slice-start.1 = ((s8[4718592]{0:T(1024)(128)(4,1)}), s8[524288]{0:T(1024)(128)(4,1)S(1)}, s32[]{:S(2)}) async-start(s8[4718592]{0:T(1024)(128)(4,1)} %bitcast.202), calls=%async_computation.1 | async-start | bytes 1048576
  48.9 1.2 copy-start
  52.6 10.9 %collective-permute-start.5 = (bf16[512,1,128]{0,2,1:T(8,128)(2,1)}, bf16[512,1,128]{0,2,1:T(8,128)(2,1)}, u32[]{:S(2)}, u32[]{:S(2)}) collective-permute-start(bf16[512,1,128]{0,2,1:T(8,128)(2,1)} %get-tuple-element.23), channel_id=1, source_target_pairs={{2,0},{4,2},{6,4},{8,6},{10,8},{12,10},{14,12},{16,14},{18,16},{20... | collective-permute-start | bytes 393224 | tf_op jit(solution)/shard_map/ppermute | solution.py:20
  62.1 2.5 %collective-permute-start.4 = (bf16[512,1,128]{0,2,1:T(8,128)(2,1)}, bf16[512,1,128]{0,2,1:T(8,128)(2,1)}, u32[]{:S(2)}, u32[]{:S(2)}) collective-permute-start(bf16[512,1,128]{0,2,1:T(8,128)(2,1)} %get-tuple-element.22), channel_id=1, source_target_pairs={{0,2},{2,4},{4,6},{6,8},{8,10},{10,12},{12,14},{14,16},{16,18},{18... | collective-permute-start | bytes 393224 | tf_op jit(solution)/shard_map/ppermute | solution.py:17
  64.6 5.0 %slice-start.2 = ((s8[4718592]{0:T(1024)(128)(4,1)}), s8[4194304]{0:T(1024)(128)(4,1)S(1)}, s32[]{:S(2)}) async-start(s8[4718592]{0:T(1024)(128)(4,1)} %bitcast.204), calls=%async_computation.2 | async-start | bytes 8388608
  66.0 3.6 %slice-start.3 = ((s8[4718592]{0:T(1024)(128)(4,1)}), s8[524288]{0:T(1024)(128)(4,1)S(1)}, s32[]{:S(2)}) async-start(s8[4718592]{0:T(1024)(128)(4,1)} %bitcast.204), calls=%async_computation.3 | async-start | bytes 1048576
  75.7 10.2 %collective-permute-start.7 = (bf16[512,1,128]{0,2,1:T(8,128)(2,1)S(1)}, bf16[512,1,128]{0,2,1:T(8,128)(2,1)S(1)}, u32[]{:S(2)}, u32[]{:S(2)}) collective-permute-start(bf16[512,1,128]{0,2,1:T(8,128)(2,1)S(1)} %get-tuple-element.21), channel_id=1, source_target_pairs={{2,0},{4,2},{6,4},{8,6},{10,8},{12,10},{14,12},{16,14},{18,16},{20... | collective-permute-start | bytes 393224 | tf_op jit(solution)/shard_map/ppermute | solution.py:20
  84.9 2.8 %collective-permute-start.6 = (bf16[512,1,128]{0,2,1:T(8,128)(2,1)S(1)}, bf16[512,1,128]{0,2,1:T(8,128)(2,1)S(1)}, u32[]{:S(2)}, u32[]{:S(2)}) collective-permute-start(bf16[512,1,128]{0,2,1:T(8,128)(2,1)S(1)} %get-tuple-element.20), channel_id=1, source_target_pairs={{0,2},{2,4},{4,6},{6,8},{8,10},{10,12},{12,14},{14,16},{16,18},{18... | collective-permute-start | bytes 393224 | tf_op jit(solution)/shard_map/ppermute | solution.py:17
  90.6 2.6 %copy-start.1 = (bf16[256,1536]{1,0:T(8,128)(2,1)S(1)}, bf16[256,1536]{1,0:T(8,128)(2,1)}, u32[]{:S(2)}) copy-start(bf16[256,1536]{1,0:T(8,128)(2,1)} %param.13) | copy-start | bytes 2359300
  90.6 2.6 %copy-start.2 = (bf16[1536,64]{0,1:T(8,128)(2,1)S(1)}, bf16[1536,64]{0,1:T(8,128)(2,1)}, u32[]{:S(2)}) copy-start(bf16[1536,64]{0,1:T(8,128)(2,1)} %param.17) | copy-start | bytes 589828
  93.8 9.5 %collective-permute-start.9 = (bf16[80,768]{1,0:T(8,128)(2,1)S(1)}, bf16[80,768]{1,0:T(8,128)(2,1)S(1)}, u32[]{:S(2)}, u32[]{:S(2)}) collective-permute-start(bf16[80,768]{1,0:T(8,128)(2,1)S(1)} %dynamic-slice_convert_fusion), channel_id=1, source_target_pairs={{0,2},{2,0},{1,3},{3,1},{4,6},{6,4},{5,7},{7,5},{8,10},{10,8},{9,1... | collective-permute-start | bytes 368648 | tf_op jit(solution)/shard_map/ppermute | solution.py:75
  103.3 5.8 %collective-permute-start.12 = (bf16[80,768]{1,0:T(8,128)(2,1)S(1)}, bf16[80,768]{1,0:T(8,128)(2,1)S(1)}, u32[]{:S(2)}, u32[]{:S(2)}) collective-permute-start(bf16[80,768]{1,0:T(8,128)(2,1)S(1)} %fusion.156), channel_id=1, source_target_pairs={{0,12},{4,0},{8,4},{12,8},{1,13},{5,1},{9,5},{13,9},{2,14},{6,2},{... | collective-permute-start | bytes 368648 | tf_op jit(solution)/shard_map/ppermute | solution.py:80
  103.4 10.8 %collective-permute-start.11 = (bf16[80,768]{1,0:T(8,128)(2,1)S(1)}, bf16[80,768]{1,0:T(8,128)(2,1)S(1)}, u32[]{:S(2)}, u32[]{:S(2)}) collective-permute-start(bf16[80,768]{1,0:T(8,128)(2,1)S(1)} %fusion.156), channel_id=1, source_target_pairs={{0,8},{4,12},{8,0},{12,4},{1,9},{5,13},{9,1},{13,5},{2,10},{6,14},... | collective-permute-start | bytes 368648 | tf_op jit(solution)/shard_map/ppermute | solution.py:80
  103.5 10.7 %collective-permute-start.10 = (bf16[80,768]{1,0:T(8,128)(2,1)S(1)}, bf16[80,768]{1,0:T(8,128)(2,1)S(1)}, u32[]{:S(2)}, u32[]{:S(2)}) collective-permute-start(bf16[80,768]{1,0:T(8,128)(2,1)S(1)} %fusion.156), channel_id=1, source_target_pairs={{0,4},{4,8},{8,12},{12,0},{1,5},{5,9},{9,13},{13,1},{2,6},{6,10},{... | collective-permute-start | bytes 368648 | tf_op jit(solution)/shard_map/ppermute | solution.py:80
  114.3 3.8 %collective-permute-start.15 = (bf16[80,768]{1,0:T(8,128)(2,1)S(1)}, bf16[80,768]{1,0:T(8,128)(2,1)S(1)}, u32[]{:S(2)}, u32[]{:S(2)}) collective-permute-start(bf16[80,768]{1,0:T(8,128)(2,1)S(1)} %get-tuple-element.18), channel_id=1, source_target_pairs={{0,48},{16,0},{32,16},{48,32},{1,49},{17,1},{33,17},{49,33},{2,50}... | collective-permute-start | bytes 368648 | tf_op jit(solution)/shard_map/ppermute | solution.py:80
  114.4 5.4 %collective-permute-start.14 = (bf16[80,768]{1,0:T(8,128)(2,1)S(1)}, bf16[80,768]{1,0:T(8,128)(2,1)S(1)}, u32[]{:S(2)}, u32[]{:S(2)}) collective-permute-start(bf16[80,768]{1,0:T(8,128)(2,1)S(1)} %get-tuple-element.18), channel_id=1, source_target_pairs={{0,32},{16,48},{32,0},{48,16},{1,33},{17,49},{33,1},{49,17},{2,34}... | collective-permute-start | bytes 368648 | tf_op jit(solution)/shard_map/ppermute | solution.py:80
  114.5 8.7 %collective-permute-start.13 = (bf16[80,768]{1,0:T(8,128)(2,1)S(1)}, bf16[80,768]{1,0:T(8,128)(2,1)S(1)}, u32[]{:S(2)}, u32[]{:S(2)}) collective-permute-start(bf16[80,768]{1,0:T(8,128)(2,1)S(1)} %get-tuple-element.18), channel_id=1, source_target_pairs={{0,16},{16,32},{32,48},{48,0},{1,17},{17,33},{33,49},{49,1},{2,18}... | collective-permute-start | bytes 368648 | tf_op jit(solution)/shard_map/ppermute | solution.py:80
  123.3 3.8 %collective-permute-start.18 = (bf16[80,768]{1,0:T(8,128)(2,1)S(1)}, bf16[80,768]{1,0:T(8,128)(2,1)S(1)}, u32[]{:S(2)}, u32[]{:S(2)}) collective-permute-start(bf16[80,768]{1,0:T(8,128)(2,1)S(1)} %fusion.166), channel_id=1, source_target_pairs={{0,192},{64,0},{128,64},{192,128},{1,193},{65,1},{129,65},{193,129... | collective-permute-start | bytes 368648 | tf_op jit(solution)/shard_map/ppermute | solution.py:80
  124.7 5.3 %collective-permute-start.17 = (bf16[80,768]{1,0:T(8,128)(2,1)S(1)}, bf16[80,768]{1,0:T(8,128)(2,1)S(1)}, u32[]{:S(2)}, u32[]{:S(2)}) collective-permute-start(bf16[80,768]{1,0:T(8,128)(2,1)S(1)} %fusion.166), channel_id=1, source_target_pairs={{0,128},{64,192},{128,0},{192,64},{1,129},{65,193},{129,1},{193,65... | collective-permute-start | bytes 368648 | tf_op jit(solution)/shard_map/ppermute | solution.py:80
  124.7 8.7 %collective-permute-start.16 = (bf16[80,768]{1,0:T(8,128)(2,1)S(1)}, bf16[80,768]{1,0:T(8,128)(2,1)S(1)}, u32[]{:S(2)}, u32[]{:S(2)}) collective-permute-start(bf16[80,768]{1,0:T(8,128)(2,1)S(1)} %fusion.166), channel_id=1, source_target_pairs={{0,64},{64,128},{128,192},{192,0},{1,65},{65,129},{129,193},{193,1... | collective-permute-start | bytes 368648 | tf_op jit(solution)/shard_map/ppermute | solution.py:80
  133.6 2.4 %collective-permute-start.19 = (bf16[80,768]{1,0:T(8,128)(2,1)S(1)}, bf16[80,768]{1,0:T(8,128)(2,1)S(1)}, u32[]{:S(2)}, u32[]{:S(2)}) collective-permute-start(bf16[80,768]{1,0:T(8,128)(2,1)S(1)} %add_convert_fusion), channel_id=1, source_target_pairs={{0,2},{2,0},{1,3},{3,1},{4,6},{6,4},{5,7},{7,5},{8,10},{10,8},{9,1... | collective-permute-start | bytes 368648 | tf_op jit(solution)/shard_map/ppermute | solution.py:86

commit v2 on v0

v2 whole, which is shorter than its diff:
```python
import functools

import jax
import jax.numpy as jnp
from jax import lax
from jax.experimental import pallas as pl
from jax.experimental.pallas import tpu as pltpu
from jax.sharding import Mesh, PartitionSpec as P

BF = jnp.bfloat16
F32 = jnp.float32
TILE = ("y", "x", "zl", "core")
RINGS = ("zl", "x", "y")
OVER_0 = (((0,), (0,)), ((), ()))
OVER_1 = (((1,), (1,)), ((), ()))
WHOLE = pl.BlockSpec(memory_space=pltpu.VMEM)
SCALARS = pl.BlockSpec(memory_space=pltpu.SMEM)


def dot(a, b, dims=(((1,), (0,)), ((), ()))):
    return lax.dot_general(a, b, dims, preferred_element_type=F32)


def before(v, axis):
    place = lax.broadcasted_iota(jnp.int32, v.shape, axis)
    return jnp.where(place == 0, 0.0, pltpu.roll(v, 1, axis))


def after(v, axis):
    n = v.shape[axis]
    place = lax.broadcasted_iota(jnp.int32, v.shape, axis)
    return jnp.where(place == n - 1, 0.0, pltpu.roll(v, n - 1, axis))


def sigmoid(h):
    return 0.5 + 0.5 * jnp.tanh(0.5 * h)


def convs_kernel(rows, width, flags, low, high, lat_own, cot_own, w1, w1t, w2_hbm, out,
                 w2, lats, acts, dsilu, grads, inner, sem):
    ch = lat_own.shape[1]
    load = pltpu.make_async_copy(w2_hbm, w2, sem)
    load.start()
    top, bottom, step = flags[0], flags[1], flags[2]

    def keep(row):
        return top if row < 0 else bottom if row >= rows else None

    def masked(v, row):
        k = keep(row)
        return v if k is None else v * k

    def lat_line(row):
        if 0 <= row < rows:
            return lat_own[row]
        halo, i = (low, row + 4) if row < 0 else (high, row - rows)
        return halo[2 * width :, i * width : (i + 1) * width]

    def cot_line(row):
        if 0 <= row < rows:
            return cot_own[row]
        halo, i = (low, row + 2) if row < 0 else (high, row - rows)
        return halo[i * width : (i + 1) * width, :]

    for i in range(rows + 8):
        row = i - 4
        v = masked(lat_line(row).astype(F32), row)
        lats[0, i] = before(v, 1).astype(BF)
        lats[1, i] = v.astype(BF)
        lats[2, i] = after(v, 1).astype(BF)

    def store3(ref, i, v):
        at = pl.ds(i * width, width)
        ref[0, at, :] = before(v, 0).astype(BF)
        ref[1, at, :] = v.astype(BF)
        ref[2, at, :] = after(v, 0).astype(BF)

    for i in range(rows + 6):
        row = i - 3
        taps = [lats[kx, i + ky] for ky in range(3) for kx in range(3)]
        pre = dot(jnp.concatenate(taps, 0), w1[...], OVER_0)
        s = sigmoid(pre)
        act = pre * s
        if -1 <= row <= rows:
            dsilu[pl.ds((row + 1) * width, width), :] = s * (1.0 + pre * (1.0 - s))
        store3(acts, i, masked(act.astype(BF).astype(F32), row))
    load.wait()

    per = 2
    for i in range(0, rows + 4, per):
        pre = None
        for ky in range(3):
            for kx in range(3):
                part = dot(acts[kx, pl.ds((i + ky) * width, per * width), :], w2[3 * ky + kx], OVER_1)
                pre = part if pre is None else pre + part
        s = sigmoid(pre)
        slope = s * (1.0 + pre * (1.0 - s))
        for j in range(per):
            row = i + j - 2
            cot = cot_line(row).astype(F32)
            g = masked(cot * slope[j * width : (j + 1) * width], row)
            store3(grads, i + j, g)

    for i in range(0, rows + 2, per):
        back = None
        for ky in range(3):
            for kx in range(3):
                part = dot(grads[2 - kx, pl.ds((i + 2 - ky) * width, per * width), :], w2[3 * ky + kx])
                back = part if back is None else back + part
        for j in range(per):
            at = pl.ds((i + j) * width, width)
            g = back[j * width : (j + 1) * width] * dsilu[at, :]
            inner[at, :] = masked(g, i + j - 1).astype(BF)

    taps = dot(w1t[...], inner[...], OVER_1)
    lines = []
    for row in range(rows):
        by_kx = []
        for kx in range(3):
            total = None
            for ky in range(3):
                k = 3 * ky + kx
                at = (row + 2 - ky) * width
                part = taps[k * ch : (k + 1) * ch, at : at + width]
                total = part if total is None else total + part
            by_kx.append(total)
        whole = after(by_kx[0], 1) + by_kx[1] + before(by_kx[2], 1)
        lines.append((whole * step).astype(BF))

    half = width // 2
    spot = lax.broadcasted_iota(jnp.int32, (2 * width, 2 * width), 0)
    goal = lax.broadcasted_iota(jnp.int32, (2 * width, 2 * width), 1)
    within = lax.rem(goal, width)
    pick = (lax.div(spot, width) == lax.div(within, half)) & (
        lax.rem(spot, width) == 2 * lax.rem(within, half) + lax.div(goal, width)
    )
    pick = jnp.where(pick, 1.0, 0.0).astype(BF)
    stacked = [
        jnp.concatenate([lines[4 * h + a], lines[4 * h + 2 + a]], 1)
        for h in range(rows // 4)
        for a in range(2)
    ]
    apart = dot(jnp.concatenate(stacked, 0), pick).astype(BF)
    for h in range(rows // 4):
        for a in range(2):
            for b in range(2):
                out[pl.ds((2 * a + b) * ch, ch), pl.ds(h * width, width)] = apart[
                    (2 * h + a) * ch : (2 * h + a + 1) * ch, b * width : (b + 1) * width
                ]


def shift_and_gain(places, mod):
    chosen = mod[places[0]].astype(F32)
    return chosen[0:1], 1.0 + chosen[1:2]


def stats_kernel(places, hidden, mod, wt, out):
    _, gain = shift_and_gain(places, mod)
    patch = wt.shape[0]
    tokens = hidden.shape[0]
    w_gain = (wt[...].astype(F32) * gain).astype(BF)
    out[...] = jnp.zeros_like(out)
    out[0:tokens, 0:patch] = dot(hidden[...], w_gain, OVER_1)
    states = hidden[...].astype(F32)
    out[0:tokens, patch : patch + 1] = jnp.sum(states, axis=1, keepdims=True)
    out[0:tokens, patch + 1 : patch + 2] = jnp.sum(states * states, axis=1, keepdims=True)
    out[tokens:, 0:patch] = dot(jnp.ones((8, wt.shape[1]), BF), w_gain, OVER_1)


def norm_of(width_all, patch, stats, stats_far, hidden):
    tokens = hidden.shape[0]
    both = stats[...] + stats_far[...]
    mean_val = both[0:tokens, patch : patch + 1] / width_all
    spread = both[0:tokens, patch + 1 : patch + 2] / width_all - mean_val * mean_val
    scale = 1.0 / jnp.sqrt(spread + 1e-06)
    w_sum = both[tokens : tokens + 1, 0:patch]
    cross = (both[0:tokens, 0:patch] - mean_val * w_sum) * scale
    return (hidden[...].astype(F32) - mean_val) * scale, scale, w_sum, cross


def sums_kernel(width_all, images, places, gvt, stats, stats_far, hidden, mod, wt, send, keep, held):
    patch = gvt.shape[0]
    shift, gain = shift_and_gain(places, mod)
    normed = norm_of(width_all, patch, stats, stats_far, hidden)[0]
    cross_grad = dot(gvt[...], normed.astype(BF))
    column = jnp.sum(gvt[...].astype(F32), axis=1, keepdims=True)
    held[0:patch, :] = cross_grad * gain + shift * column
    mod_row = jnp.sum(cross_grad * wt[...].astype(F32), axis=0, keepdims=True)
    image = places[1]
    spot = lax.broadcasted_iota(jnp.int32, (images, mod_row.shape[1]), 0)
    held[patch : patch + images, :] = jnp.where(spot == image, mod_row, 0.0)
    row = dot(jnp.ones((8, gvt.shape[1]), BF), gvt[...], OVER_1)
    held[patch + images :, :] = jnp.zeros((8, mod_row.shape[1]), F32)
    wide = jnp.concatenate([row] * images, 1)
    lane = lax.broadcasted_iota(jnp.int32, wide.shape, 1)
    held[patch + images :, 0 : images * patch] = jnp.where(lax.div(lane, patch) == image, wide, 0.0)
    half = keep.shape[1]
    core = places[2]
    keep[...] = held[:, pl.ds(pl.multiple_of(core * half, half), half)]
    send[...] = held[:, pl.ds(pl.multiple_of((1 - core) * half, half), half)].astype(BF)


def hidden_kernel(width_all, places, gvt, stats, stats_far, hidden, mod, wt, out):
    patch = gvt.shape[0]
    _, gain = shift_and_gain(places, mod)
    normed, scale, w_sum, cross = norm_of(width_all, patch, stats, stats_far, hidden)
    gv = gvt[...].astype(F32).T
    first = jnp.sum(gv * w_sum, axis=1, keepdims=True) / width_all
    second = jnp.sum(gv * cross, axis=1, keepdims=True) / width_all
    grad = dot(gv.astype(BF), wt[...]) * gain
    out[...] = ((grad - first - normed * second) * scale).astype(BF)


def last_kernel(images, places, mine, other, wt, proj, mod):
    patch = wt.shape[0]
    half = mine.shape[1]
    core = places[2]
    source = lax.broadcasted_iota(jnp.int32, (patch, patch), 0)
    target = lax.broadcasted_iota(jnp.int32, (patch, patch), 1)
    ch = patch // 4
    order = jnp.where(target == 4 * lax.rem(source, ch) + lax.div(source, ch), 1.0, 0.0).astype(BF)
    for block, place in ((mine, core), (other, 1 - core)):
        at = pl.ds(pl.multiple_of(place * half, half), half)
        proj[at, :] = dot(block[0:patch, :], order, OVER_0)
        mod[:, 1, at] = block[patch : patch + images, :].astype(F32)
    wide = images * patch
    tail = patch + images
    mine_sum = mine[patch:, 0:wide].astype(F32)[images : images + 1]
    other_sum = other[patch:, 0:wide].astype(F32)[images : images + 1]
    line = jnp.where(core == 0, mine_sum, other_sum)
    sums = jnp.concatenate([line[:, i * patch : (i + 1) * patch] for i in range(images)], 0)
    mod[:, 0, :] = dot(sums.astype(BF), wt[...])


def call(kernel, out_shape, n_in, cost, name, scratch=(), smem=1):
    return pl.pallas_call(
        kernel,
        out_shape=out_shape,
        in_specs=[SCALARS] * smem + [WHOLE] * (n_in - smem),
        out_specs=jax.tree.map(lambda _: WHOLE, out_shape),
        scratch_shapes=list(scratch),
        compiler_params=pltpu.CompilerParams(vmem_limit_bytes=24 * 2**20),
        cost_estimate=pl.CostEstimate(flops=cost[0], bytes_accessed=cost[1], transcendentals=0),
        name=name,
    )


def sum_over_rings(total):
    for axis in RINGS:
        count = lax.axis_size(axis)
        out = total.astype(BF)
        came = [
            lax.ppermute(out, axis, [(i, (i + d) % count) for i in range(count)])
            for d in range(1, count)
        ]
        for block in came:
            total = total + block.astype(F32)
    return total


def body(feat_cot, latent, dec_w1, dec_w2, hidden, modulation, prompt_ids, step_size, proj_w):
    ch, rows, width = latent.shape
    mid = dec_w2.shape[1]
    images = prompt_ids.shape[0]
    tokens, features = hidden.shape
    patch = proj_w.shape[1]
    width_all = lax.axis_size("mp") * features
    tile = lax.axis_index(TILE)
    core = lax.axis_index("core")

    lat_own = latent.transpose(1, 0, 2)
    cot_own = feat_cot.transpose(1, 2, 0)

    def pack(lat_part, cot_part):
        return jnp.concatenate([cot_part.reshape(2 * width, mid), lat_part.reshape(ch, 4 * width)], 0)

    count = lax.axis_size(TILE)
    up = [(i, (i + 1) % count) for i in range(count)]
    low = lax.ppermute(pack(latent[:, -4:], cot_own[-2:]), TILE, up)
    high = lax.ppermute(pack(latent[:, :4], cot_own[:2]), TILE, [(b, a) for a, b in up])

    row_start = (tile * rows + width // 2) % width
    image = (tile * rows + width // 2) // width % images
    places = jnp.stack([prompt_ids[image], image, core]).astype(jnp.int32)
    flags = jnp.stack(
        [(row_start > 0).astype(F32), (row_start + rows < width).astype(F32), -step_size[image]]
    )
    wt = proj_w.reshape(features, ch, 4).transpose(2, 1, 0).reshape(patch, features)

    stats = call(
        stats_kernel, jax.ShapeDtypeStruct((tokens + 8, 128), F32), 4, (10**8, 10**6), "stats"
    )(places, hidden, modulation, wt)
    stats_far = lax.ppermute(stats, "mp", [(0, 1), (1, 0)])

    w1 = dec_w1.transpose(0, 2, 1).reshape(9 * ch, mid)
    gvt = pl.pallas_call(
        functools.partial(convs_kernel, rows, width),
        out_shape=jax.ShapeDtypeStruct((4 * ch, tokens), BF),
        in_specs=[SCALARS] + [WHOLE] * 6 + [pl.BlockSpec(memory_space=pl.ANY)],
        out_specs=WHOLE,
        scratch_shapes=[
            pltpu.VMEM(dec_w2.shape, BF),
            pltpu.VMEM((3, rows + 8, ch, width), BF),
            pltpu.VMEM((3, (rows + 6) * width, mid), BF),
            pltpu.VMEM(((rows + 2) * width, mid), F32),
            pltpu.VMEM((3, (rows + 4) * width, mid), BF),
            pltpu.VMEM(((rows + 2) * width, mid), BF),
            pltpu.SemaphoreType.DMA,
        ],
        compiler_params=pltpu.CompilerParams(vmem_limit_bytes=48 * 2**20),
        cost_estimate=pl.CostEstimate(
            flops=14 * 10**9, bytes_accessed=8 * 10**6, transcendentals=2 * 10**6
        ),
        name="convs",
    )(flags, low, high, lat_own, cot_own, w1, w1, dec_w2)

    lines = patch + images + 8
    half = features // 2
    send, keep = call(
        functools.partial(sums_kernel, width_all, images),
        (jax.ShapeDtypeStruct((lines, half), BF), jax.ShapeDtypeStruct((lines, half), F32)),
        7,
        (10**8, 2 * 10**6),
        "sums",
        scratch=(pltpu.VMEM((lines, features), F32),),
    )(places, gvt, stats, stats_far, hidden, modulation, wt)
    swap = [(0, 1), (1, 0)]
    mine = sum_over_rings(keep + lax.ppermute(send, "core", swap).astype(F32)).astype(BF)
    other = lax.ppermute(mine, "core", swap)

    grad_hidden = call(
        functools.partial(hidden_kernel, width_all),
        jax.ShapeDtypeStruct((tokens, features), BF),
        7,
        (10**8, 2 * 10**6),
        "grad_hidden",
    )(places, gvt, stats, stats_far, hidden, modulation, wt)

    grad_proj, grad_mod = call(
        functools.partial(last_kernel, images),
        (
            jax.ShapeDtypeStruct((features, patch), F32),
            jax.ShapeDtypeStruct((images, 2, features), F32),
        ),
        4,
        (10**7, 10**6),
        "last",
    )(places, mine, other, wt)
    return (grad_hidden, grad_proj, grad_mod)


def solution(mesh):
    fine = Mesh(mesh.devices.reshape(4, 4, 4, 2, 2), ("y", "x", "zl", "core", "mp"))
    return jax.shard_map(
        body,
        mesh=fine,
        in_specs=(
            P(None, TILE, None),
            P(None, TILE, None),
            P(),
            P(),
            P(TILE, "mp"),
            P(None, None, "mp"),
            P(),
            P(),
            P("mp", None),
        ),
        out_specs=(P(TILE, "mp"), P("mp", None), P(None, None, "mp")),
        check_vma=False,
    )
```

time: 1320 us -> 83.5 us (0.06)
  waiting for transfers between devices: 1210 us -> 17.9 us
  matrix products: 27.1 us -> 0 us
  Pallas kernels: 0 us -> 25 us
  blocking collectives: 15.7 us -> 0 us
  between operations: 15 us -> 1.5 us
    psum x1 -> x0, waiting for transfers between devices: 1210 us -> none  [body(): grad_proj, grad_mod = lax.psum((proj_part, mod_spread), 'tile')]
    dot_general x39 -> x0, matrix products: 27.1 us -> none  [the longest x18 13.4 us: conv_forward(): jnp.einsum('oc,crw->orw', weight[kernel_tap], widened[:, row_off:row_off...]
    pallas_call x0 -> x5, Pallas kernels: none -> 25 us  [the longest x1 19 us: body(): pl.pallas_call(functools.partial(convs_kernel, rows, width), out_shape=ja...]
    ppermute x8 -> x14, waiting for transfers between devices: 0.85 us -> 17.9 us  [the longest x9 16.9 us: sum_over_rings(): lax.ppermute(out, axis, [(i, (i + d) % count) for i in range(count)])]
    psum x2 -> x0, blocking collectives: 15.7 us -> none  [the longest x1 8.02 us: body(): lax.psum((jnp.sum(states, axis=1), jnp.sum(states * states, axis=1)), 'mp')]
    ppermute x8 -> x14, starting transfers between devices: 32.3 us -> 30.7 us  [the longest x9 11.5 us: sum_over_rings(): lax.ppermute(out, axis, [(i, (i + d) % count) for i in range(count)])]
  transfers between devices with their start and end apart: 9 -> 14, of which waited for: 4 -> 9; matrix products, arithmetic and copies ran while one was open for 1% -> 4% of each run, Pallas kernels for 0% -> 27%
where the time goes in v2:
time: 83.5 us; the launch traced here: 82.7 us
  starting transfers between devices  30.7 us (37%)
  Pallas kernels  25 us (30%)
  waiting for transfers between devices  17.9 us (21%)
  local copies, waits for them, and re-layouts  5.84 us (7%)
  other arithmetic  1.8 us (2%)
  between operations  1.5 us (2%)
    pallas_call x1, Pallas kernels, body(): pl.pallas_call(functools.partial(convs_kernel, rows, width), out_shape=ja...  19 us
    ppermute x9, waiting for transfers between devices, sum_over_rings(): lax.ppermute(out, axis, [(i, (i + d) % count) for i in range(count)])  16.9 us
    ppermute x9, starting transfers between devices, sum_over_rings(): lax.ppermute(out, axis, [(i, (i + d) % count) for i in range(count)])  11.5 us
    ppermute x1, starting transfers between devices, body(): lax.ppermute(send, 'core', swap).astype(F32)  7.49 us
    ppermute x1, starting transfers between devices, body(): stats_far = lax.ppermute(stats, 'mp', [(0, 1), (1, 0)])  6.02 us
    ppermute x1, starting transfers between devices, body(): low = lax.ppermute(pack(latent[:, -4:], cot_own[-2:]), TILE, up)  3.1 us
    unnamed x17, local copies, waits for them, and re-layouts  2.75 us
    ppermute x1, starting transfers between devices, body(): other = lax.ppermute(mine, 'core', swap)  2.33 us
  transfers between devices with their start and end apart: 14, of which 9 were waited for; matrix products, arithmetic and copies ran while one was open for 4% of the time, Pallas kernels for 27%

profile of v2, /device:TPU:1, one launch (start us, length us, event | category | flops | bytes accessed | tf_op | source)
XLA Modules:
  0.0 82.7 jit_solution(4114526475370124004)
XLA Ops:
  0.7 1.7 %copy.16 = bf16[512,8,128]{0,2,1:T(8,128)(2,1)S(1)} copy(bf16[512,8,128]{2,1,0:T(8,128)(2,1)} %param.9) | data formatting | bytes 2097152 | tf_op args[0]
  2.5 0.9 %fusion.4 = (bf16[16,4,128]{2,1,0:T(4,128)(2,1)S(1)}, bf16[16,4,128]{2,1,0:T(4,128)(2,1)S(1)}) fusion(bf16[16,8,128]{2,1,0:T(8,128)(2,1)} %param.10), kind=kLoop, calls=%fused_computation.15 | loop fusion | bytes 65536 | tf_op jit(solution)/shard_map/slice | solution.py:280
  3.4 3.1 %collective-permute-start = (bf16[272,512]{1,0:T(8,128)(2,1)S(1)}, bf16[272,512]{1,0:T(8,128)(2,1)S(1)}, u32[]{:S(2)}, u32[]{:S(2)}) collective-permute-start(bf16[272,512]{1,0:T(8,128)(2,1)S(1)} %pad_maximum_fusion), channel_id=1, source_target_pairs={{0,2},{2,4},{4,6},{6,8},{8,10},{10,12},{12,14},{14,16},{16,18},{18... | collective-permute-start | bytes 835592 | tf_op jit(solution)/shard_map/ppermute | solution.py:279
  6.5 0.7 pad_maximum_fusion.1
  7.2 0.2 collective-permute-start.1
  7.4 1.0 %reshape.34 = bf16[1536,16,4]{0,2,1:T(4,128)(2,1)S(1)} reshape(bf16[1536,64]{0,1:T(8,128)(2,1)} %param.17) | data formatting | bytes 393216 | tf_op jit(solution)/shard_map/reshape | solution.py:288
  8.5 0.6 dynamic_slice.6
  9.1 0.7 pad_add_fusion.places
  9.8 1.0 %stats.1 = f32[264,128]{1,0:T(8,128)S(1)} custom-call(s32[3]{0:T(128)S(1)} %pad_add_fusion.places, bf16[256,1536]{1,0:T(8,128)(2,1)S(1)} %copy-done, bf16[16,2,1536]{2,1,0:T(2,128)(2,1)S(1)} %copy-done.1, bf16[64,1536]{1,0:T(8,128)(2,1)S(1)} %bitcast.26), custom_call_target="tpu_custom_call" | custom-call | flops 100000000 | bytes 1000000 | tf_op jit(solution)/shard_map/stats/pallas_call | solution.py:290
  10.8 6.0 %collective-permute-start.2 = (f32[264,128]{1,0:T(8,128)S(1)}, f32[264,128]{1,0:T(8,128)S(1)}, u32[]{:S(2)}, u32[]{:S(2)}) collective-permute-start(f32[264,128]{1,0:T(8,128)S(1)} %stats.1), channel_id=1, source_target_pairs={{0,1},{1,0},{2,3},{3,2},{4,5},{5,4},{6,7},{7,6},{8,9},{9,8},{10,11... | collective-permute-start | bytes 405512 | tf_op jit(solution)/shard_map/ppermute | solution.py:293
  16.9 0.6 dynamic_slice.7
  18.2 19.0 %convs.1.gvt = bf16[64,256]{1,0:T(8,128)(2,1)S(1)} custom-call(f32[3]{0:T(128)S(1)} %pad_maximum_fusion.2.flags, bf16[272,512]{1,0:T(8,128)(2,1)S(1)} %collective-permute-done.low, bf16[272,512]{1,0:T(8,128)(2,1)S(1)} %collective-permute-done.1.high, bf16[8,16,128]{2,1,0:T(8,128)(2,1)S(1)} %bitcast.32, bf16[8,128,512]{2,1,0:T(8,128)(2,1)S(1)} %bitcast.31, ...), custom_call_target="tpu_custom_call" | custom-call | flops 14000000000 | bytes 8000000 | tf_op jit(solution)/shard_map/convs/pallas_call | solution.py:296
  37.2 1.1 %sums.1 = (bf16[80,768]{1,0:T(8,128)(2,1)S(1)}, f32[80,768]{1,0:T(8,128)S(1)}) custom-call(s32[3]{0:T(128)S(1)} %pad_add_fusion.places, bf16[64,256]{1,0:T(8,128)(2,1)S(1)} %convs.1.gvt, f32[264,128]{1,0:T(8,128)S(1)} %stats.1, f32[264,128]{1,0:T(8,128)S(1)} %collective-permute-done.2.stats_far, bf16[256,1536]{1,0:T(8,128)(2,1)S(1)} %copy-done, ...), custom_call_target="tpu_custom_call" | custom-call | flops 100000000 | bytes 2000000 | tf_op jit(solution)/shard_map/sums/pallas_call | solution.py:319
  38.4 7.5 %collective-permute-start.3 = (bf16[80,768]{1,0:T(8,128)(2,1)S(1)}, bf16[80,768]{1,0:T(8,128)(2,1)S(1)}, u32[]{:S(2)}, u32[]{:S(2)}) collective-permute-start(bf16[80,768]{1,0:T(8,128)(2,1)S(1)} %get-tuple-element.8), channel_id=1, source_target_pairs={{0,2},{2,0},{1,3},{3,1},{4,6},{6,4},{5,7},{7,5},{8,10},{10,8},{9,1... | collective-permute-start | bytes 368648 | tf_op jit(solution)/shard_map/ppermute | solution.py:328
  45.9 1.0 %collective-permute-done.3 = bf16[80,768]{1,0:T(8,128)(2,1)S(1)} collective-permute-done((bf16[80,768]{1,0:T(8,128)(2,1)S(1)}, bf16[80,768]{1,0:T(8,128)(2,1)S(1)}, u32[]{:S(2)}, u32[]{:S(2)}) %collective-permute-start.3) | collective-permute-done | bytes 122912 | tf_op jit(solution)/shard_map/ppermute | solution.py:328
  47.1 3.2 %collective-permute-start.6 = (bf16[80,768]{1,0:T(8,128)(2,1)S(1)}, bf16[80,768]{1,0:T(8,128)(2,1)S(1)}, u32[]{:S(2)}, u32[]{:S(2)}) collective-permute-start(bf16[80,768]{1,0:T(8,128)(2,1)S(1)} %fusion), channel_id=1, source_target_pairs={{0,12},{4,0},{8,4},{12,8},{1,13},{5,1},{9,5},{13,9},{2,14},{6,2},{... | collective-permute-start | bytes 368648 | tf_op jit(solution)/shard_map/ppermute | solution.py:253
  50.2 3.1 %collective-permute-done.4 = bf16[80,768]{1,0:T(8,128)(2,1)S(1)} collective-permute-done((bf16[80,768]{1,0:T(8,128)(2,1)S(1)}, bf16[80,768]{1,0:T(8,128)(2,1)S(1)}, u32[]{:S(2)}, u32[]{:S(2)}) %collective-permute-start.4) | collective-permute-done | bytes 122912 | tf_op jit(solution)/shard_map/ppermute | solution.py:253
  53.4 4.5 %collective-permute-done.5 = bf16[80,768]{1,0:T(8,128)(2,1)S(1)} collective-permute-done((bf16[80,768]{1,0:T(8,128)(2,1)S(1)}, bf16[80,768]{1,0:T(8,128)(2,1)S(1)}, u32[]{:S(2)}, u32[]{:S(2)}) %collective-permute-start.5) | collective-permute-done | bytes 122912 | tf_op jit(solution)/shard_map/ppermute | solution.py:253
  58.0 0.3 collective-permute-start.8
  58.3 2.3 %collective-permute-start.9 = (bf16[80,768]{1,0:T(8,128)(2,1)S(1)}, bf16[80,768]{1,0:T(8,128)(2,1)S(1)}, u32[]{:S(2)}, u32[]{:S(2)}) collective-permute-start(bf16[80,768]{1,0:T(8,128)(2,1)S(1)} %get-tuple-element.17), channel_id=1, source_target_pairs={{0,48},{16,0},{32,16},{48,32},{1,49},{17,1},{33,17},{49,33},{2,50}... | collective-permute-start | bytes 368648 | tf_op jit(solution)/shard_map/ppermute | solution.py:253
  60.7 3.2 %collective-permute-done.7 = bf16[80,768]{1,0:T(8,128)(2,1)S(1)} collective-permute-done((bf16[80,768]{1,0:T(8,128)(2,1)S(1)}, bf16[80,768]{1,0:T(8,128)(2,1)S(1)}, u32[]{:S(2)}, u32[]{:S(2)}) %collective-permute-start.7) | collective-permute-done | bytes 122912 | tf_op jit(solution)/shard_map/ppermute | solution.py:253
  63.8 0.5 collective-permute-done.8
  64.4 0.8 collective-permute-done.9
  65.2 0.2 collective-permute-start.10
  65.4 5.3 %collective-permute-start.11 = (bf16[80,768]{1,0:T(8,128)(2,1)S(1)}, bf16[80,768]{1,0:T(8,128)(2,1)S(1)}, u32[]{:S(2)}, u32[]{:S(2)}) collective-permute-start(bf16[80,768]{1,0:T(8,128)(2,1)S(1)} %fusion.1), channel_id=1, source_target_pairs={{0,128},{64,192},{128,0},{192,64},{1,129},{65,193},{129,1},{193,65... | collective-permute-start | bytes 368648 | tf_op jit(solution)/shard_map/ppermute | solution.py:253
  70.7 1.1 %collective-permute-done.10 = bf16[80,768]{1,0:T(8,128)(2,1)S(1)} collective-permute-done((bf16[80,768]{1,0:T(8,128)(2,1)S(1)}, bf16[80,768]{1,0:T(8,128)(2,1)S(1)}, u32[]{:S(2)}, u32[]{:S(2)}) %collective-permute-start.10) | collective-permute-done | bytes 122912 | tf_op jit(solution)/shard_map/ppermute | solution.py:253
  71.8 3.1 %collective-permute-done.11 = bf16[80,768]{1,0:T(8,128)(2,1)S(1)} collective-permute-done((bf16[80,768]{1,0:T(8,128)(2,1)S(1)}, bf16[80,768]{1,0:T(8,128)(2,1)S(1)}, u32[]{:S(2)}, u32[]{:S(2)}) %collective-permute-start.11) | collective-permute-done | bytes 122912 | tf_op jit(solution)/shard_map/ppermute | solution.py:253
  74.9 0.6 collective-permute-done.12
  75.6 2.3 %collective-permute-start.13 = (bf16[80,768]{1,0:T(8,128)(2,1)S(1)}, bf16[80,768]{1,0:T(8,128)(2,1)S(1)}, u32[]{:S(2)}, u32[]{:S(2)}) collective-permute-start(bf16[80,768]{1,0:T(8,128)(2,1)S(1)} %add_convert_fusion.mine), channel_id=1, source_target_pairs={{0,2},{2,0},{1,3},{3,1},{4,6},{6,4},{5,7},{7,5},{8,10},{10,8},{9,1... | collective-permute-start | bytes 368648 | tf_op jit(solution)/shard_map/ppermute | solution.py:329
  77.9 2.3 %grad_hidden.1 = bf16[256,1536]{1,0:T(8,128)(2,1)} custom-call(s32[3]{0:T(128)S(1)} %pad_add_fusion.places, bf16[64,256]{1,0:T(8,128)(2,1)S(1)} %convs.1.gvt, f32[264,128]{1,0:T(8,128)S(1)} %stats.1, f32[264,128]{1,0:T(8,128)S(1)} %collective-permute-done.2.stats_far, bf16[256,1536]{1,0:T(8,128)(2,1)S(1)} %copy-done, bf16[16,2,1536]{2,1,0:T(2,128)(2,1)S(1)} %copy-done.1, ...), custom_call_target="tpu_custom_call" | custom-call | flops 100000000 | bytes 2000000 | tf_op jit(solution)/shard_map/grad_hidden/pallas_call | solution.py:331
  80.2 1.5 %last.1 = (f32[1536,64]{1,0:T(8,128)S(1)}, f32[8,2,1536]{2,1,0:T(2,128)}) custom-call(s32[3]{0:T(128)S(1)} %pad_add_fusion.places, bf16[80,768]{1,0:T(8,128)(2,1)S(1)} %add_convert_fusion.mine, bf16[80,768]{1,0:T(8,128)(2,1)S(1)} %collective-permute-done.13.other, bf16[64,1536]{1,0:T(8,128)(2,1)S(1)} %bitcast.29), custom_call_target="tpu_custom_call" | custom-call | flops 10000000 | bytes 1000000 | tf_op jit(solution)/shard_map/last/pallas_call | solution.py:339
  81.7 1.0 %copy.19 = f32[1536,64]{0,1:T(8,128)} copy(f32[1536,64]{1,0:T(8,128)S(1)} %get-tuple-element.15) | data formatting | bytes 786432
  (32 shorter events, 0.8 us)
Async XLA Ops:
  0.6 16.2 %copy-start.3 = (bf16[16,8,128]{2,1,0:T(8,128)(2,1)S(1)}, bf16[16,8,128]{2,1,0:T(8,128)(2,1)}, u32[]{:S(2)}) copy-start(bf16[16,8,128]{2,1,0:T(8,128)(2,1)} %param.10) | copy-start | bytes 98308
  0.6 7.8 %copy-start.4 = (s32[8]{0:T(128)S(1)}, s32[8]{0:T(128)}, u32[]{:S(2)}) copy-start(s32[8]{0:T(128)} %param.15) | copy-start | bytes 100
  0.7 9.1 %copy-start = (bf16[256,1536]{1,0:T(8,128)(2,1)S(1)}, bf16[256,1536]{1,0:T(8,128)(2,1)}, u32[]{:S(2)}) copy-start(bf16[256,1536]{1,0:T(8,128)(2,1)} %hidden.5) | copy-start | bytes 2359300
  0.7 9.1 %copy-start.1 = (bf16[16,2,1536]{2,1,0:T(2,128)(2,1)S(1)}, bf16[16,2,1536]{2,1,0:T(2,128)(2,1)}, u32[]{:S(2)}) copy-start(bf16[16,2,1536]{2,1,0:T(2,128)(2,1)} %mod.5) | copy-start | bytes 294916
  0.7 16.2 %copy-start.5 = (f32[8]{0:T(128)S(1)}, f32[8]{0:T(128)}, u32[]{:S(2)}) copy-start(f32[8]{0:T(128)} %param.16) | copy-start | bytes 100
  0.7 17.5 %copy-start.2 = (bf16[9,512,16]{1,2,0:T(8,128)(2,1)S(1)}, bf16[9,512,16]{1,2,0:T(8,128)(2,1)}, u32[]{:S(2)}) copy-start(bf16[9,512,16]{1,2,0:T(8,128)(2,1)} %param.11) | copy-start | bytes 442372
  3.4 14.8 %collective-permute-start = (bf16[272,512]{1,0:T(8,128)(2,1)S(1)}, bf16[272,512]{1,0:T(8,128)(2,1)S(1)}, u32[]{:S(2)}, u32[]{:S(2)}) collective-permute-start(bf16[272,512]{1,0:T(8,128)(2,1)S(1)} %pad_maximum_fusion), channel_id=1, source_target_pairs={{0,2},{2,4},{4,6},{6,8},{8,10},{10,12},{12,14},{14,16},{16,18},{18... | collective-permute-start | bytes 835592 | tf_op jit(solution)/shard_map/ppermute | solution.py:279
  7.2 11.0 %collective-permute-start.1 = (bf16[272,512]{1,0:T(8,128)(2,1)}, bf16[272,512]{1,0:T(8,128)(2,1)S(1)}, u32[]{:S(2)}, u32[]{:S(2)}) collective-permute-start(bf16[272,512]{1,0:T(8,128)(2,1)} %pad_maximum_fusion.1), channel_id=1, source_target_pairs={{2,0},{4,2},{6,4},{8,6},{10,8},{12,10},{14,12},{16,14},{18,16},{20... | collective-permute-start | bytes 835592 | tf_op jit(solution)/shard_map/ppermute | solution.py:280
  10.8 26.4 %collective-permute-start.2 = (f32[264,128]{1,0:T(8,128)S(1)}, f32[264,128]{1,0:T(8,128)S(1)}, u32[]{:S(2)}, u32[]{:S(2)}) collective-permute-start(f32[264,128]{1,0:T(8,128)S(1)} %stats.1), channel_id=1, source_target_pairs={{0,1},{1,0},{2,3},{3,2},{4,5},{5,4},{6,7},{7,6},{8,9},{9,8},{10,11... | collective-permute-start | bytes 405512 | tf_op jit(solution)/shard_map/ppermute | solution.py:293
  38.4 8.5 %collective-permute-start.3 = (bf16[80,768]{1,0:T(8,128)(2,1)S(1)}, bf16[80,768]{1,0:T(8,128)(2,1)S(1)}, u32[]{:S(2)}, u32[]{:S(2)}) collective-permute-start(bf16[80,768]{1,0:T(8,128)(2,1)S(1)} %get-tuple-element.8), channel_id=1, source_target_pairs={{0,2},{2,0},{1,3},{3,1},{4,6},{6,4},{5,7},{7,5},{8,10},{10,8},{9,1... | collective-permute-start | bytes 368648 | tf_op jit(solution)/shard_map/ppermute | solution.py:328
  46.9 6.5 %collective-permute-start.4 = (bf16[80,768]{1,0:T(8,128)(2,1)S(1)}, bf16[80,768]{1,0:T(8,128)(2,1)S(1)}, u32[]{:S(2)}, u32[]{:S(2)}) collective-permute-start(bf16[80,768]{1,0:T(8,128)(2,1)S(1)} %fusion), channel_id=1, source_target_pairs={{0,4},{4,8},{8,12},{12,0},{1,5},{5,9},{9,13},{13,1},{2,6},{6,10},{... | collective-permute-start | bytes 368648 | tf_op jit(solution)/shard_map/ppermute | solution.py:253
  47.0 10.8 %collective-permute-start.5 = (bf16[80,768]{1,0:T(8,128)(2,1)S(1)}, bf16[80,768]{1,0:T(8,128)(2,1)S(1)}, u32[]{:S(2)}, u32[]{:S(2)}) collective-permute-start(bf16[80,768]{1,0:T(8,128)(2,1)S(1)} %fusion), channel_id=1, source_target_pairs={{0,8},{4,12},{8,0},{12,4},{1,9},{5,13},{9,1},{13,5},{2,10},{6,14},... | collective-permute-start | bytes 368648 | tf_op jit(solution)/shard_map/ppermute | solution.py:253
  47.1 10.7 %collective-permute-start.6 = (bf16[80,768]{1,0:T(8,128)(2,1)S(1)}, bf16[80,768]{1,0:T(8,128)(2,1)S(1)}, u32[]{:S(2)}, u32[]{:S(2)}) collective-permute-start(bf16[80,768]{1,0:T(8,128)(2,1)S(1)} %fusion), channel_id=1, source_target_pairs={{0,12},{4,0},{8,4},{12,8},{1,13},{5,1},{9,5},{13,9},{2,14},{6,2},{... | collective-permute-start | bytes 368648 | tf_op jit(solution)/shard_map/ppermute | solution.py:253
  57.9 5.9 %collective-permute-start.7 = (bf16[80,768]{1,0:T(8,128)(2,1)S(1)}, bf16[80,768]{1,0:T(8,128)(2,1)S(1)}, u32[]{:S(2)}, u32[]{:S(2)}) collective-permute-start(bf16[80,768]{1,0:T(8,128)(2,1)S(1)} %get-tuple-element.17), channel_id=1, source_target_pairs={{0,16},{16,32},{32,48},{48,0},{1,17},{17,33},{33,49},{49,1},{2,18}... | collective-permute-start | bytes 368648 | tf_op jit(solution)/shard_map/ppermute | solution.py:253
  58.0 6.4 %collective-permute-start.8 = (bf16[80,768]{1,0:T(8,128)(2,1)S(1)}, bf16[80,768]{1,0:T(8,128)(2,1)S(1)}, u32[]{:S(2)}, u32[]{:S(2)}) collective-permute-start(bf16[80,768]{1,0:T(8,128)(2,1)S(1)} %get-tuple-element.17), channel_id=1, source_target_pairs={{0,32},{16,48},{32,0},{48,16},{1,33},{17,49},{33,1},{49,17},{2,34}... | collective-permute-start | bytes 368648 | tf_op jit(solution)/shard_map/ppermute | solution.py:253
  58.3 6.8 %collective-permute-start.9 = (bf16[80,768]{1,0:T(8,128)(2,1)S(1)}, bf16[80,768]{1,0:T(8,128)(2,1)S(1)}, u32[]{:S(2)}, u32[]{:S(2)}) collective-permute-start(bf16[80,768]{1,0:T(8,128)(2,1)S(1)} %get-tuple-element.17), channel_id=1, source_target_pairs={{0,48},{16,0},{32,16},{48,32},{1,49},{17,1},{33,17},{49,33},{2,50}... | collective-permute-start | bytes 368648 | tf_op jit(solution)/shard_map/ppermute | solution.py:253
  65.2 6.6 %collective-permute-start.10 = (bf16[80,768]{1,0:T(8,128)(2,1)S(1)}, bf16[80,768]{1,0:T(8,128)(2,1)S(1)}, u32[]{:S(2)}, u32[]{:S(2)}) collective-permute-start(bf16[80,768]{1,0:T(8,128)(2,1)S(1)} %fusion.1), channel_id=1, source_target_pairs={{0,64},{64,128},{128,192},{192,0},{1,65},{65,129},{129,193},{193,1... | collective-permute-start | bytes 368648 | tf_op jit(solution)/shard_map/ppermute | solution.py:253
  65.4 9.5 %collective-permute-start.11 = (bf16[80,768]{1,0:T(8,128)(2,1)S(1)}, bf16[80,768]{1,0:T(8,128)(2,1)S(1)}, u32[]{:S(2)}, u32[]{:S(2)}) collective-permute-start(bf16[80,768]{1,0:T(8,128)(2,1)S(1)} %fusion.1), channel_id=1, source_target_pairs={{0,128},{64,192},{128,0},{192,64},{1,129},{65,193},{129,1},{193,65... | collective-permute-start | bytes 368648 | tf_op jit(solution)/shard_map/ppermute | solution.py:253
  70.7 4.8 %collective-permute-start.12 = (bf16[80,768]{1,0:T(8,128)(2,1)S(1)}, bf16[80,768]{1,0:T(8,128)(2,1)S(1)}, u32[]{:S(2)}, u32[]{:S(2)}) collective-permute-start(bf16[80,768]{1,0:T(8,128)(2,1)S(1)} %fusion.1), channel_id=1, source_target_pairs={{0,192},{64,0},{128,64},{192,128},{1,193},{65,1},{129,65},{193,129... | collective-permute-start | bytes 368648 | tf_op jit(solution)/shard_map/ppermute | solution.py:253
  75.6 4.6 %collective-permute-start.13 = (bf16[80,768]{1,0:T(8,128)(2,1)S(1)}, bf16[80,768]{1,0:T(8,128)(2,1)S(1)}, u32[]{:S(2)}, u32[]{:S(2)}) collective-permute-start(bf16[80,768]{1,0:T(8,128)(2,1)S(1)} %add_convert_fusion.mine), channel_id=1, source_target_pairs={{0,2},{2,0},{1,3},{3,1},{4,6},{6,4},{5,7},{7,5},{8,10},{10,8},{9,1... | collective-permute-start | bytes 368648 | tf_op jit(solution)/shard_map/ppermute | solution.py:329

commit v3 on v2

v3 whole, which is shorter than its diff:
```python
import functools

import jax
import jax.numpy as jnp
from jax import lax
from jax.experimental import pallas as pl
from jax.experimental.pallas import tpu as pltpu
from jax.sharding import Mesh, PartitionSpec as P

BF = jnp.bfloat16
F32 = jnp.float32
TILE = ("y", "x", "zl", "core")
RINGS = ("zl", "x", "y")
OVER_0 = (((0,), (0,)), ((), ()))
OVER_1 = (((1,), (1,)), ((), ()))
WHOLE = pl.BlockSpec(memory_space=pltpu.VMEM)
SCALARS = pl.BlockSpec(memory_space=pltpu.SMEM)


def dot(a, b, dims=(((1,), (0,)), ((), ()))):
    return lax.dot_general(a, b, dims, preferred_element_type=F32)


def before(v, axis):
    place = lax.broadcasted_iota(jnp.int32, v.shape, axis)
    return jnp.where(place == 0, 0.0, pltpu.roll(v, 1, axis))


def after(v, axis):
    n = v.shape[axis]
    place = lax.broadcasted_iota(jnp.int32, v.shape, axis)
    return jnp.where(place == n - 1, 0.0, pltpu.roll(v, n - 1, axis))


def sigmoid(h):
    return 0.5 + 0.5 * jnp.tanh(0.5 * h)


def put_beside(ref, i, v):
    at = pl.ds(i * v.shape[0], v.shape[0])
    ref[0, at, :] = before(v, 0).astype(BF)
    ref[1, at, :] = v.astype(BF)
    ref[2, at, :] = after(v, 0).astype(BF)


def keeper(rows, width, images):
    row_start = place_of(rows, width, images)[1]
    top = jnp.where(row_start > 0, 1.0, 0.0)
    bottom = jnp.where(row_start + rows < width, 1.0, 0.0)

    def masked(v, row):
        return v * top if row < 0 else v * bottom if row >= rows else v

    return masked


def line_of(low, own, high, row):
    if row < 0:
        return low[low.shape[0] + row]
    return own[row] if row < own.shape[0] else high[row - own.shape[0]]


def forward_kernel(geometry, lat_low, lat_own, lat_high, w1, w2_far, slope_two, slope_one, lats, acts,
                   w2, sem):
    rows, width, _ = geometry
    load = pltpu.make_async_copy(w2_far, w2, sem)
    load.start()
    masked = keeper(*geometry)
    for i in range(rows + 8):
        row = i - 4
        v = masked(line_of(lat_low, lat_own, lat_high, row).astype(F32), row)
        lats[0, i] = before(v, 1).astype(BF)
        lats[1, i] = v.astype(BF)
        lats[2, i] = after(v, 1).astype(BF)

    for i in range(rows + 6):
        row = i - 3
        taps = [lats[kx, i + ky] for ky in range(3) for kx in range(3)]
        pre = dot(jnp.concatenate(taps, 0), w1[...], OVER_0)
        s = sigmoid(pre)
        if -1 <= row <= rows:
            slope_one[pl.ds((row + 1) * width, width), :] = s * (1.0 + pre * (1.0 - s))
        put_beside(acts, i, masked((pre * s).astype(BF).astype(F32), row))

    load.wait()
    per = 2
    for i in range(0, rows + 4, per):
        pre = None
        for ky in range(3):
            for kx in range(3):
                part = dot(acts[kx, pl.ds((i + ky) * width, per * width), :], w2[3 * ky + kx], OVER_1)
                pre = part if pre is None else pre + part
        s = sigmoid(pre)
        slope_two[pl.ds(i * width, per * width), :] = s * (1.0 + pre * (1.0 - s))


def backward_kernel(geometry, steps, slope_two, slope_one, cot_low, cot_own, cot_high, w1t, w2, out,
                    grads, inner):
    rows, width, _ = geometry
    ch = w1t.shape[0] // 9
    masked = keeper(*geometry)
    step = -steps[place_of(*geometry)[0]]
    for i in range(rows + 4):
        cot = line_of(cot_low, cot_own, cot_high, i - 2).astype(F32)
        g = masked(cot * slope_two[pl.ds(i * width, width), :], i - 2)
        put_beside(grads, i, g.astype(BF).astype(F32))

    per = 2
    for i in range(0, rows + 2, per):
        back = None
        for ky in range(3):
            for kx in range(3):
                part = dot(grads[2 - kx, pl.ds((i + 2 - ky) * width, per * width), :], w2[3 * ky + kx])
                back = part if back is None else back + part
        for j in range(per):
            at = pl.ds((i + j) * width, width)
            g = back[j * width : (j + 1) * width] * slope_one[at, :]
            inner[at, :] = masked(g, i + j - 1).astype(BF)

    taps = dot(w1t[...], inner[...], OVER_1)
    lines = []
    for row in range(rows):
        by_kx = []
        for kx in range(3):
            total = None
            for ky in range(3):
                k = 3 * ky + kx
                at = (row + 2 - ky) * width
                part = taps[k * ch : (k + 1) * ch, at : at + width]
                total = part if total is None else total + part
            by_kx.append(total)
        whole = after(by_kx[0], 1) + by_kx[1] + before(by_kx[2], 1)
        lines.append((whole * step).astype(BF))

    half = width // 2
    spot = lax.broadcasted_iota(jnp.int32, (2 * width, 2 * width), 0)
    goal = lax.broadcasted_iota(jnp.int32, (2 * width, 2 * width), 1)
    within = lax.rem(goal, width)
    pick = (lax.div(spot, width) == lax.div(within, half)) & (
        lax.rem(spot, width) == 2 * lax.rem(within, half) + lax.div(goal, width)
    )
    pick = jnp.where(pick, 1.0, 0.0).astype(BF)
    stacked = [
        jnp.concatenate([lines[4 * h + a], lines[4 * h + 2 + a]], 1)
        for h in range(rows // 4)
        for a in range(2)
    ]
    apart = dot(jnp.concatenate(stacked, 0), pick).astype(BF)
    by_tap = jnp.concatenate(
        [
            jnp.concatenate(
                [
                    apart[(2 * h + a) * ch : (2 * h + a + 1) * ch, b * width : (b + 1) * width]
                    for h in range(rows // 4)
                ],
                1,
            )
            for a in range(2)
            for b in range(2)
        ],
        0,
    )
    goal = lax.broadcasted_iota(jnp.int32, (4 * ch, 4 * ch), 0)
    spot = lax.broadcasted_iota(jnp.int32, (4 * ch, 4 * ch), 1)
    order = jnp.where(goal == 4 * lax.rem(spot, ch) + lax.div(spot, ch), 1.0, 0.0).astype(BF)
    out[...] = dot(order, by_tap).astype(BF)


def place_of(rows, width, images):
    tile = 0
    for axis in TILE:
        tile = tile * lax.axis_size(axis) + lax.axis_index(axis)
    row = tile * rows + width // 2
    return lax.rem(lax.div(row, width), images), lax.rem(row, width)


def shift_and_gain(prompt, mod):
    chosen = mod[prompt].astype(F32)
    return chosen[0:1], 1.0 + chosen[1:2]


def stats_kernel(geometry, prompts, hidden, mod, wt, out):
    _, gain = shift_and_gain(prompts[place_of(*geometry)[0]], mod)
    patch = wt.shape[0]
    tokens = hidden.shape[0]
    w_gain = (wt[...].astype(F32) * gain).astype(BF)
    out[...] = jnp.zeros_like(out)
    out[0:tokens, 0:patch] = dot(hidden[...], w_gain, OVER_1)
    states = hidden[...].astype(F32)
    out[0:tokens, patch : patch + 1] = jnp.sum(states, axis=1, keepdims=True)
    out[0:tokens, patch + 1 : patch + 2] = jnp.sum(states * states, axis=1, keepdims=True)
    out[tokens:, 0:patch] = dot(jnp.ones((8, wt.shape[1]), BF), w_gain, OVER_1)


def norm_of(width_all, patch, stats, stats_far, hidden):
    tokens = hidden.shape[0]
    both = stats[...] + stats_far[...]
    mean_val = both[0:tokens, patch : patch + 1] / width_all
    spread = both[0:tokens, patch + 1 : patch + 2] / width_all - mean_val * mean_val
    scale = 1.0 / jnp.sqrt(spread + 1e-06)
    w_sum = both[tokens : tokens + 1, 0:patch]
    cross = (both[0:tokens, 0:patch] - mean_val * w_sum) * scale
    return (hidden[...].astype(F32) - mean_val) * scale, scale, w_sum, cross


def sums_kernel(width_all, geometry, prompts, gvt, stats, stats_far, hidden, mod, wt, send, keep, held):
    patch = gvt.shape[0]
    image, images = place_of(*geometry)[0], geometry[2]
    shift, gain = shift_and_gain(prompts[image], mod)
    normed = norm_of(width_all, patch, stats, stats_far, hidden)[0]
    cross_grad = dot(gvt[...], normed.astype(BF))
    column = jnp.sum(gvt[...].astype(F32), axis=1, keepdims=True)
    held[0:patch, :] = cross_grad * gain + shift * column
    mod_row = jnp.sum(cross_grad * wt[...].astype(F32), axis=0, keepdims=True)
    spot = lax.broadcasted_iota(jnp.int32, (images, mod_row.shape[1]), 0)
    held[patch : patch + images, :] = jnp.where(spot == image, mod_row, 0.0)
    row = dot(jnp.ones((8, gvt.shape[1]), BF), gvt[...], OVER_1)
    held[patch + images :, :] = jnp.zeros((8, mod_row.shape[1]), F32)
    wide = jnp.concatenate([row] * images, 1)
    lane = lax.broadcasted_iota(jnp.int32, wide.shape, 1)
    held[patch + images :, 0 : images * patch] = jnp.where(lax.div(lane, patch) == image, wide, 0.0)
    half = keep.shape[1]
    core = lax.axis_index("core")
    keep[...] = held[:, pl.ds(pl.multiple_of(core * half, half), half)]
    send[...] = held[:, pl.ds(pl.multiple_of((1 - core) * half, half), half)].astype(BF)


def hidden_kernel(width_all, geometry, prompts, gvt, stats, stats_far, hidden, mod, wt, out):
    patch = gvt.shape[0]
    _, gain = shift_and_gain(prompts[place_of(*geometry)[0]], mod)
    normed, scale, w_sum, cross = norm_of(width_all, patch, stats, stats_far, hidden)
    gv = gvt[...].astype(F32).T
    first = jnp.sum(gv * w_sum, axis=1, keepdims=True) / width_all
    second = jnp.sum(gv * cross, axis=1, keepdims=True) / width_all
    grad = dot(gv.astype(BF), wt[...]) * gain
    out[...] = ((grad - first - normed * second) * scale).astype(BF)


def last_kernel(images, mine, other, wt, proj, mod):
    patch = wt.shape[0]
    half = mine.shape[1]
    core = lax.axis_index("core")
    for block, place in ((mine, core), (other, 1 - core)):
        at = pl.ds(pl.multiple_of(place * half, half), half)
        proj[:, at] = block[0:patch, :].astype(F32)
        mod[:, 1, at] = block[patch : patch + images, :].astype(F32)
    wide = images * patch
    mine_sum = mine[patch:, 0:wide].astype(F32)[images : images + 1]
    other_sum = other[patch:, 0:wide].astype(F32)[images : images + 1]
    line = jnp.where(core == 0, mine_sum, other_sum)
    sums = jnp.concatenate([line[:, i * patch : (i + 1) * patch] for i in range(images)], 0)
    mod[:, 0, :] = dot(sums.astype(BF), wt[...])


def call(kernel, out_shape, n_in, cost, name, scratch=(), smem=1, far=0):
    return pl.pallas_call(
        kernel,
        out_shape=out_shape,
        in_specs=[SCALARS] * smem + [WHOLE] * (n_in - smem - far) + [pl.BlockSpec(memory_space=pl.ANY)] * far,
        out_specs=jax.tree.map(lambda _: WHOLE, out_shape),
        scratch_shapes=list(scratch),
        compiler_params=pltpu.CompilerParams(vmem_limit_bytes=40 * 2**20),
        cost_estimate=pl.CostEstimate(flops=cost[0], bytes_accessed=cost[1], transcendentals=0),
        name=name,
    )


def sum_over_rings(total, beside):
    for axis in RINGS:
        count = lax.axis_size(axis)
        out = total.astype(BF)
        came = [
            lax.ppermute(out, axis, [(i, (i + d) % count) for i in range(count)])
            for d in range(1, count)
        ]
        if axis == RINGS[0]:
            came, beside = lax.optimization_barrier((came, beside))
        for block in came:
            total = total + block.astype(F32)
    return total, beside


def body(feat_cot, latent, dec_w1, dec_w2, hidden, modulation, prompt_ids, step_size, proj_w):
    ch, rows, width = latent.shape
    mid = dec_w2.shape[1]
    images = prompt_ids.shape[0]
    tokens, features = hidden.shape
    patch = proj_w.shape[1]
    width_all = lax.axis_size("mp") * features
    geometry = (rows, width, images)
    count = lax.axis_size(TILE)
    up = [(i, (i + 1) % count) for i in range(count)]
    down = [(b, a) for a, b in up]

    lat_own = lax.optimization_barrier(latent.transpose(1, 0, 2))
    lat_low = lax.ppermute(lat_own[-4:], TILE, up)
    lat_high = lax.ppermute(lat_own[:4], TILE, down)
    cot_own = lax.optimization_barrier(feat_cot.transpose(1, 2, 0))
    cot_low = lax.ppermute(cot_own[-2:], TILE, up)
    cot_high = lax.ppermute(cot_own[:2], TILE, down)
    wt = proj_w.T

    stats = call(
        functools.partial(stats_kernel, geometry),
        jax.ShapeDtypeStruct((tokens + 8, 128), F32),
        4,
        (10**8, 10**6),
        "stats",
    )(prompt_ids, hidden, modulation, wt)
    stats_far = lax.ppermute(stats, "mp", [(0, 1), (1, 0)])

    w1 = dec_w1.transpose(0, 2, 1).reshape(9 * ch, mid)
    slope_two, slope_one = call(
        functools.partial(forward_kernel, geometry),
        (
            jax.ShapeDtypeStruct(((rows + 4) * width, mid), F32),
            jax.ShapeDtypeStruct(((rows + 2) * width, mid), F32),
        ),
        5,
        (8 * 10**9, 8 * 10**6),
        "forward",
        scratch=(
            pltpu.VMEM((3, rows + 8, ch, width), BF),
            pltpu.VMEM((3, (rows + 6) * width, mid), BF),
            pltpu.VMEM(dec_w2.shape, BF),
            pltpu.SemaphoreType.DMA,
        ),
        smem=0,
        far=1,
    )(lat_low, lat_own, lat_high, w1, dec_w2)
    gvt = call(
        functools.partial(backward_kernel, geometry),
        jax.ShapeDtypeStruct((4 * ch, tokens), BF),
        8,
        (7 * 10**9, 8 * 10**6),
        "backward",
        scratch=(
            pltpu.VMEM((3, (rows + 4) * width, mid), BF),
            pltpu.VMEM(((rows + 2) * width, mid), BF),
        ),
    )(step_size, slope_two, slope_one, cot_low, cot_own, cot_high, w1, dec_w2)

    lines = patch + images + 8
    half = features // 2
    send, keep = call(
        functools.partial(sums_kernel, width_all, geometry),
        (jax.ShapeDtypeStruct((lines, half), BF), jax.ShapeDtypeStruct((lines, half), F32)),
        7,
        (10**8, 2 * 10**6),
        "sums",
        scratch=(pltpu.VMEM((lines, features), F32),),
    )(prompt_ids, gvt, stats, stats_far, hidden, modulation, wt)
    grad_hidden = call(
        functools.partial(hidden_kernel, width_all, geometry),
        jax.ShapeDtypeStruct((tokens, features), BF),
        7,
        (10**8, 2 * 10**6),
        "grad_hidden",
    )(prompt_ids, gvt, stats, stats_far, hidden, modulation, wt)

    swap = [(0, 1), (1, 0)]
    total, grad_hidden = sum_over_rings(
        keep + lax.ppermute(send, "core", swap).astype(F32), grad_hidden
    )
    mine = total.astype(BF)
    other = lax.ppermute(mine, "core", swap)

    grad_proj, grad_mod = call(
        functools.partial(last_kernel, images),
        (
            jax.ShapeDtypeStruct((patch, features), F32),
            jax.ShapeDtypeStruct((images, 2, features), F32),
        ),
        3,
        (10**7, 10**6),
        "last",
        smem=0,
    )(mine, other, wt)
    return (grad_hidden, grad_proj.T, grad_mod)


def solution(mesh):
    fine = Mesh(mesh.devices.reshape(4, 4, 4, 2, 2), ("y", "x", "zl", "core", "mp"))
    return jax.shard_map(
        body,
        mesh=fine,
        in_specs=(
            P(None, TILE, None),
            P(None, TILE, None),
            P(),
            P(),
            P(TILE, "mp"),
            P(None, None, "mp"),
            P(),
            P(),
            P("mp", None),
        ),
        out_specs=(P(TILE, "mp"), P("mp", None), P(None, None, "mp")),
        check_vma=False,
    )
```

time: 83.5 us -> 85 us (1.018)
  starting transfers between devices: 30.7 us -> 36.6 us
  other arithmetic: 1.8 us -> 0.29 us
  Pallas kernels: 25 us -> 24 us
  local copies, waits for them, and re-layouts: 5.84 us -> 4.89 us
  waiting for transfers between devices: 17.9 us -> 17 us
    ppermute x2 -> x4, starting transfers between devices: 3.34 us -> 11.2 us  [the longest x1 6.32 us: body(): cot_high = lax.ppermute(cot_own[:2], TILE, down)]
    ppermute x9, starting transfers between devices: 11.5 us -> 7.71 us  [sum_over_rings(): lax.ppermute(out, axis, [(i, (i + d) % count) for i in range(count)])]
    unnamed x17 -> x18, local copies, waits for them, and re-layouts: 2.75 us -> 4.84 us
    ppermute x1, starting transfers between devices: 2.33 us -> 4.39 us  [body(): other = lax.ppermute(mine, 'core', swap)]
    ppermute x9, waiting for transfers between devices: 16.9 us -> 15 us  [sum_over_rings(): lax.ppermute(out, axis, [(i, (i + d) % count) for i in range(count)])]
    dynamic_slice x2 -> x0, local copies, waits for them, and re-layouts: 1.19 us -> none  [the longest x1 0.6 us: body(): places = jnp.stack([prompt_ids[image], image, core]).astype(jnp.int32)]
    reshape x2 -> x0, local copies, waits for them, and re-layouts: 1.01 us -> none  [body(): proj_w.reshape(features, ch, 4).transpose(2, 1, 0).reshape(patch, features)]
    ppermute x1, waiting for transfers between devices: 0.01 us -> 0.98 us  [body(): other = lax.ppermute(mine, 'core', swap)]
  transfers between devices with their start and end apart: 14 -> 16, of which waited for: 9 -> 8; matrix products, arithmetic and copies ran while one was open for 4% -> 2% of each run, Pallas kernels for 27% -> 26%
where the time goes in v3:
time: 85 us; the launch traced here: 83.6 us
  starting transfers between devices  36.6 us (43%)
  Pallas kernels  24 us (28%)
  waiting for transfers between devices  17 us (20%)
  local copies, waits for them, and re-layouts  4.89 us (6%)
    ppermute x9, waiting for transfers between devices, sum_over_rings(): lax.ppermute(out, axis, [(i, (i + d) % count) for i in range(count)])  15 us
    pallas_call x1, Pallas kernels, body(): call(functools.partial(forward_kernel, geometry), (jax.ShapeDtypeStruct((...  10.5 us
    pallas_call x1, Pallas kernels, body(): call(functools.partial(backward_kernel, geometry), jax.ShapeDtypeStruct((...  8.18 us
    ppermute x1, starting transfers between devices, body(): lax.ppermute(send, 'core', swap).astype(F32)  8.02 us
    ppermute x9, starting transfers between devices, sum_over_rings(): lax.ppermute(out, axis, [(i, (i + d) % count) for i in range(count)])  7.71 us
    ppermute x1, starting transfers between devices, body(): cot_high = lax.ppermute(cot_own[:2], TILE, down)  6.32 us
    ppermute x1, starting transfers between devices, body(): stats_far = lax.ppermute(stats, 'mp', [(0, 1), (1, 0)])  5.24 us
    unnamed x18, local copies, waits for them, and re-layouts  4.84 us
  transfers between devices with their start and end apart: 16, of which 8 were waited for; matrix products, arithmetic and copies ran while one was open for 2% of the time, Pallas kernels for 26%

profile of v3, /device:TPU:1, one launch (start us, length us, event | category | flops | bytes accessed | tf_op | source)
XLA Modules:
  0.0 83.6 jit_solution(5451773494920798686)
XLA Ops:
  0.7 0.9 %copy.15 = bf16[16,8,128]{2,0,1:T(8,128)(2,1)S(1)} copy(bf16[16,8,128]{2,1,0:T(8,128)(2,1)} %param.10) | data formatting | bytes 65536 | tf_op args[1]
  1.5 3.1 %collective-permute-start = (bf16[4,16,128]{2,1,0:T(8,128)(2,1)S(1)}, bf16[4,16,128]{2,1,0:T(8,128)(2,1)S(1)}, u32[]{:S(2)}, u32[]{:S(2)}) collective-permute-start(bf16[4,16,128]{2,1,0:T(8,128)(2,1)S(1)} %get-tuple-element.28), channel_id=1, source_target_pairs={{0,2},{2,4},{4,6},{6,8},{8,10},{10,12},{12,14},{14,16},{16,18},{18... | collective-permute-start | bytes 49160 | tf_op jit(solution)/shard_map/ppermute | solution.py:296
  4.7 0.3 collective-permute-start.1
  5.0 1.6 %copy.13 = bf16[512,8,128]{0,2,1:T(8,128)(2,1)S(1)} copy(bf16[512,8,128]{2,1,0:T(8,128)(2,1)} %param.9) | data formatting | bytes 2097152 | tf_op args[0]
  6.6 1.5 %collective-permute-start.2 = (bf16[2,128,512]{2,1,0:T(8,128)(2,1)S(1)}, bf16[2,128,512]{2,1,0:T(8,128)(2,1)S(1)}, u32[]{:S(2)}, u32[]{:S(2)}) collective-permute-start(bf16[2,128,512]{2,1,0:T(8,128)(2,1)S(1)} %get-tuple-element.26), channel_id=1, source_target_pairs={{0,2},{2,4},{4,6},{6,8},{8,10},{10,12},{12,14},{14,16},{16,18},{18... | collective-permute-start | bytes 786440 | tf_op jit(solution)/shard_map/ppermute | solution.py:299
  8.2 6.3 %collective-permute-start.3 = (bf16[2,128,512]{2,1,0:T(8,128)(2,1)S(1)}, bf16[2,128,512]{2,1,0:T(8,128)(2,1)S(1)}, u32[]{:S(2)}, u32[]{:S(2)}) collective-permute-start(bf16[2,128,512]{2,1,0:T(8,128)(2,1)S(1)} %get-tuple-element.25), channel_id=1, source_target_pairs={{2,0},{4,2},{6,4},{8,6},{10,8},{12,10},{14,12},{16,14},{18,16},{20... | collective-permute-start | bytes 786440 | tf_op jit(solution)/shard_map/ppermute | solution.py:300
  14.5 1.0 %stats.1 = f32[264,128]{1,0:T(8,128)S(1)} custom-call(s32[8]{0:T(128)S(1)} %copy-done.3, bf16[256,1536]{1,0:T(8,128)(2,1)S(1)} %copy-done, bf16[16,2,1536]{2,1,0:T(2,128)(2,1)S(1)} %copy-done.2, bf16[64,1536]{1,0:T(8,128)(2,1)S(1)} %bitcast.9), custom_call_target="tpu_custom_call" | custom-call | flops 100000000 | bytes 1000000 | tf_op jit(solution)/shard_map/stats/pallas_call | solution.py:303
  15.5 5.2 %collective-permute-start.4 = (f32[264,128]{1,0:T(8,128)S(1)}, f32[264,128]{1,0:T(8,128)S(1)}, u32[]{:S(2)}, u32[]{:S(2)}) collective-permute-start(f32[264,128]{1,0:T(8,128)S(1)} %stats.1), channel_id=1, source_target_pairs={{0,1},{1,0},{2,3},{3,2},{4,5},{5,4},{6,7},{7,6},{8,9},{9,8},{10,11... | collective-permute-start | bytes 405512 | tf_op jit(solution)/shard_map/ppermute | solution.py:310
  20.8 2.3 %copy-done.4 = bf16[9,512,512]{2,1,0:T(8,128)(2,1)S(1)} copy-done((bf16[9,512,512]{2,1,0:T(8,128)(2,1)S(1)}, bf16[9,512,512]{2,1,0:T(8,128)(2,1)}, u32[]{:S(2)}) %copy-start.4) | copy-done | bytes 4718616
  23.1 10.5 %forward.1 = (f32[1536,512]{1,0:T(8,128)S(1)}, f32[1280,512]{1,0:T(8,128)S(1)}) custom-call(bf16[4,16,128]{2,1,0:T(8,128)(2,1)S(1)} %collective-permute-done.lat_low, bf16[8,16,128]{2,1,0:T(8,128)(2,1)S(1)} %bitcast.16, bf16[4,16,128]{2,1,0:T(8,128)(2,1)S(1)} %collective-permute-done.1.lat_high, bf16[144,512]{1,0:T(8,128)(2,1)S(1)} %bitcast.17, ...), custom_call_target="tpu_custom_call" | custom-call | flops 8000000000 | bytes 8000000 | tf_op jit(solution)/shard_map/forward/pallas_call | solution.py:313
  33.7 8.2 %backward.1.gvt = bf16[64,256]{1,0:T(8,128)(2,1)S(1)} custom-call(f32[8]{0:T(128)S(1)} %copy-done.7, f32[1536,512]{1,0:T(8,128)S(1)} %get-tuple-element.13.slope_two, f32[1280,512]{1,0:T(8,128)S(1)} %get-tuple-element.14.slope_one, bf16[2,128,512]{2,1,0:T(8,128)(2,1)S(1)} %collective-permute-done.2.cot_low, bf16[8,128,512]{2,1,0:T(8,128)(2,1)S(1)} %bitcast.14, ...), custom_call_target="tpu_custom_call" | custom-call | flops 7000000000 | bytes 8000000 | tf_op jit(solution)/shard_map/backward/pallas_call | solution.py:331
  41.9 1.1 %sums.1 = (bf16[80,768]{1,0:T(8,128)(2,1)S(1)}, f32[80,768]{1,0:T(8,128)S(1)}) custom-call(s32[8]{0:T(128)S(1)} %copy-done.3, bf16[64,256]{1,0:T(8,128)(2,1)S(1)} %backward.1.gvt, f32[264,128]{1,0:T(8,128)S(1)} %stats.1, f32[264,128]{1,0:T(8,128)S(1)} %collective-permute-done.4.stats_far, bf16[256,1536]{1,0:T(8,128)(2,1)S(1)} %copy-done, ...), custom_call_target="tpu_custom_call" | custom-call | flops 100000000 | bytes 2000000 | tf_op jit(solution)/shard_map/sums/pallas_call | solution.py:345
  43.0 8.0 %collective-permute-start.5 = (bf16[80,768]{1,0:T(8,128)(2,1)S(1)}, bf16[80,768]{1,0:T(8,128)(2,1)S(1)}, u32[]{:S(2)}, u32[]{:S(2)}) collective-permute-start(bf16[80,768]{1,0:T(8,128)(2,1)S(1)} %get-tuple-element.16), channel_id=1, source_target_pairs={{0,2},{2,0},{1,3},{3,1},{4,6},{6,4},{5,7},{7,5},{8,10},{10,8},{9,1... | collective-permute-start | bytes 368648 | tf_op jit(solution)/shard_map/ppermute | solution.py:363
  51.1 1.0 %collective-permute-done.5 = bf16[80,768]{1,0:T(8,128)(2,1)S(1)} collective-permute-done((bf16[80,768]{1,0:T(8,128)(2,1)S(1)}, bf16[80,768]{1,0:T(8,128)(2,1)S(1)}, u32[]{:S(2)}, u32[]{:S(2)}) %collective-permute-start.5) | collective-permute-done | bytes 122912 | tf_op jit(solution)/shard_map/ppermute | solution.py:363
  52.1 0.1 collective-permute-start.6
  52.2 0.1 collective-permute-start.7
  52.3 3.2 %collective-permute-start.8 = (bf16[80,768]{1,0:T(8,128)(2,1)S(1)}, bf16[80,768]{1,0:T(8,128)(2,1)S(1)}, u32[]{:S(2)}, u32[]{:S(2)}) collective-permute-start(bf16[80,768]{1,0:T(8,128)(2,1)S(1)} %fusion), channel_id=1, source_target_pairs={{0,12},{4,0},{8,4},{12,8},{1,13},{5,1},{9,5},{13,9},{2,14},{6,2},{... | collective-permute-start | bytes 368648 | tf_op jit(solution)/shard_map/ppermute | solution.py:273
  55.4 2.2 %grad_hidden.1 = bf16[256,1536]{1,0:T(8,128)(2,1)} custom-call(s32[8]{0:T(128)S(1)} %copy-done.3, bf16[64,256]{1,0:T(8,128)(2,1)S(1)} %backward.1.gvt, f32[264,128]{1,0:T(8,128)S(1)} %stats.1, f32[264,128]{1,0:T(8,128)S(1)} %collective-permute-done.4.stats_far, bf16[256,1536]{1,0:T(8,128)(2,1)S(1)} %copy-done, bf16[16,2,1536]{2,1,0:T(2,128)(2,1)S(1)} %copy-done.2, ...), custom_call_target="tpu_custom_call" | custom-call | flops 100000000 | bytes 2000000 | tf_op jit(solution)/shard_map/grad_hidden/pallas_call | solution.py:353
  57.7 0.9 %collective-permute-done.6 = bf16[80,768]{1,0:T(8,128)(2,1)S(1)} collective-permute-done((bf16[80,768]{1,0:T(8,128)(2,1)S(1)}, bf16[80,768]{1,0:T(8,128)(2,1)S(1)}, u32[]{:S(2)}, u32[]{:S(2)}) %collective-permute-start.6) | collective-permute-done | bytes 122912 | tf_op jit(solution)/shard_map/ppermute | solution.py:273
  58.5 4.5 %collective-permute-done.7 = bf16[80,768]{1,0:T(8,128)(2,1)S(1)} collective-permute-done((bf16[80,768]{1,0:T(8,128)(2,1)S(1)}, bf16[80,768]{1,0:T(8,128)(2,1)S(1)}, u32[]{:S(2)}, u32[]{:S(2)}) %collective-permute-start.7) | collective-permute-done | bytes 122912 | tf_op jit(solution)/shard_map/ppermute | solution.py:273
  63.1 0.1 collective-permute-start.10
  63.3 1.5 %collective-permute-start.9 = (bf16[80,768]{1,0:T(8,128)(2,1)S(1)}, bf16[80,768]{1,0:T(8,128)(2,1)S(1)}, u32[]{:S(2)}, u32[]{:S(2)}) collective-permute-start(bf16[80,768]{1,0:T(8,128)(2,1)S(1)} %get-tuple-element.23), channel_id=1, source_target_pairs={{0,16},{16,32},{32,48},{48,0},{1,17},{17,33},{33,49},{49,1},{2,18}... | collective-permute-start | bytes 368648 | tf_op jit(solution)/shard_map/ppermute | solution.py:273
  64.7 3.8 %collective-permute-done.10 = bf16[80,768]{1,0:T(8,128)(2,1)S(1)} collective-permute-done((bf16[80,768]{1,0:T(8,128)(2,1)S(1)}, bf16[80,768]{1,0:T(8,128)(2,1)S(1)}, u32[]{:S(2)}, u32[]{:S(2)}) %collective-permute-start.10) | collective-permute-done | bytes 122912 | tf_op jit(solution)/shard_map/ppermute | solution.py:273
  68.5 1.7 %collective-permute-done.9 = bf16[80,768]{1,0:T(8,128)(2,1)S(1)} collective-permute-done((bf16[80,768]{1,0:T(8,128)(2,1)S(1)}, bf16[80,768]{1,0:T(8,128)(2,1)S(1)}, u32[]{:S(2)}, u32[]{:S(2)}) %collective-permute-start.9) | collective-permute-done | bytes 122912 | tf_op jit(solution)/shard_map/ppermute | solution.py:273
  70.4 1.5 %collective-permute-start.13 = (bf16[80,768]{1,0:T(8,128)(2,1)S(1)}, bf16[80,768]{1,0:T(8,128)(2,1)S(1)}, u32[]{:S(2)}, u32[]{:S(2)}) collective-permute-start(bf16[80,768]{1,0:T(8,128)(2,1)S(1)} %fusion.1), channel_id=1, source_target_pairs={{0,128},{64,192},{128,0},{192,64},{1,129},{65,193},{129,1},{193,65... | collective-permute-start | bytes 368648 | tf_op jit(solution)/shard_map/ppermute | solution.py:273
  71.9 1.2 %collective-permute-start.14 = (bf16[80,768]{1,0:T(8,128)(2,1)S(1)}, bf16[80,768]{1,0:T(8,128)(2,1)S(1)}, u32[]{:S(2)}, u32[]{:S(2)}) collective-permute-start(bf16[80,768]{1,0:T(8,128)(2,1)S(1)} %fusion.1), channel_id=1, source_target_pairs={{0,192},{64,0},{128,64},{192,128},{1,193},{65,1},{129,65},{193,129... | collective-permute-start | bytes 368648 | tf_op jit(solution)/shard_map/ppermute | solution.py:273
  73.1 3.6 %collective-permute-done.12 = bf16[80,768]{1,0:T(8,128)(2,1)S(1)} collective-permute-done((bf16[80,768]{1,0:T(8,128)(2,1)S(1)}, bf16[80,768]{1,0:T(8,128)(2,1)S(1)}, u32[]{:S(2)}, u32[]{:S(2)}) %collective-permute-start.12) | collective-permute-done | bytes 122912 | tf_op jit(solution)/shard_map/ppermute | solution.py:273
  76.6 0.6 collective-permute-done.14
  77.3 0.1 add_convert_fusion.mine
  77.4 4.4 %collective-permute-start.15 = (bf16[80,768]{1,0:T(8,128)(2,1)S(1)}, bf16[80,768]{1,0:T(8,128)(2,1)S(1)}, u32[]{:S(2)}, u32[]{:S(2)}) collective-permute-start(bf16[80,768]{1,0:T(8,128)(2,1)S(1)} %add_convert_fusion.mine), channel_id=1, source_target_pairs={{0,2},{2,0},{1,3},{3,1},{4,6},{6,4},{5,7},{7,5},{8,10},{10,8},{9,1... | collective-permute-start | bytes 368648 | tf_op jit(solution)/shard_map/ppermute | solution.py:366
  81.8 1.0 %collective-permute-done.15.other = bf16[80,768]{1,0:T(8,128)(2,1)S(1)} collective-permute-done((bf16[80,768]{1,0:T(8,128)(2,1)S(1)}, bf16[80,768]{1,0:T(8,128)(2,1)S(1)}, u32[]{:S(2)}, u32[]{:S(2)}) %collective-permute-start.15) | collective-permute-done | bytes 122912 | tf_op jit(solution)/shard_map/ppermute | solution.py:366
  82.7 0.9 %last.1 = (f32[64,1536]{1,0:T(8,128)}, f32[8,2,1536]{2,1,0:T(2,128)}) custom-call(bf16[80,768]{1,0:T(8,128)(2,1)S(1)} %add_convert_fusion.mine, bf16[80,768]{1,0:T(8,128)(2,1)S(1)} %collective-permute-done.15.other, bf16[64,1536]{1,0:T(8,128)(2,1)S(1)} %bitcast.12), custom_call_target="tpu_custom_call" | custom-call | flops 10000000 | bytes 1000000 | tf_op jit(solution)/shard_map/last/pallas_call | solution.py:368
  (30 shorter events, 0.4 us)
Async XLA Ops:
  0.6 13.8 %copy-start.1 = (bf16[1536,64]{0,1:T(8,128)(2,1)S(1)}, bf16[1536,64]{0,1:T(8,128)(2,1)}, u32[]{:S(2)}) copy-start(bf16[1536,64]{0,1:T(8,128)(2,1)} %param.17) | copy-start | bytes 589828
  0.6 13.8 %copy-start = (bf16[256,1536]{1,0:T(8,128)(2,1)S(1)}, bf16[256,1536]{1,0:T(8,128)(2,1)}, u32[]{:S(2)}) copy-start(bf16[256,1536]{1,0:T(8,128)(2,1)} %hidden.5) | copy-start | bytes 2359300
  0.7 13.8 %copy-start.2 = (bf16[16,2,1536]{2,1,0:T(2,128)(2,1)S(1)}, bf16[16,2,1536]{2,1,0:T(2,128)(2,1)}, u32[]{:S(2)}) copy-start(bf16[16,2,1536]{2,1,0:T(2,128)(2,1)} %mod.5) | copy-start | bytes 294916
  0.7 13.8 %copy-start.3 = (s32[8]{0:T(128)S(1)}, s32[8]{0:T(128)}, u32[]{:S(2)}) copy-start(s32[8]{0:T(128)} %prompts.5) | copy-start | bytes 100
  0.7 20.1 %copy-start.6 = (bf16[9,512,16]{1,2,0:T(8,128)(2,1)S(1)}, bf16[9,512,16]{1,2,0:T(8,128)(2,1)}, u32[]{:S(2)}) copy-start(bf16[9,512,16]{1,2,0:T(8,128)(2,1)} %param.11) | copy-start | bytes 442372
  1.5 19.2 %collective-permute-start = (bf16[4,16,128]{2,1,0:T(8,128)(2,1)S(1)}, bf16[4,16,128]{2,1,0:T(8,128)(2,1)S(1)}, u32[]{:S(2)}, u32[]{:S(2)}) collective-permute-start(bf16[4,16,128]{2,1,0:T(8,128)(2,1)S(1)} %get-tuple-element.28), channel_id=1, source_target_pairs={{0,2},{2,4},{4,6},{6,8},{8,10},{10,12},{12,14},{14,16},{16,18},{18... | collective-permute-start | bytes 49160 | tf_op jit(solution)/shard_map/ppermute | solution.py:296
  4.7 16.1 %collective-permute-start.1 = (bf16[4,16,128]{2,1,0:T(8,128)(2,1)S(1)}, bf16[4,16,128]{2,1,0:T(8,128)(2,1)S(1)}, u32[]{:S(2)}, u32[]{:S(2)}) collective-permute-start(bf16[4,16,128]{2,1,0:T(8,128)(2,1)S(1)} %get-tuple-element.27), channel_id=1, source_target_pairs={{2,0},{4,2},{6,4},{8,6},{10,8},{12,10},{14,12},{16,14},{18,16},{20... | collective-permute-start | bytes 49160 | tf_op jit(solution)/shard_map/ppermute | solution.py:297
  6.6 27.0 %collective-permute-start.2 = (bf16[2,128,512]{2,1,0:T(8,128)(2,1)S(1)}, bf16[2,128,512]{2,1,0:T(8,128)(2,1)S(1)}, u32[]{:S(2)}, u32[]{:S(2)}) collective-permute-start(bf16[2,128,512]{2,1,0:T(8,128)(2,1)S(1)} %get-tuple-element.26), channel_id=1, source_target_pairs={{0,2},{2,4},{4,6},{6,8},{8,10},{10,12},{12,14},{14,16},{16,18},{18... | collective-permute-start | bytes 786440 | tf_op jit(solution)/shard_map/ppermute | solution.py:299
  8.2 25.5 %collective-permute-start.3 = (bf16[2,128,512]{2,1,0:T(8,128)(2,1)S(1)}, bf16[2,128,512]{2,1,0:T(8,128)(2,1)S(1)}, u32[]{:S(2)}, u32[]{:S(2)}) collective-permute-start(bf16[2,128,512]{2,1,0:T(8,128)(2,1)S(1)} %get-tuple-element.25), channel_id=1, source_target_pairs={{2,0},{4,2},{6,4},{8,6},{10,8},{12,10},{14,12},{16,14},{18,16},{20... | collective-permute-start | bytes 786440 | tf_op jit(solution)/shard_map/ppermute | solution.py:300
  15.5 26.3 %collective-permute-start.4 = (f32[264,128]{1,0:T(8,128)S(1)}, f32[264,128]{1,0:T(8,128)S(1)}, u32[]{:S(2)}, u32[]{:S(2)}) collective-permute-start(f32[264,128]{1,0:T(8,128)S(1)} %stats.1), channel_id=1, source_target_pairs={{0,1},{1,0},{2,3},{3,2},{4,5},{5,4},{6,7},{7,6},{8,9},{9,8},{10,11... | collective-permute-start | bytes 405512 | tf_op jit(solution)/shard_map/ppermute | solution.py:310
  20.8 2.3 %copy-start.4 = (bf16[9,512,512]{2,1,0:T(8,128)(2,1)S(1)}, bf16[9,512,512]{2,1,0:T(8,128)(2,1)}, u32[]{:S(2)}) copy-start(bf16[9,512,512]{2,1,0:T(8,128)(2,1)} %w2.1) | copy-start | bytes 14155780
  23.1 10.6 %copy-start.5 = (bf16[9,512,512]{2,1,0:T(8,128)(2,1)S(1)}, bf16[9,512,512]{2,1,0:T(8,128)(2,1)}, u32[]{:S(2)}) copy-start(bf16[9,512,512]{2,1,0:T(8,128)(2,1)} %w2.1) | copy-start | bytes 14155780
  23.1 10.6 %copy-start.7 = (f32[8]{0:T(128)S(1)}, f32[8]{0:T(128)}, u32[]{:S(2)}) copy-start(f32[8]{0:T(128)} %steps.1) | copy-start | bytes 100
  43.0 9.0 %collective-permute-start.5 = (bf16[80,768]{1,0:T(8,128)(2,1)S(1)}, bf16[80,768]{1,0:T(8,128)(2,1)S(1)}, u32[]{:S(2)}, u32[]{:S(2)}) collective-permute-start(bf16[80,768]{1,0:T(8,128)(2,1)S(1)} %get-tuple-element.16), channel_id=1, source_target_pairs={{0,2},{2,0},{1,3},{3,1},{4,6},{6,4},{5,7},{7,5},{8,10},{10,8},{9,1... | collective-permute-start | bytes 368648 | tf_op jit(solution)/shard_map/ppermute | solution.py:363
  52.1 6.5 %collective-permute-start.6 = (bf16[80,768]{1,0:T(8,128)(2,1)S(1)}, bf16[80,768]{1,0:T(8,128)(2,1)S(1)}, u32[]{:S(2)}, u32[]{:S(2)}) collective-permute-start(bf16[80,768]{1,0:T(8,128)(2,1)S(1)} %fusion), channel_id=1, source_target_pairs={{0,4},{4,8},{8,12},{12,0},{1,5},{5,9},{9,13},{13,1},{2,6},{6,10},{... | collective-permute-start | bytes 368648 | tf_op jit(solution)/shard_map/ppermute | solution.py:273
  52.2 10.8 %collective-permute-start.7 = (bf16[80,768]{1,0:T(8,128)(2,1)S(1)}, bf16[80,768]{1,0:T(8,128)(2,1)S(1)}, u32[]{:S(2)}, u32[]{:S(2)}) collective-permute-start(bf16[80,768]{1,0:T(8,128)(2,1)S(1)} %fusion), channel_id=1, source_target_pairs={{0,8},{4,12},{8,0},{12,4},{1,9},{5,13},{9,1},{13,5},{2,10},{6,14},... | collective-permute-start | bytes 368648 | tf_op jit(solution)/shard_map/ppermute | solution.py:273
  52.3 10.7 %collective-permute-start.8 = (bf16[80,768]{1,0:T(8,128)(2,1)S(1)}, bf16[80,768]{1,0:T(8,128)(2,1)S(1)}, u32[]{:S(2)}, u32[]{:S(2)}) collective-permute-start(bf16[80,768]{1,0:T(8,128)(2,1)S(1)} %fusion), channel_id=1, source_target_pairs={{0,12},{4,0},{8,4},{12,8},{1,13},{5,1},{9,5},{13,9},{2,14},{6,2},{... | collective-permute-start | bytes 368648 | tf_op jit(solution)/shard_map/ppermute | solution.py:273
  63.1 5.4 %collective-permute-start.10 = (bf16[80,768]{1,0:T(8,128)(2,1)S(1)}, bf16[80,768]{1,0:T(8,128)(2,1)S(1)}, u32[]{:S(2)}, u32[]{:S(2)}) collective-permute-start(bf16[80,768]{1,0:T(8,128)(2,1)S(1)} %get-tuple-element.23), channel_id=1, source_target_pairs={{0,32},{16,48},{32,0},{48,16},{1,33},{17,49},{33,1},{49,17},{2,34}... | collective-permute-start | bytes 368648 | tf_op jit(solution)/shard_map/ppermute | solution.py:273
  63.2 5.3 %collective-permute-start.11 = (bf16[80,768]{1,0:T(8,128)(2,1)S(1)}, bf16[80,768]{1,0:T(8,128)(2,1)S(1)}, u32[]{:S(2)}, u32[]{:S(2)}) collective-permute-start(bf16[80,768]{1,0:T(8,128)(2,1)S(1)} %get-tuple-element.23), channel_id=1, source_target_pairs={{0,48},{16,0},{32,16},{48,32},{1,49},{17,1},{33,17},{49,33},{2,50}... | collective-permute-start | bytes 368648 | tf_op jit(solution)/shard_map/ppermute | solution.py:273
  63.3 7.0 %collective-permute-start.9 = (bf16[80,768]{1,0:T(8,128)(2,1)S(1)}, bf16[80,768]{1,0:T(8,128)(2,1)S(1)}, u32[]{:S(2)}, u32[]{:S(2)}) collective-permute-start(bf16[80,768]{1,0:T(8,128)(2,1)S(1)} %get-tuple-element.23), channel_id=1, source_target_pairs={{0,16},{16,32},{32,48},{48,0},{1,17},{17,33},{33,49},{49,1},{2,18}... | collective-permute-start | bytes 368648 | tf_op jit(solution)/shard_map/ppermute | solution.py:273
  70.3 6.3 %collective-permute-start.12 = (bf16[80,768]{1,0:T(8,128)(2,1)S(1)}, bf16[80,768]{1,0:T(8,128)(2,1)S(1)}, u32[]{:S(2)}, u32[]{:S(2)}) collective-permute-start(bf16[80,768]{1,0:T(8,128)(2,1)S(1)} %fusion.1), channel_id=1, source_target_pairs={{0,64},{64,128},{128,192},{192,0},{1,65},{65,129},{129,193},{193,1... | collective-permute-start | bytes 368648 | tf_op jit(solution)/shard_map/ppermute | solution.py:273
  70.4 6.2 %collective-permute-start.13 = (bf16[80,768]{1,0:T(8,128)(2,1)S(1)}, bf16[80,768]{1,0:T(8,128)(2,1)S(1)}, u32[]{:S(2)}, u32[]{:S(2)}) collective-permute-start(bf16[80,768]{1,0:T(8,128)(2,1)S(1)} %fusion.1), channel_id=1, source_target_pairs={{0,128},{64,192},{128,0},{192,64},{1,129},{65,193},{129,1},{193,65... | collective-permute-start | bytes 368648 | tf_op jit(solution)/shard_map/ppermute | solution.py:273
  71.9 5.4 %collective-permute-start.14 = (bf16[80,768]{1,0:T(8,128)(2,1)S(1)}, bf16[80,768]{1,0:T(8,128)(2,1)S(1)}, u32[]{:S(2)}, u32[]{:S(2)}) collective-permute-start(bf16[80,768]{1,0:T(8,128)(2,1)S(1)} %fusion.1), channel_id=1, source_target_pairs={{0,192},{64,0},{128,64},{192,128},{1,193},{65,1},{129,65},{193,129... | collective-permute-start | bytes 368648 | tf_op jit(solution)/shard_map/ppermute | solution.py:273
  77.4 5.4 %collective-permute-start.15 = (bf16[80,768]{1,0:T(8,128)(2,1)S(1)}, bf16[80,768]{1,0:T(8,128)(2,1)S(1)}, u32[]{:S(2)}, u32[]{:S(2)}) collective-permute-start(bf16[80,768]{1,0:T(8,128)(2,1)S(1)} %add_convert_fusion.mine), channel_id=1, source_target_pairs={{0,2},{2,0},{1,3},{3,1},{4,6},{6,4},{5,7},{7,5},{8,10},{10,8},{9,1... | collective-permute-start | bytes 368648 | tf_op jit(solution)/shard_map/ppermute | solution.py:366

commit v4 on v3

--- a/solution.py
+++ b/solution.py
@@ -10,7 +10,6 @@
 BF = jnp.bfloat16
 F32 = jnp.float32
 TILE = ("y", "x", "zl", "core")
-RINGS = ("zl", "x", "y")
 OVER_0 = (((0,), (0,)), ((), ()))
 OVER_1 = (((1,), (1,)), ((), ()))
 WHOLE = pl.BlockSpec(memory_space=pltpu.VMEM)
@@ -36,11 +35,11 @@
     return 0.5 + 0.5 * jnp.tanh(0.5 * h)
 
 
-def put_beside(ref, i, v):
+def put_beside(ref, i, v, cols):
     at = pl.ds(i * v.shape[0], v.shape[0])
-    ref[0, at, :] = before(v, 0).astype(BF)
-    ref[1, at, :] = v.astype(BF)
-    ref[2, at, :] = after(v, 0).astype(BF)
+    ref[0, at, cols] = before(v, 0).astype(BF)
+    ref[1, at, cols] = v.astype(BF)
+    ref[2, at, cols] = after(v, 0).astype(BF)
 
 
 def keeper(rows, width, images):
@@ -60,11 +59,22 @@
     return own[row] if row < own.shape[0] else high[row - own.shape[0]]
 
 
+def conv_tile(tap, meanwhile):
+    total = None
+    for k in range(9):
+        part = tap(k)
+        total = part if total is None else total + part
+        for step in meanwhile[k::9]:
+            step()
+    return total
+
+
 def forward_kernel(geometry, lat_low, lat_own, lat_high, w1, w2_far, slope_two, slope_one, lats, acts,
-                   w2, sem):
+                   w2, sems):
     rows, width, _ = geometry
-    load = pltpu.make_async_copy(w2_far, w2, sem)
-    load.start()
+    loads = [pltpu.make_async_copy(w2_far.at[k], w2.at[k], sems.at[k]) for k in range(9)]
+    for load in loads:
+        load.start()
     masked = keeper(*geometry)
     for i in range(rows + 8):
         row = i - 4
@@ -72,52 +82,100 @@
         lats[0, i] = before(v, 1).astype(BF)
         lats[1, i] = v.astype(BF)
         lats[2, i] = after(v, 1).astype(BF)
-
-    for i in range(rows + 6):
+    mid = w1.shape[1]
+    part_width = mid // 2
+    halves = [slice(0, part_width), slice(part_width, mid)]
+
+    def first_layer(i, cols):
         row = i - 3
         taps = [lats[kx, i + ky] for ky in range(3) for kx in range(3)]
-        pre = dot(jnp.concatenate(taps, 0), w1[...], OVER_0)
+        pre = dot(jnp.concatenate(taps, 0), w1[:, cols], OVER_0)
         s = sigmoid(pre)
         if -1 <= row <= rows:
-            slope_one[pl.ds((row + 1) * width, width), :] = s * (1.0 + pre * (1.0 - s))
-        put_beside(acts, i, masked((pre * s).astype(BF).astype(F32), row))
-
-    load.wait()
+            slope_one[pl.ds((row + 1) * width, width), cols] = s * (1.0 + pre * (1.0 - s))
+        put_beside(acts, i, masked((pre * s).astype(BF).astype(F32), row), cols)
+
+    def finish(i, pre, j, cols):
+        h = pre[j * width : (j + 1) * width, cols]
+        s = sigmoid(h)
+        slope_two[pl.ds((i + j) * width, width), cols] = s * (1.0 + h * (1.0 - s))
+
     per = 2
+    for i in range(per + 2):
+        for cols in halves:
+            first_layer(i, cols)
+    steps = []
     for i in range(0, rows + 4, per):
-        pre = None
-        for ky in range(3):
-            for kx in range(3):
-                part = dot(acts[kx, pl.ds((i + ky) * width, per * width), :], w2[3 * ky + kx], OVER_1)
-                pre = part if pre is None else pre + part
-        s = sigmoid(pre)
-        slope_two[pl.ds(i * width, per * width), :] = s * (1.0 + pre * (1.0 - s))
+        nexts = [
+            functools.partial(first_layer, i + per + 2 + j, cols)
+            for j in range(per)
+            for cols in halves
+            if i + per + 2 + j < rows + 6
+        ]
+
+        def tap(k):
+            if i == 0:
+                loads[k].wait()
+            return dot(acts[k % 3, pl.ds((i + k // 3) * width, per * width), :], w2[k], OVER_1)
+
+        pre = conv_tile(tap, nexts + steps)
+        steps = [
+            functools.partial(finish, i, pre, j, cols) for j in range(per) for cols in halves
+        ]
+    for step in steps:
+        step()
 
 
 def backward_kernel(geometry, steps, slope_two, slope_one, cot_low, cot_own, cot_high, w1t, w2, out,
                     grads, inner):
     rows, width, _ = geometry
     ch = w1t.shape[0] // 9
+    mid = w2.shape[1]
+    part_width = mid // 2
+    halves = [slice(0, part_width), slice(part_width, mid)]
     masked = keeper(*geometry)
     step = -steps[place_of(*geometry)[0]]
-    for i in range(rows + 4):
-        cot = line_of(cot_low, cot_own, cot_high, i - 2).astype(F32)
-        g = masked(cot * slope_two[pl.ds(i * width, width), :], i - 2)
-        put_beside(grads, i, g.astype(BF).astype(F32))
+
+    def second_grad(i, cols):
+        cot = line_of(cot_low, cot_own, cot_high, i - 2)[:, cols].astype(F32)
+        g = masked(cot * slope_two[pl.ds(i * width, width), cols], i - 2)
+        put_beside(grads, i, g.astype(BF).astype(F32), cols)
+
+    taps = []
+
+    def finish(i, back, j, cols):
+        at = pl.ds((i + j) * width, width)
+        g = back[j * width : (j + 1) * width, cols] * slope_one[at, cols]
+        inner[at, cols] = masked(g, i + j - 1).astype(BF)
 
     per = 2
+
+    def first_taps(i):
+        taps.append(dot(w1t[...], inner[pl.ds(i * width, per * width), :], OVER_1))
+
+    for i in range(per + 2):
+        for cols in halves:
+            second_grad(i, cols)
+    todo = []
     for i in range(0, rows + 2, per):
-        back = None
-        for ky in range(3):
-            for kx in range(3):
-                part = dot(grads[2 - kx, pl.ds((i + 2 - ky) * width, per * width), :], w2[3 * ky + kx])
-                back = part if back is None else back + part
-        for j in range(per):
-            at = pl.ds((i + j) * width, width)
-            g = back[j * width : (j + 1) * width] * slope_one[at, :]
-            inner[at, :] = masked(g, i + j - 1).astype(BF)
-
-    taps = dot(w1t[...], inner[...], OVER_1)
+        nexts = [
+            functools.partial(second_grad, i + per + 2 + j, cols)
+            for j in range(per)
+            for cols in halves
+            if i + per + 2 + j < rows + 4
+        ]
+
+        def tap(k):
+            at = pl.ds((i + 2 - k // 3) * width, per * width)
+            return dot(grads[2 - k % 3, at, :], w2[k])
+
+        back = conv_tile(tap, nexts + todo)
+        todo = [functools.partial(finish, i, back, j, cols) for j in range(per) for cols in halves]
+        todo.append(functools.partial(first_taps, i))
+    for part in todo:
+        part()
+    taps = jnp.concatenate(taps, 1)
+
     lines = []
     for row in range(rows):
         by_kx = []
@@ -219,10 +277,13 @@
     wide = jnp.concatenate([row] * images, 1)
     lane = lax.broadcasted_iota(jnp.int32, wide.shape, 1)
     held[patch + images :, 0 : images * patch] = jnp.where(lax.div(lane, patch) == image, wide, 0.0)
-    half = keep.shape[1]
+    lines, count = held.shape[0], keep.shape[0] // held.shape[0]
     core = lax.axis_index("core")
-    keep[...] = held[:, pl.ds(pl.multiple_of(core * half, half), half)]
-    send[...] = held[:, pl.ds(pl.multiple_of((1 - core) * half, half), half)].astype(BF)
+    for j in range(count):
+        at = pl.ds(j * lines, lines)
+        for ref, side in ((keep, core), (send, 1 - core)):
+            lanes = pl.ds(pl.multiple_of((side * count + j) * 128, 128), 128)
+            ref[at, :] = held[:, lanes].astype(ref.dtype)
 
 
 def hidden_kernel(width_all, geometry, prompts, gvt, stats, stats_far, hidden, mod, wt, out):
@@ -236,48 +297,67 @@
     out[...] = ((grad - first - normed * second) * scale).astype(BF)
 
 
-def last_kernel(images, mine, other, wt, proj, mod):
+def last_kernel(images, mine, other, wt, proj, mod, held):
     patch = wt.shape[0]
-    half = mine.shape[1]
-    core = lax.axis_index("core")
-    for block, place in ((mine, core), (other, 1 - core)):
-        at = pl.ds(pl.multiple_of(place * half, half), half)
-        proj[:, at] = block[0:patch, :].astype(F32)
-        mod[:, 1, at] = block[patch : patch + images, :].astype(F32)
-    wide = images * patch
-    mine_sum = mine[patch:, 0:wide].astype(F32)[images : images + 1]
-    other_sum = other[patch:, 0:wide].astype(F32)[images : images + 1]
-    line = jnp.where(core == 0, mine_sum, other_sum)
-    sums = jnp.concatenate([line[:, i * patch : (i + 1) * patch] for i in range(images)], 0)
-    mod[:, 0, :] = dot(sums.astype(BF), wt[...])
-
-
-def call(kernel, out_shape, n_in, cost, name, scratch=(), smem=1, far=0):
+    count, piece = mine.shape[0], mine.shape[1]
+    lines = patch + images + 8
+    core, zl = lax.axis_index("core"), lax.axis_index("zl")
+    for d in range(count):
+        at = pl.ds(pl.multiple_of(lax.rem(zl + d, count) * piece, 8), piece)
+        held[core, at, :] = mine[d].astype(F32)
+        held[1 - core, at, :] = other[d].astype(F32)
+    blocks = count * piece // lines
+    for side in range(2):
+        for j in range(blocks):
+            at = pl.ds((side * blocks + j) * 128, 128)
+            proj[:, at] = held[side, pl.ds(j * lines, patch), :]
+            mod[:, 1, at] = held[side, pl.ds(j * lines + patch, images), :]
+    sums = []
+    for i in range(images):
+        j, lane = divmod(i * patch, 128)
+        row = held[0, pl.ds(j * lines + patch + images, 1), :]
+        sums.append(row[:, lane : lane + patch])
+    mod[:, 0, :] = dot(jnp.concatenate(sums, 0).astype(BF), wt[...])
+
+
+def call(kernel, out_shape, n_in, cost, name, scratch=(), smem=1, far=0, vmem=24):
     return pl.pallas_call(
         kernel,
         out_shape=out_shape,
-        in_specs=[SCALARS] * smem + [WHOLE] * (n_in - smem - far) + [pl.BlockSpec(memory_space=pl.ANY)] * far,
+        in_specs=[SCALARS] * smem + [WHOLE] * (n_in - smem - far) + [pl.BlockSpec(memory_space=pltpu.HBM)] * far,
         out_specs=jax.tree.map(lambda _: WHOLE, out_shape),
         scratch_shapes=list(scratch),
-        compiler_params=pltpu.CompilerParams(vmem_limit_bytes=40 * 2**20),
+        compiler_params=pltpu.CompilerParams(vmem_limit_bytes=vmem * 2**20),
         cost_estimate=pl.CostEstimate(flops=cost[0], bytes_accessed=cost[1], transcendentals=0),
         name=name,
     )
 
 
-def sum_over_rings(total, beside):
-    for axis in RINGS:
-        count = lax.axis_size(axis)
-        out = total.astype(BF)
-        came = [
-            lax.ppermute(out, axis, [(i, (i + d) % count) for i in range(count)])
-            for d in range(1, count)
-        ]
-        if axis == RINGS[0]:
-            came, beside = lax.optimization_barrier((came, beside))
-        for block in came:
-            total = total + block.astype(F32)
-    return total, beside
+def sum_over_chips(part, beside):
+    count = lax.axis_size("zl")
+    zl = lax.axis_index("zl")
+
+    def piece(d):
+        return lax.dynamic_index_in_dim(part, lax.rem(zl + d, count), 0, False)
+
+    total = piece(0)
+    came = [
+        lax.ppermute(piece(d).astype(BF), "zl", [(i, (i + d) % count) for i in range(count)])
+        for d in range(1, count)
+    ]
+    came, beside = lax.optimization_barrier((came, beside))
+    for block in came:
+        total = total + block.astype(F32)
+    plane = ("y", "x")
+    chips = lax.axis_size(plane)
+    copies = jnp.broadcast_to(total.astype(BF)[None], (chips,) + total.shape)
+    total = jnp.sum(lax.all_to_all(copies, plane, 0, 0).astype(F32), axis=0)
+    total = lax.optimization_barrier(total).astype(BF)
+    came = [
+        lax.ppermute(total, "zl", [(i, (i - d) % count) for i in range(count)])
+        for d in range(1, count)
+    ]
+    return jnp.stack([total] + came, 0), beside
 
 
 def body(feat_cot, latent, dec_w1, dec_w2, hidden, modulation, prompt_ids, step_size, proj_w):
@@ -292,12 +372,11 @@
     up = [(i, (i + 1) % count) for i in range(count)]
     down = [(b, a) for a, b in up]
 
+    cot_own = lax.optimization_barrier(feat_cot.transpose(1, 2, 0))
+    latent, cot_own = lax.optimization_barrier((latent, cot_own))
     lat_own = lax.optimization_barrier(latent.transpose(1, 0, 2))
     lat_low = lax.ppermute(lat_own[-4:], TILE, up)
-    lat_high = lax.ppermute(lat_own[:4], TILE, down)
-    cot_own = lax.optimization_barrier(feat_cot.transpose(1, 2, 0))
     cot_low = lax.ppermute(cot_own[-2:], TILE, up)
-    cot_high = lax.ppermute(cot_own[:2], TILE, down)
     wt = proj_w.T
 
     stats = call(
@@ -307,8 +386,12 @@
         (10**8, 10**6),
         "stats",
     )(prompt_ids, hidden, modulation, wt)
+    lat_own, cot_own, stats = lax.optimization_barrier((lat_own, cot_own, stats))
+    lat_high = lax.ppermute(lat_own[:4], TILE, down)
+    cot_high = lax.ppermute(cot_own[:2], TILE, down)
     stats_far = lax.ppermute(stats, "mp", [(0, 1), (1, 0)])
 
+    lat_low, cot_low = lax.optimization_barrier((lat_low, cot_low))
     w1 = dec_w1.transpose(0, 2, 1).reshape(9 * ch, mid)
     slope_two, slope_one = call(
         functools.partial(forward_kernel, geometry),
@@ -323,10 +406,11 @@
             pltpu.VMEM((3, rows + 8, ch, width), BF),
             pltpu.VMEM((3, (rows + 6) * width, mid), BF),
             pltpu.VMEM(dec_w2.shape, BF),
-            pltpu.SemaphoreType.DMA,
+            pltpu.SemaphoreType.DMA((9,)),
         ),
         smem=0,
         far=1,
+        vmem=46,
     )(lat_low, lat_own, lat_high, w1, dec_w2)
     gvt = call(
         functools.partial(backward_kernel, geometry),
@@ -341,10 +425,11 @@
     )(step_size, slope_two, slope_one, cot_low, cot_own, cot_high, w1, dec_w2)
 
     lines = patch + images + 8
-    half = features // 2
+    pieces = lax.axis_size("zl")
+    high = lines * features // 256
     send, keep = call(
         functools.partial(sums_kernel, width_all, geometry),
-        (jax.ShapeDtypeStruct((lines, half), BF), jax.ShapeDtypeStruct((lines, half), F32)),
+        (jax.ShapeDtypeStruct((high, 128), BF), jax.ShapeDtypeStruct((high, 128), F32)),
         7,
         (10**8, 2 * 10**6),
         "sums",
@@ -359,10 +444,8 @@
     )(prompt_ids, gvt, stats, stats_far, hidden, modulation, wt)
 
     swap = [(0, 1), (1, 0)]
-    total, grad_hidden = sum_over_rings(
-        keep + lax.ppermute(send, "core", swap).astype(F32), grad_hidden
-    )
-    mine = total.astype(BF)
+    total = keep + lax.ppermute(send, "core", swap).astype(F32)
+    mine, grad_hidden = sum_over_chips(total.reshape(pieces, high // pieces, 128), grad_hidden)
     other = lax.ppermute(mine, "core", swap)
 
     grad_proj, grad_mod = call(
@@ -374,6 +457,7 @@
         3,
         (10**7, 10**6),
         "last",
+        scratch=(pltpu.VMEM((2, high, 128), F32),),
         smem=0,
     )(mine, other, wt)
     return (grad_hidden, grad_proj.T, grad_mod)

time: 85 us -> 81.2 us (0.955); the launches traced: 83.6 us -> 80.9 us
  blocking collectives: 0 us -> 15.7 us
  starting transfers between devices: 36.6 us -> 26.1 us
  waiting for transfers between devices: 17 us -> 8.04 us
  Pallas kernels: 24 us -> 24.9 us
    all_to_all x0 -> x1, blocking collectives: none -> 15.7 us  [sum_over_chips(): total = jnp.sum(lax.all_to_all(copies, plane, 0, 0).astype(F32), axis=0)]
    ppermute x10 -> x7, starting transfers between devices: 15.7 us -> 5.24 us  [the longest x3 3.05 us: sum_over_chips(): lax.ppermute(total, 'zl', [(i, (i - d) % count) for i in range(count)])]
    ppermute x10 -> x7, waiting for transfers between devices: 16 us -> 7.05 us  [the longest x3 4.57 us: sum_over_chips(): lax.ppermute(total, 'zl', [(i, (i - d) % count) for i in range(count)])]
    ppermute x1, starting transfers between devices: 3.1 us -> 0.09 us  [body(): lat_low = lax.ppermute(lat_own[-4:], TILE, up)]
    ppermute x1, starting transfers between devices: 1.52 us -> 3.1 us  [body(): cot_low = lax.ppermute(cot_own[-2:], TILE, up)]
    pallas_call x1, Pallas kernels: 10.5 us -> 11.4 us  [body(): call(functools.partial(forward_kernel, geometry), (jax.ShapeDtypeStruct((...]
    ppermute x1, starting transfers between devices: 6.32 us -> 7.19 us  [body(): cot_high = lax.ppermute(cot_own[:2], TILE, down)]
    unnamed x18 -> x23, local copies, waits for them, and re-layouts: 4.84 us -> 4.22 us
  transfers between devices with their start and end apart: 16 -> 13, of which waited for: 8 -> 7; matrix products, arithmetic and copies ran while one was open for 2% -> 1% of each run, Pallas kernels for 26% -> 28%
where the time goes in v4:
time: 81.2 us; the launch traced here: 80.9 us
  starting transfers between devices  26.1 us (32%)
  Pallas kernels  24.9 us (31%)
  blocking collectives  15.7 us (19%)
  waiting for transfers between devices  8.04 us (10%)
  local copies, waits for them, and re-layouts  5.12 us (6%)
  between operations  0.88 us (1%)
    all_to_all x1, blocking collectives, sum_over_chips(): total = jnp.sum(lax.all_to_all(copies, plane, 0, 0).astype(F32), axis=0)  15.7 us
    pallas_call x1, Pallas kernels, body(): call(functools.partial(forward_kernel, geometry), (jax.ShapeDtypeStruct((...  11.4 us
    pallas_call x1, Pallas kernels, body(): call(functools.partial(backward_kernel, geometry), jax.ShapeDtypeStruct((...  8.09 us
    ppermute x1, starting transfers between devices, body(): cot_high = lax.ppermute(cot_own[:2], TILE, down)  7.19 us
    ppermute x1, starting transfers between devices, body(): stats_far = lax.ppermute(stats, 'mp', [(0, 1), (1, 0)])  6 us
    ppermute x3, waiting for transfers between devices, sum_over_chips(): lax.ppermute(total, 'zl', [(i, (i - d) % count) for i in range(count)])  4.57 us
    unnamed x23, local copies, waits for them, and re-layouts  4.22 us
    ppermute x1, starting transfers between devices, body(): other = lax.ppermute(mine, 'core', swap)  3.92 us
  transfers between devices with their start and end apart: 13, of which 7 were waited for; matrix products, arithmetic and copies ran while one was open for 1% of the time, Pallas kernels for 28%

profile of v4, /device:TPU:1, one launch (start us, length us, event | category | flops | bytes accessed | tf_op | source)
XLA Modules:
  0.0 80.9 jit_solution(1658553048576129169)
XLA Ops:
  0.7 1.7 %copy.14 = bf16[512,8,128]{0,2,1:T(8,128)(2,1)S(1)} copy(bf16[512,8,128]{2,1,0:T(8,128)(2,1)} %param.9) | data formatting | bytes 2097152 | tf_op args[0]
  2.4 3.1 %collective-permute-start.1 = (bf16[2,128,512]{2,1,0:T(8,128)(2,1)S(1)}, bf16[2,128,512]{2,1,0:T(8,128)(2,1)S(1)}, u32[]{:S(2)}, u32[]{:S(2)}) collective-permute-start(bf16[2,128,512]{2,1,0:T(8,128)(2,1)S(1)} %slice.13), channel_id=1, source_target_pairs={{0,2},{2,4},{4,6},{6,8},{8,10},{10,12},{12,14},{14,16},{16,18},{18... | collective-permute-start | bytes 786440 | tf_op jit(solution)/shard_map/ppermute | solution.py:379
  5.5 0.8 copy.17
  6.3 0.1 collective-permute-start
  6.4 0.9 %copy-done.1 = bf16[1536,64]{0,1:T(8,128)(2,1)S(1)} copy-done((bf16[1536,64]{0,1:T(8,128)(2,1)S(1)}, bf16[1536,64]{0,1:T(8,128)(2,1)}, u32[]{:S(2)}) %copy-start.1) | copy-done | bytes 196632
  7.3 0.9 %copy-done.3 = bf16[16,2,1536]{2,1,0:T(2,128)(2,1)S(1)} copy-done((bf16[16,2,1536]{2,1,0:T(2,128)(2,1)S(1)}, bf16[16,2,1536]{2,1,0:T(2,128)(2,1)}, u32[]{:S(2)}) %copy-start.3) | copy-done | bytes 98328
  8.2 0.7 copy-done.5
  8.8 1.0 %stats.1 = f32[264,128]{1,0:T(8,128)S(1)} custom-call(s32[8]{0:T(128)S(1)} %copy-done.5, bf16[256,1536]{1,0:T(8,128)(2,1)S(1)} %copy-done, bf16[16,2,1536]{2,1,0:T(2,128)(2,1)S(1)} %copy-done.3, bf16[64,1536]{1,0:T(8,128)(2,1)S(1)} %bitcast.28), custom_call_target="tpu_custom_call" | custom-call | flops 100000000 | bytes 1000000 | tf_op jit(solution)/shard_map/stats/pallas_call | solution.py:382
  9.9 0.6 collective-permute-start.2
  10.5 6.0 %collective-permute-start.4 = (f32[264,128]{1,0:T(8,128)S(1)}, f32[264,128]{1,0:T(8,128)S(1)}, u32[]{:S(2)}, u32[]{:S(2)}) collective-permute-start(f32[264,128]{1,0:T(8,128)S(1)} %stats.1), channel_id=1, source_target_pairs={{0,1},{1,0},{2,3},{3,2},{4,5},{5,4},{6,7},{7,6},{8,9},{9,8},{10,11... | collective-permute-start | bytes 405512 | tf_op jit(solution)/shard_map/ppermute | solution.py:392
  16.5 7.2 %collective-permute-start.3 = (bf16[2,128,512]{2,1,0:T(8,128)(2,1)S(1)}, bf16[2,128,512]{2,1,0:T(8,128)(2,1)S(1)}, u32[]{:S(2)}, u32[]{:S(2)}) collective-permute-start(bf16[2,128,512]{2,1,0:T(8,128)(2,1)S(1)} %slice.15), channel_id=1, source_target_pairs={{2,0},{4,2},{6,4},{8,6},{10,8},{12,10},{14,12},{16,14},{18,16},{20... | collective-permute-start | bytes 786440 | tf_op jit(solution)/shard_map/ppermute | solution.py:391
  23.7 11.4 %forward.1 = (f32[1536,512]{1,0:T(8,128)S(1)}, f32[1280,512]{1,0:T(8,128)S(1)}) custom-call(bf16[4,16,128]{2,1,0:T(8,128)(2,1)S(1)} %collective-permute-done.lat_low, bf16[8,16,128]{2,1,0:T(8,128)(2,1)S(1)} %bitcast.37, bf16[4,16,128]{2,1,0:T(8,128)(2,1)S(1)} %collective-permute-done.2.lat_high, bf16[144,512]{1,0:T(8,128)(2,1)S(1)} %bitcast.40, ...), custom_call_target="tpu_custom_call" | custom-call | flops 8000000000 | bytes 8000000 | tf_op jit(solution)/shard_map/forward/pallas_call | solution.py:396
  35.2 8.1 %backward.1.gvt = bf16[64,256]{1,0:T(8,128)(2,1)S(1)} custom-call(f32[8]{0:T(128)S(1)} %copy-done.8, f32[1536,512]{1,0:T(8,128)S(1)} %get-tuple-element.24.slope_two, f32[1280,512]{1,0:T(8,128)S(1)} %get-tuple-element.25.slope_one, bf16[2,128,512]{2,1,0:T(8,128)(2,1)S(1)} %collective-permute-done.1.cot_low, bf16[8,128,512]{2,1,0:T(8,128)(2,1)S(1)} %bitcast.34, ...), custom_call_target="tpu_custom_call" | custom-call | flops 7000000000 | bytes 8000000 | tf_op jit(solution)/shard_map/backward/pallas_call | solution.py:415
  43.4 1.2 %sums.1 = (bf16[480,128]{1,0:T(8,128)(2,1)S(1)}, f32[480,128]{1,0:T(8,128)S(1)}) custom-call(s32[8]{0:T(128)S(1)} %copy-done.6, bf16[64,256]{1,0:T(8,128)(2,1)S(1)} %backward.1.gvt, f32[264,128]{1,0:T(8,128)S(1)} %stats.1, f32[264,128]{1,0:T(8,128)S(1)} %collective-permute-done.4.stats_far, bf16[256,1536]{1,0:T(8,128)(2,1)S(1)} %copy-done, ...), custom_call_target="tpu_custom_call" | custom-call | flops 100000000 | bytes 2000000 | tf_op jit(solution)/shard_map/sums/pallas_call | solution.py:430
  44.5 0.7 collective-permute-start.5
  45.2 1.0 %collective-permute-done.5 = bf16[480,128]{1,0:T(8,128)(2,1)S(1)} collective-permute-done((bf16[480,128]{1,0:T(8,128)(2,1)S(1)}, bf16[480,128]{1,0:T(8,128)(2,1)S(1)}, u32[]{:S(2)}, u32[]{:S(2)}) %collective-permute-start.5) | collective-permute-done | bytes 122912 | tf_op jit(solution)/shard_map/ppermute | solution.py:447
  46.2 0.1 collective-permute-start.8
  46.3 0.1 collective-permute-start.7
  46.4 1.4 %collective-permute-start.6 = (bf16[120,128]{1,0:T(8,128)(2,1)S(1)}, bf16[120,128]{1,0:T(8,128)(2,1)S(1)}, u32[]{:S(2)}, u32[]{:S(2)}) collective-permute-start(bf16[120,128]{1,0:T(8,128)(2,1)S(1)} %get-tuple-element.39), channel_id=1, source_target_pairs={{0,4},{4,8},{8,12},{12,0},{1,5},{5,9},{9,13},{13,1},{2,6},{6,10},{... | collective-permute-start | bytes 92168 | tf_op jit(solution)/shard_map/ppermute | solution.py:345
  47.8 2.3 %grad_hidden.1 = bf16[256,1536]{1,0:T(8,128)(2,1)} custom-call(s32[8]{0:T(128)S(1)} %copy-done.6, bf16[64,256]{1,0:T(8,128)(2,1)S(1)} %backward.1.gvt, f32[264,128]{1,0:T(8,128)S(1)} %stats.1, f32[264,128]{1,0:T(8,128)S(1)} %collective-permute-done.4.stats_far, bf16[256,1536]{1,0:T(8,128)(2,1)S(1)} %copy-done, bf16[16,2,1536]{2,1,0:T(2,128)(2,1)S(1)} %copy-done.4, ...), custom_call_target="tpu_custom_call" | custom-call | flops 100000000 | bytes 2000000 | tf_op jit(solution)/shard_map/grad_hidden/pallas_call | solution.py:438
  50.0 0.1 collective-permute-done.7
  50.1 1.4 %collective-permute-done.6 = bf16[120,128]{1,0:T(8,128)(2,1)S(1)} collective-permute-done((bf16[120,128]{1,0:T(8,128)(2,1)S(1)}, bf16[120,128]{1,0:T(8,128)(2,1)S(1)}, u32[]{:S(2)}, u32[]{:S(2)}) %collective-permute-start.6) | collective-permute-done | bytes 30752 | tf_op jit(solution)/shard_map/ppermute | solution.py:345
  51.6 15.7 %all_to_all.5 = bf16[16,120,128]{2,1,0:T(8,128)(2,1)S(1)} all-to-all(bf16[16,120,128]{2,1,0:T(8,128)(2,1)S(1)} %broadcast_in_dim.2), channel_id=1, replica_groups=mesh['y'=4,'x'=4,'zl'=4,'core'=2,'mp'=2] {'y','x'}, dimensions={0} | all-to-all | bytes 983040 | tf_op jit(solution)/shard_map/all_to_all | solution.py:354
  67.3 0.1 convert_reduce_fusion
  67.4 0.7 collective-permute-start.10
  68.1 2.4 %collective-permute-start.9 = (bf16[120,128]{1,0:T(8,128)(2,1)S(1)}, bf16[120,128]{1,0:T(8,128)(2,1)S(1)}, u32[]{:S(2)}, u32[]{:S(2)}) collective-permute-start(bf16[120,128]{1,0:T(8,128)(2,1)S(1)} %convert_reduce_fusion), channel_id=1, source_target_pairs={{0,12},{4,0},{8,4},{12,8},{1,13},{5,1},{9,5},{13,9},{2,14},{6,2},{... | collective-permute-start | bytes 92168 | tf_op jit(solution)/shard_map/ppermute | solution.py:357
  70.5 0.7 collective-permute-done.10
  71.1 0.3 collective-permute-done.9
  71.5 3.6 %collective-permute-done.11 = bf16[120,128]{1,0:T(8,128)(2,1)S(1)} collective-permute-done((bf16[120,128]{1,0:T(8,128)(2,1)S(1)}, bf16[120,128]{1,0:T(8,128)(2,1)S(1)}, u32[]{:S(2)}, u32[]{:S(2)}) %collective-permute-start.11) | collective-permute-done | bytes 30752 | tf_op jit(solution)/shard_map/ppermute | solution.py:357
  75.1 3.9 %collective-permute-start.12 = (bf16[4,120,128]{2,1,0:T(8,128)(2,1)S(1)}, bf16[4,120,128]{2,1,0:T(8,128)(2,1)S(1)}, u32[]{:S(2)}, u32[]{:S(2)}) collective-permute-start(bf16[4,120,128]{2,1,0:T(8,128)(2,1)S(1)} %pad_maximum_fusion.mine), channel_id=1, source_target_pairs={{0,2},{2,0},{1,3},{3,1},{4,6},{6,4},{5,7},{7,5},{8,10},{10,8},{9,1... | collective-permute-start | bytes 368648 | tf_op jit(solution)/shard_map/ppermute | solution.py:449
  79.0 1.0 %collective-permute-done.12.other = bf16[4,120,128]{2,1,0:T(8,128)(2,1)S(1)} collective-permute-done((bf16[4,120,128]{2,1,0:T(8,128)(2,1)S(1)}, bf16[4,120,128]{2,1,0:T(8,128)(2,1)S(1)}, u32[]{:S(2)}, u32[]{:S(2)}) %collective-permute-start.12) | collective-permute-done | bytes 122912 | tf_op jit(solution)/shard_map/ppermute | solution.py:449
  80.0 1.0 %last.1 = (f32[64,1536]{1,0:T(8,128)}, f32[8,2,1536]{2,1,0:T(2,128)}) custom-call(bf16[4,120,128]{2,1,0:T(8,128)(2,1)S(1)} %pad_maximum_fusion.mine, bf16[4,120,128]{2,1,0:T(8,128)(2,1)S(1)} %collective-permute-done.12.other, bf16[64,1536]{1,0:T(8,128)(2,1)S(1)} %bitcast.31), custom_call_target="tpu_custom_call" | custom-call | flops 10000000 | bytes 1000000 | tf_op jit(solution)/shard_map/last/pallas_call | solution.py:451
  (36 shorter events, 0.3 us)
Async XLA Ops:
  0.6 5.7 %copy-start = (bf16[256,1536]{1,0:T(8,128)(2,1)S(1)}, bf16[256,1536]{1,0:T(8,128)(2,1)}, u32[]{:S(2)}) copy-start(bf16[256,1536]{1,0:T(8,128)(2,1)} %hidden.5) | copy-start | bytes 2359300
  0.6 23.0 %copy-start.7 = (bf16[9,512,16]{1,2,0:T(8,128)(2,1)S(1)}, bf16[9,512,16]{1,2,0:T(8,128)(2,1)}, u32[]{:S(2)}) copy-start(bf16[9,512,16]{1,2,0:T(8,128)(2,1)} %param.11) | copy-start | bytes 442372
  2.4 21.3 %collective-permute-start.1 = (bf16[2,128,512]{2,1,0:T(8,128)(2,1)S(1)}, bf16[2,128,512]{2,1,0:T(8,128)(2,1)S(1)}, u32[]{:S(2)}, u32[]{:S(2)}) collective-permute-start(bf16[2,128,512]{2,1,0:T(8,128)(2,1)S(1)} %slice.13), channel_id=1, source_target_pairs={{0,2},{2,4},{4,6},{6,8},{8,10},{10,12},{12,14},{14,16},{16,18},{18... | collective-permute-start | bytes 786440 | tf_op jit(solution)/shard_map/ppermute | solution.py:379
  6.3 17.4 %collective-permute-start = (bf16[4,16,128]{2,1,0:T(8,128)(2,1)S(1)}, bf16[4,16,128]{2,1,0:T(8,128)(2,1)S(1)}, u32[]{:S(2)}, u32[]{:S(2)}) collective-permute-start(bf16[4,16,128]{2,1,0:T(8,128)(2,1)S(1)} %slice.16), channel_id=1, source_target_pairs={{0,2},{2,4},{4,6},{6,8},{8,10},{10,12},{12,14},{14,16},{16,18},{18... | collective-permute-start | bytes 49160 | tf_op jit(solution)/shard_map/ppermute | solution.py:378
  6.4 0.9 %copy-start.1 = (bf16[1536,64]{0,1:T(8,128)(2,1)S(1)}, bf16[1536,64]{0,1:T(8,128)(2,1)}, u32[]{:S(2)}) copy-start(bf16[1536,64]{0,1:T(8,128)(2,1)} %param.17) | copy-start | bytes 589828
  7.3 0.9 %copy-start.3 = (bf16[16,2,1536]{2,1,0:T(2,128)(2,1)S(1)}, bf16[16,2,1536]{2,1,0:T(2,128)(2,1)}, u32[]{:S(2)}) copy-start(bf16[16,2,1536]{2,1,0:T(2,128)(2,1)} %mod.5) | copy-start | bytes 294916
  8.2 0.7 copy-start.5
  9.9 13.8 %collective-permute-start.2 = (bf16[4,16,128]{2,1,0:T(8,128)(2,1)S(1)}, bf16[4,16,128]{2,1,0:T(8,128)(2,1)S(1)}, u32[]{:S(2)}, u32[]{:S(2)}) collective-permute-start(bf16[4,16,128]{2,1,0:T(8,128)(2,1)S(1)} %slice.14), channel_id=1, source_target_pairs={{2,0},{4,2},{6,4},{8,6},{10,8},{12,10},{14,12},{16,14},{18,16},{20... | collective-permute-start | bytes 49160 | tf_op jit(solution)/shard_map/ppermute | solution.py:390
  10.5 32.9 %collective-permute-start.4 = (f32[264,128]{1,0:T(8,128)S(1)}, f32[264,128]{1,0:T(8,128)S(1)}, u32[]{:S(2)}, u32[]{:S(2)}) collective-permute-start(f32[264,128]{1,0:T(8,128)S(1)} %stats.1), channel_id=1, source_target_pairs={{0,1},{1,0},{2,3},{3,2},{4,5},{5,4},{6,7},{7,6},{8,9},{9,8},{10,11... | collective-permute-start | bytes 405512 | tf_op jit(solution)/shard_map/ppermute | solution.py:392
  16.5 18.7 %slice-start = ((s8[4718592]{0:T(1024)(128)(4,1)}), s8[4194304]{0:T(1024)(128)(4,1)S(1)}, s32[]{:S(2)}) async-start(s8[4718592]{0:T(1024)(128)(4,1)} %bitcast.38), calls=%async_computation.1 | async-start | bytes 8388608
  16.5 18.7 %collective-permute-start.3 = (bf16[2,128,512]{2,1,0:T(8,128)(2,1)S(1)}, bf16[2,128,512]{2,1,0:T(8,128)(2,1)S(1)}, u32[]{:S(2)}, u32[]{:S(2)}) collective-permute-start(bf16[2,128,512]{2,1,0:T(8,128)(2,1)S(1)} %slice.15), channel_id=1, source_target_pairs={{2,0},{4,2},{6,4},{8,6},{10,8},{12,10},{14,12},{16,14},{18,16},{20... | collective-permute-start | bytes 786440 | tf_op jit(solution)/shard_map/ppermute | solution.py:391
  23.7 11.5 %slice-start.1 = ((s8[4718592]{0:T(1024)(128)(4,1)}), s8[524288]{0:T(1024)(128)(4,1)S(1)}, s32[]{:S(2)}) async-start(s8[4718592]{0:T(1024)(128)(4,1)} %bitcast.38), calls=%async_computation.2 | async-start | bytes 1048576
  23.7 11.5 %copy-start.8 = (f32[8]{0:T(128)S(1)}, f32[8]{0:T(128)}, u32[]{:S(2)}) copy-start(f32[8]{0:T(128)} %steps.1) | copy-start | bytes 100
  35.2 8.1 %copy-start.2 = (bf16[1536,64]{0,1:T(8,128)(2,1)S(1)}, bf16[1536,64]{0,1:T(8,128)(2,1)}, u32[]{:S(2)}) copy-start(bf16[1536,64]{0,1:T(8,128)(2,1)} %param.17) | copy-start | bytes 589828
  35.2 8.1 %copy-start.4 = (bf16[16,2,1536]{2,1,0:T(2,128)(2,1)S(1)}, bf16[16,2,1536]{2,1,0:T(2,128)(2,1)}, u32[]{:S(2)}) copy-start(bf16[16,2,1536]{2,1,0:T(2,128)(2,1)} %mod.5) | copy-start | bytes 294916
  35.2 8.1 %copy-start.6 = (s32[8]{0:T(128)S(1)}, s32[8]{0:T(128)}, u32[]{:S(2)}) copy-start(s32[8]{0:T(128)} %prompts.5) | copy-start | bytes 100
  44.5 1.6 %collective-permute-start.5 = (bf16[480,128]{1,0:T(8,128)(2,1)S(1)}, bf16[480,128]{1,0:T(8,128)(2,1)S(1)}, u32[]{:S(2)}, u32[]{:S(2)}) collective-permute-start(bf16[480,128]{1,0:T(8,128)(2,1)S(1)} %get-tuple-element.30), channel_id=1, source_target_pairs={{0,2},{2,0},{1,3},{3,1},{4,6},{6,4},{5,7},{7,5},{8,10},{10,8},{9,1... | collective-permute-start | bytes 368648 | tf_op jit(solution)/shard_map/ppermute | solution.py:447
  46.2 3.8 %collective-permute-start.8 = (bf16[120,128]{1,0:T(8,128)(2,1)S(1)}, bf16[120,128]{1,0:T(8,128)(2,1)S(1)}, u32[]{:S(2)}, u32[]{:S(2)}) collective-permute-start(bf16[120,128]{1,0:T(8,128)(2,1)S(1)} %get-tuple-element.37), channel_id=1, source_target_pairs={{0,12},{4,0},{8,4},{12,8},{1,13},{5,1},{9,5},{13,9},{2,14},{6,2},{... | collective-permute-start | bytes 92168 | tf_op jit(solution)/shard_map/ppermute | solution.py:345
  46.3 3.8 %collective-permute-start.7 = (bf16[120,128]{1,0:T(8,128)(2,1)S(1)}, bf16[120,128]{1,0:T(8,128)(2,1)S(1)}, u32[]{:S(2)}, u32[]{:S(2)}) collective-permute-start(bf16[120,128]{1,0:T(8,128)(2,1)S(1)} %get-tuple-element.38), channel_id=1, source_target_pairs={{0,8},{4,12},{8,0},{12,4},{1,9},{5,13},{9,1},{13,5},{2,10},{6,14},... | collective-permute-start | bytes 92168 | tf_op jit(solution)/shard_map/ppermute | solution.py:345
  46.4 5.1 %collective-permute-start.6 = (bf16[120,128]{1,0:T(8,128)(2,1)S(1)}, bf16[120,128]{1,0:T(8,128)(2,1)S(1)}, u32[]{:S(2)}, u32[]{:S(2)}) collective-permute-start(bf16[120,128]{1,0:T(8,128)(2,1)S(1)} %get-tuple-element.39), channel_id=1, source_target_pairs={{0,4},{4,8},{8,12},{12,0},{1,5},{5,9},{9,13},{13,1},{2,6},{6,10},{... | collective-permute-start | bytes 92168 | tf_op jit(solution)/shard_map/ppermute | solution.py:345
  67.4 3.7 %collective-permute-start.10 = (bf16[120,128]{1,0:T(8,128)(2,1)S(1)}, bf16[120,128]{1,0:T(8,128)(2,1)S(1)}, u32[]{:S(2)}, u32[]{:S(2)}) collective-permute-start(bf16[120,128]{1,0:T(8,128)(2,1)S(1)} %convert_reduce_fusion), channel_id=1, source_target_pairs={{0,8},{4,12},{8,0},{12,4},{1,9},{5,13},{9,1},{13,5},{2,10},{6,14},... | collective-permute-start | bytes 92168 | tf_op jit(solution)/shard_map/ppermute | solution.py:357
  68.1 3.4 %collective-permute-start.9 = (bf16[120,128]{1,0:T(8,128)(2,1)S(1)}, bf16[120,128]{1,0:T(8,128)(2,1)S(1)}, u32[]{:S(2)}, u32[]{:S(2)}) collective-permute-start(bf16[120,128]{1,0:T(8,128)(2,1)S(1)} %convert_reduce_fusion), channel_id=1, source_target_pairs={{0,12},{4,0},{8,4},{12,8},{1,13},{5,1},{9,5},{13,9},{2,14},{6,2},{... | collective-permute-start | bytes 92168 | tf_op jit(solution)/shard_map/ppermute | solution.py:357
  70.5 4.6 %collective-permute-start.11 = (bf16[120,128]{1,0:T(8,128)(2,1)S(1)}, bf16[120,128]{1,0:T(8,128)(2,1)S(1)}, u32[]{:S(2)}, u32[]{:S(2)}) collective-permute-start(bf16[120,128]{1,0:T(8,128)(2,1)S(1)} %convert_reduce_fusion), channel_id=1, source_target_pairs={{0,4},{4,8},{8,12},{12,0},{1,5},{5,9},{9,13},{13,1},{2,6},{6,10},{... | collective-permute-start | bytes 92168 | tf_op jit(solution)/shard_map/ppermute | solution.py:357
  75.1 4.9 %collective-permute-start.12 = (bf16[4,120,128]{2,1,0:T(8,128)(2,1)S(1)}, bf16[4,120,128]{2,1,0:T(8,128)(2,1)S(1)}, u32[]{:S(2)}, u32[]{:S(2)}) collective-permute-start(bf16[4,120,128]{2,1,0:T(8,128)(2,1)S(1)} %pad_maximum_fusion.mine), channel_id=1, source_target_pairs={{0,2},{2,0},{1,3},{3,1},{4,6},{6,4},{5,7},{7,5},{8,10},{10,8},{9,1... | collective-permute-start | bytes 368648 | tf_op jit(solution)/shard_map/ppermute | solution.py:449

commit v5 on v4

--- a/solution.py
+++ b/solution.py
@@ -64,7 +64,7 @@
     for k in range(9):
         part = tap(k)
         total = part if total is None else total + part
-        for step in meanwhile[k::9]:
+        for step in meanwhile[k * len(meanwhile) // 9 : (k + 1) * len(meanwhile) // 9]:
             step()
     return total
 
@@ -100,7 +100,7 @@
         s = sigmoid(h)
         slope_two[pl.ds((i + j) * width, width), cols] = s * (1.0 + h * (1.0 - s))
 
-    per = 2
+    per = 4
     for i in range(per + 2):
         for cols in halves:
             first_layer(i, cols)
@@ -148,7 +148,7 @@
         g = back[j * width : (j + 1) * width, cols] * slope_one[at, cols]
         inner[at, cols] = masked(g, i + j - 1).astype(BF)
 
-    per = 2
+    per = 5
 
     def first_taps(i):
         taps.append(dot(w1t[...], inner[pl.ds(i * width, per * width), :], OVER_1))
@@ -237,28 +237,58 @@
     return chosen[0:1], 1.0 + chosen[1:2]
 
 
-def stats_kernel(geometry, prompts, hidden, mod, wt, out):
+def in_three(v):
+    high = v.astype(BF).astype(F32)
+    mid = (v - high).astype(BF).astype(F32)
+    return [high, mid, v - high - mid]
+
+
+def stats_kernel(geometry, prompts, hidden, mod, wt, own, send):
     _, gain = shift_and_gain(prompts[place_of(*geometry)[0]], mod)
-    patch = wt.shape[0]
+    patch, features = wt.shape
     tokens = hidden.shape[0]
     w_gain = (wt[...].astype(F32) * gain).astype(BF)
-    out[...] = jnp.zeros_like(out)
-    out[0:tokens, 0:patch] = dot(hidden[...], w_gain, OVER_1)
     states = hidden[...].astype(F32)
-    out[0:tokens, patch : patch + 1] = jnp.sum(states, axis=1, keepdims=True)
-    out[0:tokens, patch + 1 : patch + 2] = jnp.sum(states * states, axis=1, keepdims=True)
-    out[tokens:, 0:patch] = dot(jnp.ones((8, wt.shape[1]), BF), w_gain, OVER_1)
+    first = jnp.sum(states, axis=1, keepdims=True)
+    second = jnp.sum(states * states, axis=1, keepdims=True)
+    lane = lax.broadcasted_iota(jnp.int32, (tokens, 128), 1)
+    rows = jnp.where(lane == 0, first, jnp.where(lane == 1, second, 0.0)).T
+    first, second = rows[0:1], rows[1:2]
+    column = jnp.sum(w_gain.astype(F32), axis=1, keepdims=True)
+    cross = dot(w_gain, hidden[...], OVER_1) - column * (first / features)
+    line = dot(jnp.ones((8, features), BF), w_gain, OVER_1)[0:1]
+    line = jnp.concatenate([line, jnp.zeros((1, tokens - patch), F32)], 1)
+    none = jnp.zeros((1, tokens), F32)
+    own[0:patch, :] = cross
+    own[patch:, :] = jnp.concatenate([first, second, line] + [none] * 13, 0)
+    send[0:patch, :] = cross.astype(BF)
+    parts = in_three(first) + in_three(second) + in_three(line)
+    send[patch:, :] = jnp.concatenate(parts + [none] * 7, 0).astype(BF)
 
 
 def norm_of(width_all, patch, stats, stats_far, hidden):
-    tokens = hidden.shape[0]
-    both = stats[...] + stats_far[...]
-    mean_val = both[0:tokens, patch : patch + 1] / width_all
-    spread = both[0:tokens, patch + 1 : patch + 2] / width_all - mean_val * mean_val
+    own = stats[...]
+    far = stats_far[...].astype(F32)
+    tokens, half = hidden.shape
+    mine = [own[patch + i : patch + i + 1] for i in range(3)]
+    theirs = [
+        far[patch + 3 * i : patch + 3 * i + 1]
+        + far[patch + 3 * i + 1 : patch + 3 * i + 2]
+        + far[patch + 3 * i + 2 : patch + 3 * i + 3]
+        for i in range(3)
+    ]
+    mean_val = (mine[0] + theirs[0]) / width_all
+    spread = (mine[1] + theirs[1]) / width_all - mean_val * mean_val
     scale = 1.0 / jnp.sqrt(spread + 1e-06)
-    w_sum = both[tokens : tokens + 1, 0:patch]
-    cross = (both[0:tokens, 0:patch] - mean_val * w_sum) * scale
-    return (hidden[...].astype(F32) - mean_val) * scale, scale, w_sum, cross
+    apart = [mine[0] / half - mean_val, theirs[0] / half - mean_val]
+    rows = [own[0:patch] + far[0:patch], mean_val, scale] + apart
+    rows.append(jnp.zeros((128 - patch - 4, tokens), F32))
+    turned = jnp.concatenate(rows, 0).T
+    mean_val, scale = turned[:, patch : patch + 1], turned[:, patch + 1 : patch + 2]
+    w_own, w_far = mine[2][:, 0:patch], theirs[2][:, 0:patch]
+    cross = turned[:, 0:patch]
+    cross = cross + turned[:, patch + 2 : patch + 3] * w_own + turned[:, patch + 3 : patch + 4] * w_far
+    return (hidden[...].astype(F32) - mean_val) * scale, scale, w_own + w_far, cross * scale
 
 
 def sums_kernel(width_all, geometry, prompts, gvt, stats, stats_far, hidden, mod, wt, send, keep, held):
@@ -379,17 +409,20 @@
     cot_low = lax.ppermute(cot_own[-2:], TILE, up)
     wt = proj_w.T
 
-    stats = call(
+    stats, stats_send = call(
         functools.partial(stats_kernel, geometry),
-        jax.ShapeDtypeStruct((tokens + 8, 128), F32),
+        (
+            jax.ShapeDtypeStruct((patch + 16, tokens), F32),
+            jax.ShapeDtypeStruct((patch + 16, tokens), BF),
+        ),
         4,
         (10**8, 10**6),
         "stats",
+        vmem=54,
     )(prompt_ids, hidden, modulation, wt)
     lat_own, cot_own, stats = lax.optimization_barrier((lat_own, cot_own, stats))
     lat_high = lax.ppermute(lat_own[:4], TILE, down)
     cot_high = lax.ppermute(cot_own[:2], TILE, down)
-    stats_far = lax.ppermute(stats, "mp", [(0, 1), (1, 0)])
 
     lat_low, cot_low = lax.optimization_barrier((lat_low, cot_low))
     w1 = dec_w1.transpose(0, 2, 1).reshape(9 * ch, mid)
@@ -412,6 +445,8 @@
         far=1,
         vmem=46,
     )(lat_low, lat_own, lat_high, w1, dec_w2)
+    stats_send, slope_two = lax.optimization_barrier((stats_send, slope_two))
+    stats_far = lax.ppermute(stats_send, "mp", [(0, 1), (1, 0)])
     gvt = call(
         functools.partial(backward_kernel, geometry),
         jax.ShapeDtypeStruct((4 * ch, tokens), BF),

time: 81.2 us -> 82 us (level)
  local copies, waits for them, and re-layouts: 5.12 us -> 2.62 us
  blocking collectives: 15.7 us -> 17.5 us
    unnamed x23 -> x21, local copies, waits for them, and re-layouts: 4.22 us -> 1.73 us
    all_to_all x1, blocking collectives: 15.7 us -> 17.5 us  [sum_over_chips(): total = jnp.sum(lax.all_to_all(copies, plane, 0, 0).astype(F32), axis=0)]
    pallas_call x1, Pallas kernels: 1.05 us -> 2.32 us  [body(): call(functools.partial(stats_kernel, geometry), (jax.ShapeDtypeStruct((pa...]
    ppermute x1, starting transfers between devices: 0.66 us -> 1.65 us  [body(): total = keep + lax.ppermute(send, 'core', swap).astype(F32)]
  transfers between devices with their start and end apart: 13 -> 13, of which waited for: 7 -> 7; matrix products, arithmetic and copies ran while one was open for 1% -> 1% of each run, Pallas kernels for 28% -> 29%
where the time goes in v5:
time: 82 us; the launch traced here: 81.8 us
  starting transfers between devices  26.9 us (33%)
  Pallas kernels  25.5 us (31%)
  blocking collectives  17.5 us (21%)
  waiting for transfers between devices  8.17 us (10%)
  local copies, waits for them, and re-layouts  2.62 us (3%)
  between operations  0.87 us (1%)
    all_to_all x1, blocking collectives, sum_over_chips(): total = jnp.sum(lax.all_to_all(copies, plane, 0, 0).astype(F32), axis=0)  17.5 us
    pallas_call x1, Pallas kernels, body(): call(functools.partial(forward_kernel, geometry), (jax.ShapeDtypeStruct((...  11.2 us
    pallas_call x1, Pallas kernels, body(): call(functools.partial(backward_kernel, geometry), jax.ShapeDtypeStruct((...  7.57 us
    ppermute x1, starting transfers between devices, body(): cot_high = lax.ppermute(cot_own[:2], TILE, down)  7.56 us
    ppermute x1, starting transfers between devices, body(): stats_far = lax.ppermute(stats_send, 'mp', [(0, 1), (1, 0)])  5.45 us
    ppermute x3, waiting for transfers between devices, sum_over_chips(): lax.ppermute(total, 'zl', [(i, (i - d) % count) for i in range(count)])  4.57 us
    ppermute x1, starting transfers between devices, body(): other = lax.ppermute(mine, 'core', swap)  3.92 us
    ppermute x3, starting transfers between devices, sum_over_chips(): lax.ppermute(total, 'zl', [(i, (i - d) % count) for i in range(count)])  3.12 us
  transfers between devices with their start and end apart: 13, of which 7 were waited for; matrix products, arithmetic and copies ran while one was open for 1% of the time, Pallas kernels for 29%

profile of v5, /device:TPU:1, one launch (start us, length us, event | category | flops | bytes accessed | tf_op | source)
XLA Modules:
  0.0 81.8 jit_solution(6865355930668752371)
XLA Ops:
  0.6 1.7 %copy.14 = bf16[512,8,128]{0,2,1:T(8,128)(2,1)S(1)} copy(bf16[512,8,128]{2,1,0:T(8,128)(2,1)} %param.9) | data formatting | bytes 2097152 | tf_op args[0]
  2.3 3.1 %collective-permute-start.1 = (bf16[2,128,512]{2,1,0:T(8,128)(2,1)S(1)}, bf16[2,128,512]{2,1,0:T(8,128)(2,1)S(1)}, u32[]{:S(2)}, u32[]{:S(2)}) collective-permute-start(bf16[2,128,512]{2,1,0:T(8,128)(2,1)S(1)} %slice.13), channel_id=1, source_target_pairs={{0,2},{2,4},{4,6},{6,8},{8,10},{10,12},{12,14},{14,16},{16,18},{18... | collective-permute-start | bytes 786440 | tf_op jit(solution)/shard_map/ppermute | solution.py:409
  5.4 0.8 copy.17
  6.2 0.1 collective-permute-start
  6.3 2.3 %stats.1 = (f32[80,256]{1,0:T(8,128)}, bf16[80,256]{1,0:T(8,128)(2,1)}) custom-call(s32[8]{0:T(128)} %prompts.5, bf16[256,1536]{1,0:T(8,128)(2,1)} %hidden.5, bf16[16,2,1536]{2,1,0:T(2,128)(2,1)} %mod.5, bf16[64,1536]{1,0:T(8,128)(2,1)} %bitcast.28), custom_call_target="tpu_custom_call" | custom-call | flops 100000000 | bytes 1000000 | tf_op jit(solution)/shard_map/stats/pallas_call | solution.py:412
  8.6 0.5 collective-permute-start.2
  9.1 7.6 %collective-permute-start.3 = (bf16[2,128,512]{2,1,0:T(8,128)(2,1)S(1)}, bf16[2,128,512]{2,1,0:T(8,128)(2,1)S(1)}, u32[]{:S(2)}, u32[]{:S(2)}) collective-permute-start(bf16[2,128,512]{2,1,0:T(8,128)(2,1)S(1)} %slice.15), channel_id=1, source_target_pairs={{2,0},{4,2},{6,4},{8,6},{10,8},{12,10},{14,12},{16,14},{18,16},{20... | collective-permute-start | bytes 786440 | tf_op jit(solution)/shard_map/ppermute | solution.py:425
  16.7 0.0 slice-start.1
  16.8 0.0 copy-start.6
  16.8 11.2 %forward.1 = (f32[1536,512]{1,0:T(8,128)S(1)}, f32[1280,512]{1,0:T(8,128)S(1)}) custom-call(bf16[4,16,128]{2,1,0:T(8,128)(2,1)S(1)} %collective-permute-done.lat_low, bf16[8,16,128]{2,1,0:T(8,128)(2,1)S(1)} %bitcast.37, bf16[4,16,128]{2,1,0:T(8,128)(2,1)S(1)} %collective-permute-done.2.lat_high, bf16[144,512]{1,0:T(8,128)(2,1)S(1)} %bitcast.40, ...), custom_call_target="tpu_custom_call" | custom-call | flops 8000000000 | bytes 8000000 | tf_op jit(solution)/shard_map/forward/pallas_call | solution.py:429
  28.0 5.4 %collective-permute-start.4 = (bf16[80,256]{1,0:T(8,128)(2,1)S(1)}, bf16[80,256]{1,0:T(8,128)(2,1)S(1)}, u32[]{:S(2)}, u32[]{:S(2)}) collective-permute-start(bf16[80,256]{1,0:T(8,128)(2,1)S(1)} %copy-done.7), channel_id=1, source_target_pairs={{0,1},{1,0},{2,3},{3,2},{4,5},{5,4},{6,7},{7,6},{8,9},{9,8},{10,11... | collective-permute-start | bytes 122888 | tf_op jit(solution)/shard_map/ppermute | solution.py:449
  33.5 0.0 copy-start.1
  33.5 7.6 %backward.1.gvt = bf16[64,256]{1,0:T(8,128)(2,1)S(1)} custom-call(f32[8]{0:T(128)S(1)} %copy-done.6, f32[1536,512]{1,0:T(8,128)S(1)} %get-tuple-element.31.slope_two, f32[1280,512]{1,0:T(8,128)S(1)} %get-tuple-element.32.slope_one, bf16[2,128,512]{2,1,0:T(8,128)(2,1)S(1)} %collective-permute-done.1.cot_low, bf16[8,128,512]{2,1,0:T(8,128)(2,1)S(1)} %bitcast.34, ...), custom_call_target="tpu_custom_call" | custom-call | flops 7000000000 | bytes 8000000 | tf_op jit(solution)/shard_map/backward/pallas_call | solution.py:450
  41.2 1.2 %sums.1 = (bf16[480,128]{1,0:T(8,128)(2,1)S(1)}, f32[480,128]{1,0:T(8,128)S(1)}) custom-call(s32[8]{0:T(128)S(1)} %copy-done.4, bf16[64,256]{1,0:T(8,128)(2,1)S(1)} %backward.1.gvt, f32[80,256]{1,0:T(8,128)S(1)} %copy-done.3, bf16[80,256]{1,0:T(8,128)(2,1)S(1)} %collective-permute-done.4.stats_far, bf16[256,1536]{1,0:T(8,128)(2,1)S(1)} %copy-done, ...), custom_call_target="tpu_custom_call" | custom-call | flops 100000000 | bytes 2000000 | tf_op jit(solution)/shard_map/sums/pallas_call | solution.py:465
  42.4 1.6 %collective-permute-start.5 = (bf16[480,128]{1,0:T(8,128)(2,1)S(1)}, bf16[480,128]{1,0:T(8,128)(2,1)S(1)}, u32[]{:S(2)}, u32[]{:S(2)}) collective-permute-start(bf16[480,128]{1,0:T(8,128)(2,1)S(1)} %get-tuple-element.38), channel_id=1, source_target_pairs={{0,2},{2,0},{1,3},{3,1},{4,6},{6,4},{5,7},{7,5},{8,10},{10,8},{9,1... | collective-permute-start | bytes 368648 | tf_op jit(solution)/shard_map/ppermute | solution.py:482
  44.0 1.0 %collective-permute-done.5 = bf16[480,128]{1,0:T(8,128)(2,1)S(1)} collective-permute-done((bf16[480,128]{1,0:T(8,128)(2,1)S(1)}, bf16[480,128]{1,0:T(8,128)(2,1)S(1)}, u32[]{:S(2)}, u32[]{:S(2)}) %collective-permute-start.5) | collective-permute-done | bytes 122912 | tf_op jit(solution)/shard_map/ppermute | solution.py:482
  45.0 0.9 %collective-permute-start.8 = (bf16[120,128]{1,0:T(8,128)(2,1)S(1)}, bf16[120,128]{1,0:T(8,128)(2,1)S(1)}, u32[]{:S(2)}, u32[]{:S(2)}) collective-permute-start(bf16[120,128]{1,0:T(8,128)(2,1)S(1)} %get-tuple-element.45), channel_id=1, source_target_pairs={{0,12},{4,0},{8,4},{12,8},{1,13},{5,1},{9,5},{13,9},{2,14},{6,2},{... | collective-permute-start | bytes 92168 | tf_op jit(solution)/shard_map/ppermute | solution.py:375
  46.0 0.6 collective-permute-start.6
  46.6 2.3 %grad_hidden.1 = bf16[256,1536]{1,0:T(8,128)(2,1)} custom-call(s32[8]{0:T(128)S(1)} %copy-done.4, bf16[64,256]{1,0:T(8,128)(2,1)S(1)} %backward.1.gvt, f32[80,256]{1,0:T(8,128)S(1)} %copy-done.3, bf16[80,256]{1,0:T(8,128)(2,1)S(1)} %collective-permute-done.4.stats_far, bf16[256,1536]{1,0:T(8,128)(2,1)S(1)} %copy-done, bf16[16,2,1536]{2,1,0:T(2,128)(2,1)S(1)} %copy-done.2, ...), custom_call_target="tpu_custom_call" | custom-call | flops 100000000 | bytes 2000000 | tf_op jit(solution)/shard_map/grad_hidden/pallas_call | solution.py:473
  48.9 0.7 collective-permute-done.7
  49.6 0.9 %collective-permute-done.6 = bf16[120,128]{1,0:T(8,128)(2,1)S(1)} collective-permute-done((bf16[120,128]{1,0:T(8,128)(2,1)S(1)}, bf16[120,128]{1,0:T(8,128)(2,1)S(1)}, u32[]{:S(2)}, u32[]{:S(2)}) %collective-permute-start.6) | collective-permute-done | bytes 30752 | tf_op jit(solution)/shard_map/ppermute | solution.py:375
  50.5 0.1 broadcast_in_dim.2
  50.6 17.5 %all_to_all.5 = bf16[16,120,128]{2,1,0:T(8,128)(2,1)S(1)} all-to-all(bf16[16,120,128]{2,1,0:T(8,128)(2,1)S(1)} %broadcast_in_dim.2), channel_id=1, replica_groups=mesh['y'=4,'x'=4,'zl'=4,'core'=2,'mp'=2] {'y','x'}, dimensions={0} | all-to-all | bytes 983040 | tf_op jit(solution)/shard_map/all_to_all | solution.py:384
  68.1 0.1 convert_reduce_fusion
  68.2 0.7 collective-permute-start.10
  68.9 2.5 %collective-permute-start.9 = (bf16[120,128]{1,0:T(8,128)(2,1)S(1)}, bf16[120,128]{1,0:T(8,128)(2,1)S(1)}, u32[]{:S(2)}, u32[]{:S(2)}) collective-permute-start(bf16[120,128]{1,0:T(8,128)(2,1)S(1)} %convert_reduce_fusion), channel_id=1, source_target_pairs={{0,12},{4,0},{8,4},{12,8},{1,13},{5,1},{9,5},{13,9},{2,14},{6,2},{... | collective-permute-start | bytes 92168 | tf_op jit(solution)/shard_map/ppermute | solution.py:387
  71.3 0.6 collective-permute-done.10
  71.9 0.4 collective-permute-done.9
  72.3 3.6 %collective-permute-done.11 = bf16[120,128]{1,0:T(8,128)(2,1)S(1)} collective-permute-done((bf16[120,128]{1,0:T(8,128)(2,1)S(1)}, bf16[120,128]{1,0:T(8,128)(2,1)S(1)}, u32[]{:S(2)}, u32[]{:S(2)}) %collective-permute-start.11) | collective-permute-done | bytes 30752 | tf_op jit(solution)/shard_map/ppermute | solution.py:387
  75.9 3.9 %collective-permute-start.12 = (bf16[4,120,128]{2,1,0:T(8,128)(2,1)S(1)}, bf16[4,120,128]{2,1,0:T(8,128)(2,1)S(1)}, u32[]{:S(2)}, u32[]{:S(2)}) collective-permute-start(bf16[4,120,128]{2,1,0:T(8,128)(2,1)S(1)} %pad_maximum_fusion.mine), channel_id=1, source_target_pairs={{0,2},{2,0},{1,3},{3,1},{4,6},{6,4},{5,7},{7,5},{8,10},{10,8},{9,1... | collective-permute-start | bytes 368648 | tf_op jit(solution)/shard_map/ppermute | solution.py:484
  79.8 1.0 %collective-permute-done.12.other = bf16[4,120,128]{2,1,0:T(8,128)(2,1)S(1)} collective-permute-done((bf16[4,120,128]{2,1,0:T(8,128)(2,1)S(1)}, bf16[4,120,128]{2,1,0:T(8,128)(2,1)S(1)}, u32[]{:S(2)}, u32[]{:S(2)}) %collective-permute-start.12) | collective-permute-done | bytes 122912 | tf_op jit(solution)/shard_map/ppermute | solution.py:484
  80.8 1.0 %last.1 = (f32[64,1536]{1,0:T(8,128)}, f32[8,2,1536]{2,1,0:T(2,128)}) custom-call(bf16[4,120,128]{2,1,0:T(8,128)(2,1)S(1)} %pad_maximum_fusion.mine, bf16[4,120,128]{2,1,0:T(8,128)(2,1)S(1)} %collective-permute-done.12.other, bf16[64,1536]{1,0:T(8,128)(2,1)S(1)} %bitcast.31), custom_call_target="tpu_custom_call" | custom-call | flops 10000000 | bytes 1000000 | tf_op jit(solution)/shard_map/last/pallas_call | solution.py:486
  (34 shorter events, 0.2 us)
Async XLA Ops:
  0.6 16.1 %copy-start.5 = (bf16[9,512,16]{1,2,0:T(8,128)(2,1)S(1)}, bf16[9,512,16]{1,2,0:T(8,128)(2,1)}, u32[]{:S(2)}) copy-start(bf16[9,512,16]{1,2,0:T(8,128)(2,1)} %param.11) | copy-start | bytes 442372
  2.3 14.4 %collective-permute-start.1 = (bf16[2,128,512]{2,1,0:T(8,128)(2,1)S(1)}, bf16[2,128,512]{2,1,0:T(8,128)(2,1)S(1)}, u32[]{:S(2)}, u32[]{:S(2)}) collective-permute-start(bf16[2,128,512]{2,1,0:T(8,128)(2,1)S(1)} %slice.13), channel_id=1, source_target_pairs={{0,2},{2,4},{4,6},{6,8},{8,10},{10,12},{12,14},{14,16},{16,18},{18... | collective-permute-start | bytes 786440 | tf_op jit(solution)/shard_map/ppermute | solution.py:409
  6.2 10.5 %collective-permute-start = (bf16[4,16,128]{2,1,0:T(8,128)(2,1)S(1)}, bf16[4,16,128]{2,1,0:T(8,128)(2,1)S(1)}, u32[]{:S(2)}, u32[]{:S(2)}) collective-permute-start(bf16[4,16,128]{2,1,0:T(8,128)(2,1)S(1)} %slice.16), channel_id=1, source_target_pairs={{0,2},{2,4},{4,6},{6,8},{8,10},{10,12},{12,14},{14,16},{16,18},{18... | collective-permute-start | bytes 49160 | tf_op jit(solution)/shard_map/ppermute | solution.py:408
  8.6 8.1 %collective-permute-start.2 = (bf16[4,16,128]{2,1,0:T(8,128)(2,1)S(1)}, bf16[4,16,128]{2,1,0:T(8,128)(2,1)S(1)}, u32[]{:S(2)}, u32[]{:S(2)}) collective-permute-start(bf16[4,16,128]{2,1,0:T(8,128)(2,1)S(1)} %slice.14), channel_id=1, source_target_pairs={{2,0},{4,2},{6,4},{8,6},{10,8},{12,10},{14,12},{16,14},{18,16},{20... | collective-permute-start | bytes 49160 | tf_op jit(solution)/shard_map/ppermute | solution.py:424
  9.1 24.3 %slice-start = ((s8[4718592]{0:T(1024)(128)(4,1)}), s8[4194304]{0:T(1024)(128)(4,1)S(1)}, s32[]{:S(2)}) async-start(s8[4718592]{0:T(1024)(128)(4,1)} %bitcast.38), calls=%async_computation.1 | async-start | bytes 8388608
  9.1 24.3 %collective-permute-start.3 = (bf16[2,128,512]{2,1,0:T(8,128)(2,1)S(1)}, bf16[2,128,512]{2,1,0:T(8,128)(2,1)S(1)}, u32[]{:S(2)}, u32[]{:S(2)}) collective-permute-start(bf16[2,128,512]{2,1,0:T(8,128)(2,1)S(1)} %slice.15), channel_id=1, source_target_pairs={{2,0},{4,2},{6,4},{8,6},{10,8},{12,10},{14,12},{16,14},{18,16},{20... | collective-permute-start | bytes 786440 | tf_op jit(solution)/shard_map/ppermute | solution.py:425
  16.7 11.3 %copy-start.7 = (bf16[80,256]{1,0:T(8,128)(2,1)S(1)}, bf16[80,256]{1,0:T(8,128)(2,1)}, u32[]{:S(2)}) copy-start(bf16[80,256]{1,0:T(8,128)(2,1)} %get-tuple-element.36) | copy-start | bytes 122884
  16.7 16.7 %slice-start.1 = ((s8[4718592]{0:T(1024)(128)(4,1)}), s8[524288]{0:T(1024)(128)(4,1)S(1)}, s32[]{:S(2)}) async-start(s8[4718592]{0:T(1024)(128)(4,1)} %bitcast.38), calls=%async_computation.2 | async-start | bytes 1048576
  16.8 16.7 %copy-start.6 = (f32[8]{0:T(128)S(1)}, f32[8]{0:T(128)}, u32[]{:S(2)}) copy-start(f32[8]{0:T(128)} %steps.1) | copy-start | bytes 100
  28.0 13.1 %collective-permute-start.4 = (bf16[80,256]{1,0:T(8,128)(2,1)S(1)}, bf16[80,256]{1,0:T(8,128)(2,1)S(1)}, u32[]{:S(2)}, u32[]{:S(2)}) collective-permute-start(bf16[80,256]{1,0:T(8,128)(2,1)S(1)} %copy-done.7), channel_id=1, source_target_pairs={{0,1},{1,0},{2,3},{3,2},{4,5},{5,4},{6,7},{7,6},{8,9},{9,8},{10,11... | collective-permute-start | bytes 122888 | tf_op jit(solution)/shard_map/ppermute | solution.py:449
  33.5 7.7 %copy-start = (bf16[256,1536]{1,0:T(8,128)(2,1)S(1)}, bf16[256,1536]{1,0:T(8,128)(2,1)}, u32[]{:S(2)}) copy-start(bf16[256,1536]{1,0:T(8,128)(2,1)} %hidden.5) | copy-start | bytes 2359300
  33.5 7.6 %copy-start.1 = (bf16[1536,64]{0,1:T(8,128)(2,1)S(1)}, bf16[1536,64]{0,1:T(8,128)(2,1)}, u32[]{:S(2)}) copy-start(bf16[1536,64]{0,1:T(8,128)(2,1)} %param.17) | copy-start | bytes 589828
  33.5 7.6 %copy-start.2 = (bf16[16,2,1536]{2,1,0:T(2,128)(2,1)S(1)}, bf16[16,2,1536]{2,1,0:T(2,128)(2,1)}, u32[]{:S(2)}) copy-start(bf16[16,2,1536]{2,1,0:T(2,128)(2,1)} %mod.5) | copy-start | bytes 294916
  33.5 7.6 %copy-start.3 = (f32[80,256]{1,0:T(8,128)S(1)}, f32[80,256]{1,0:T(8,128)}, u32[]{:S(2)}) copy-start(f32[80,256]{1,0:T(8,128)} %get-tuple-element.35.stats) | copy-start | bytes 245764
  33.5 7.6 %copy-start.4 = (s32[8]{0:T(128)S(1)}, s32[8]{0:T(128)}, u32[]{:S(2)}) copy-start(s32[8]{0:T(128)} %prompts.5) | copy-start | bytes 100
  42.4 2.6 %collective-permute-start.5 = (bf16[480,128]{1,0:T(8,128)(2,1)S(1)}, bf16[480,128]{1,0:T(8,128)(2,1)S(1)}, u32[]{:S(2)}, u32[]{:S(2)}) collective-permute-start(bf16[480,128]{1,0:T(8,128)(2,1)S(1)} %get-tuple-element.38), channel_id=1, source_target_pairs={{0,2},{2,0},{1,3},{3,1},{4,6},{6,4},{5,7},{7,5},{8,10},{10,8},{9,1... | collective-permute-start | bytes 368648 | tf_op jit(solution)/shard_map/ppermute | solution.py:482
  45.0 3.9 %collective-permute-start.8 = (bf16[120,128]{1,0:T(8,128)(2,1)S(1)}, bf16[120,128]{1,0:T(8,128)(2,1)S(1)}, u32[]{:S(2)}, u32[]{:S(2)}) collective-permute-start(bf16[120,128]{1,0:T(8,128)(2,1)S(1)} %get-tuple-element.45), channel_id=1, source_target_pairs={{0,12},{4,0},{8,4},{12,8},{1,13},{5,1},{9,5},{13,9},{2,14},{6,2},{... | collective-permute-start | bytes 92168 | tf_op jit(solution)/shard_map/ppermute | solution.py:375
  46.0 3.6 %collective-permute-start.7 = (bf16[120,128]{1,0:T(8,128)(2,1)S(1)}, bf16[120,128]{1,0:T(8,128)(2,1)S(1)}, u32[]{:S(2)}, u32[]{:S(2)}) collective-permute-start(bf16[120,128]{1,0:T(8,128)(2,1)S(1)} %get-tuple-element.46), channel_id=1, source_target_pairs={{0,8},{4,12},{8,0},{12,4},{1,9},{5,13},{9,1},{13,5},{2,10},{6,14},... | collective-permute-start | bytes 92168 | tf_op jit(solution)/shard_map/ppermute | solution.py:375
  46.0 4.6 %collective-permute-start.6 = (bf16[120,128]{1,0:T(8,128)(2,1)S(1)}, bf16[120,128]{1,0:T(8,128)(2,1)S(1)}, u32[]{:S(2)}, u32[]{:S(2)}) collective-permute-start(bf16[120,128]{1,0:T(8,128)(2,1)S(1)} %get-tuple-element.47), channel_id=1, source_target_pairs={{0,4},{4,8},{8,12},{12,0},{1,5},{5,9},{9,13},{13,1},{2,6},{6,10},{... | collective-permute-start | bytes 92168 | tf_op jit(solution)/shard_map/ppermute | solution.py:375
  68.2 3.7 %collective-permute-start.10 = (bf16[120,128]{1,0:T(8,128)(2,1)S(1)}, bf16[120,128]{1,0:T(8,128)(2,1)S(1)}, u32[]{:S(2)}, u32[]{:S(2)}) collective-permute-start(bf16[120,128]{1,0:T(8,128)(2,1)S(1)} %convert_reduce_fusion), channel_id=1, source_target_pairs={{0,8},{4,12},{8,0},{12,4},{1,9},{5,13},{9,1},{13,5},{2,10},{6,14},... | collective-permute-start | bytes 92168 | tf_op jit(solution)/shard_map/ppermute | solution.py:387
  68.9 3.5 %collective-permute-start.9 = (bf16[120,128]{1,0:T(8,128)(2,1)S(1)}, bf16[120,128]{1,0:T(8,128)(2,1)S(1)}, u32[]{:S(2)}, u32[]{:S(2)}) collective-permute-start(bf16[120,128]{1,0:T(8,128)(2,1)S(1)} %convert_reduce_fusion), channel_id=1, source_target_pairs={{0,12},{4,0},{8,4},{12,8},{1,13},{5,1},{9,5},{13,9},{2,14},{6,2},{... | collective-permute-start | bytes 92168 | tf_op jit(solution)/shard_map/ppermute | solution.py:387
  71.3 4.6 %collective-permute-start.11 = (bf16[120,128]{1,0:T(8,128)(2,1)S(1)}, bf16[120,128]{1,0:T(8,128)(2,1)S(1)}, u32[]{:S(2)}, u32[]{:S(2)}) collective-permute-start(bf16[120,128]{1,0:T(8,128)(2,1)S(1)} %convert_reduce_fusion), channel_id=1, source_target_pairs={{0,4},{4,8},{8,12},{12,0},{1,5},{5,9},{9,13},{13,1},{2,6},{6,10},{... | collective-permute-start | bytes 92168 | tf_op jit(solution)/shard_map/ppermute | solution.py:387
  75.9 4.9 %collective-permute-start.12 = (bf16[4,120,128]{2,1,0:T(8,128)(2,1)S(1)}, bf16[4,120,128]{2,1,0:T(8,128)(2,1)S(1)}, u32[]{:S(2)}, u32[]{:S(2)}) collective-permute-start(bf16[4,120,128]{2,1,0:T(8,128)(2,1)S(1)} %pad_maximum_fusion.mine), channel_id=1, source_target_pairs={{0,2},{2,0},{1,3},{3,1},{4,6},{6,4},{5,7},{7,5},{8,10},{10,8},{9,1... | collective-permute-start | bytes 368648 | tf_op jit(solution)/shard_map/ppermute | solution.py:484

commit v6 on v5

--- a/solution.py
+++ b/solution.py
@@ -402,10 +402,11 @@
     up = [(i, (i + 1) % count) for i in range(count)]
     down = [(b, a) for a, b in up]
 
+    lat_own = lax.optimization_barrier(latent.transpose(1, 0, 2))
+    feat_cot, lat_own = lax.optimization_barrier((feat_cot, lat_own))
+    lat_low = lax.ppermute(lat_own[-4:], TILE, up)
+    lat_high = lax.ppermute(lat_own[:4], TILE, down)
     cot_own = lax.optimization_barrier(feat_cot.transpose(1, 2, 0))
-    latent, cot_own = lax.optimization_barrier((latent, cot_own))
-    lat_own = lax.optimization_barrier(latent.transpose(1, 0, 2))
-    lat_low = lax.ppermute(lat_own[-4:], TILE, up)
     cot_low = lax.ppermute(cot_own[-2:], TILE, up)
     wt = proj_w.T
 
@@ -420,11 +421,9 @@
         "stats",
         vmem=54,
     )(prompt_ids, hidden, modulation, wt)
-    lat_own, cot_own, stats = lax.optimization_barrier((lat_own, cot_own, stats))
-    lat_high = lax.ppermute(lat_own[:4], TILE, down)
+    cot_own, stats = lax.optimization_barrier((cot_own, stats))
     cot_high = lax.ppermute(cot_own[:2], TILE, down)
 
-    lat_low, cot_low = lax.optimization_barrier((lat_low, cot_low))
     w1 = dec_w1.transpose(0, 2, 1).reshape(9 * ch, mid)
     slope_two, slope_one = call(
         functools.partial(forward_kernel, geometry),

time: 82 us -> 80.6 us (0.983)
  blocking collectives: 17.5 us -> 12.2 us
  starting transfers between devices: 26.9 us -> 31.8 us
  waiting for transfers between devices: 8.17 us -> 7.27 us
    ppermute x1, starting transfers between devices: 1.65 us -> 8.12 us  [body(): total = keep + lax.ppermute(send, 'core', swap).astype(F32)]
    all_to_all x1, blocking collectives: 17.5 us -> 12.2 us  [sum_over_chips(): total = jnp.sum(lax.all_to_all(copies, plane, 0, 0).astype(F32), axis=0)]
    ppermute x1, starting transfers between devices: 0.49 us -> 3.32 us  [body(): lat_high = lax.ppermute(lat_own[:4], TILE, down)]
    ppermute x1, starting transfers between devices: 3.1 us -> 0.37 us  [body(): cot_low = lax.ppermute(cot_own[-2:], TILE, up)]
    ppermute x1, starting transfers between devices: 5.45 us -> 4.46 us  [body(): stats_far = lax.ppermute(stats_send, 'mp', [(0, 1), (1, 0)])]
    unnamed x21, local copies, waits for them, and re-layouts: 1.73 us -> 0.86 us
    optimization_barrier x1, local copies, waits for them, and re-layouts: 0.76 us -> 1.63 us  [body(): feat_cot, lat_own = lax.optimization_barrier((feat_cot, lat_own))]
  transfers between devices with their start and end apart: 13 -> 13, of which waited for: 7 -> 7; matrix products, arithmetic and copies ran while one was open for 1% -> 2% of each run, Pallas kernels for 29% -> 29%
where the time goes in v6:
time: 80.6 us; the launch traced here: 80.4 us
  starting transfers between devices  31.8 us (39%)
  Pallas kernels  25.5 us (32%)
  blocking collectives  12.2 us (15%)
  waiting for transfers between devices  7.27 us (9%)
  local copies, waits for them, and re-layouts  2.62 us (3%)
  between operations  0.89 us (1%)
    all_to_all x1, blocking collectives, sum_over_chips(): total = jnp.sum(lax.all_to_all(copies, plane, 0, 0).astype(F32), axis=0)  12.2 us
    pallas_call x1, Pallas kernels, body(): call(functools.partial(forward_kernel, geometry), (jax.ShapeDtypeStruct((...  11.2 us
    ppermute x1, starting transfers between devices, body(): total = keep + lax.ppermute(send, 'core', swap).astype(F32)  8.12 us
    pallas_call x1, Pallas kernels, body(): call(functools.partial(backward_kernel, geometry), jax.ShapeDtypeStruct((...  7.56 us
    ppermute x1, starting transfers between devices, body(): cot_high = lax.ppermute(cot_own[:2], TILE, down)  6.78 us
    ppermute x1, starting transfers between devices, body(): stats_far = lax.ppermute(stats_send, 'mp', [(0, 1), (1, 0)])  4.46 us
    ppermute x1, starting transfers between devices, body(): other = lax.ppermute(mine, 'core', swap)  4.23 us
    ppermute x3, waiting for transfers between devices, sum_over_chips(): lax.ppermute(total, 'zl', [(i, (i - d) % count) for i in range(count)])  3.86 us
  transfers between devices with their start and end apart: 13, of which 7 were waited for; matrix products, arithmetic and copies ran while one was open for 2% of the time, Pallas kernels for 29%

profile of v6, /device:TPU:1, one launch (start us, length us, event | category | flops | bytes accessed | tf_op | source)
XLA Modules:
  0.0 80.4 jit_solution(13029187256032108288)
XLA Ops:
  0.6 0.8 copy.17
  1.4 3.3 %collective-permute-start.1 = (bf16[4,16,128]{2,1,0:T(8,128)(2,1)S(1)}, bf16[4,16,128]{2,1,0:T(8,128)(2,1)S(1)}, u32[]{:S(2)}, u32[]{:S(2)}) collective-permute-start(bf16[4,16,128]{2,1,0:T(8,128)(2,1)S(1)} %get-tuple-element.42), channel_id=1, source_target_pairs={{2,0},{4,2},{6,4},{8,6},{10,8},{12,10},{14,12},{16,14},{18,16},{20... | collective-permute-start | bytes 49160 | tf_op jit(solution)/shard_map/ppermute | solution.py:408
  4.8 1.6 %copy.15 = bf16[512,8,128]{0,2,1:T(8,128)(2,1)S(1)} copy(bf16[512,8,128]{2,1,0:T(8,128)(2,1)} %param.9) | data formatting | bytes 2097152 | tf_op jit(solution)/shard_map/optimization_barrier | solution.py:406
  6.4 0.4 collective-permute-start.2
  6.8 2.3 %stats.1 = (f32[80,256]{1,0:T(8,128)}, bf16[80,256]{1,0:T(8,128)(2,1)}) custom-call(s32[8]{0:T(128)} %prompts.5, bf16[256,1536]{1,0:T(8,128)(2,1)} %hidden.5, bf16[16,2,1536]{2,1,0:T(2,128)(2,1)} %mod.5, bf16[64,1536]{1,0:T(8,128)(2,1)} %bitcast.28), custom_call_target="tpu_custom_call" | custom-call | flops 100000000 | bytes 1000000 | tf_op jit(solution)/shard_map/stats/pallas_call | solution.py:413
  9.1 6.8 %collective-permute-start.3 = (bf16[2,128,512]{2,1,0:T(8,128)(2,1)S(1)}, bf16[2,128,512]{2,1,0:T(8,128)(2,1)S(1)}, u32[]{:S(2)}, u32[]{:S(2)}) collective-permute-start(bf16[2,128,512]{2,1,0:T(8,128)(2,1)S(1)} %slice.15), channel_id=1, source_target_pairs={{2,0},{4,2},{6,4},{8,6},{10,8},{12,10},{14,12},{16,14},{18,16},{20... | collective-permute-start | bytes 786440 | tf_op jit(solution)/shard_map/ppermute | solution.py:425
  15.9 0.0 slice-start.1
  16.0 0.0 copy-start.6
  16.0 11.2 %forward.1 = (f32[1536,512]{1,0:T(8,128)S(1)}, f32[1280,512]{1,0:T(8,128)S(1)}) custom-call(bf16[4,16,128]{2,1,0:T(8,128)(2,1)S(1)} %collective-permute-done.lat_low, bf16[8,16,128]{2,1,0:T(8,128)(2,1)S(1)} %bitcast.36, bf16[4,16,128]{2,1,0:T(8,128)(2,1)S(1)} %collective-permute-done.1.lat_high, bf16[144,512]{1,0:T(8,128)(2,1)S(1)} %bitcast.39, ...), custom_call_target="tpu_custom_call" | custom-call | flops 8000000000 | bytes 8000000 | tf_op jit(solution)/shard_map/forward/pallas_call | solution.py:428
  27.2 4.5 %collective-permute-start.4 = (bf16[80,256]{1,0:T(8,128)(2,1)S(1)}, bf16[80,256]{1,0:T(8,128)(2,1)S(1)}, u32[]{:S(2)}, u32[]{:S(2)}) collective-permute-start(bf16[80,256]{1,0:T(8,128)(2,1)S(1)} %copy-done.7), channel_id=1, source_target_pairs={{0,1},{1,0},{2,3},{3,2},{4,5},{5,4},{6,7},{7,6},{8,9},{9,8},{10,11... | collective-permute-start | bytes 122888 | tf_op jit(solution)/shard_map/ppermute | solution.py:448
  31.8 7.6 %backward.1.gvt = bf16[64,256]{1,0:T(8,128)(2,1)S(1)} custom-call(f32[8]{0:T(128)S(1)} %copy-done.6, f32[1536,512]{1,0:T(8,128)S(1)} %get-tuple-element.24.slope_two, f32[1280,512]{1,0:T(8,128)S(1)} %get-tuple-element.25.slope_one, bf16[2,128,512]{2,1,0:T(8,128)(2,1)S(1)} %collective-permute-done.2.cot_low, bf16[8,128,512]{2,1,0:T(8,128)(2,1)S(1)} %bitcast.34, ...), custom_call_target="tpu_custom_call" | custom-call | flops 7000000000 | bytes 8000000 | tf_op jit(solution)/shard_map/backward/pallas_call | solution.py:449
  39.4 1.2 %sums.1 = (bf16[480,128]{1,0:T(8,128)(2,1)S(1)}, f32[480,128]{1,0:T(8,128)S(1)}) custom-call(s32[8]{0:T(128)S(1)} %copy-done.4, bf16[64,256]{1,0:T(8,128)(2,1)S(1)} %backward.1.gvt, f32[80,256]{1,0:T(8,128)S(1)} %copy-done.3, bf16[80,256]{1,0:T(8,128)(2,1)S(1)} %collective-permute-done.4.stats_far, bf16[256,1536]{1,0:T(8,128)(2,1)S(1)} %copy-done, ...), custom_call_target="tpu_custom_call" | custom-call | flops 100000000 | bytes 2000000 | tf_op jit(solution)/shard_map/sums/pallas_call | solution.py:464
  40.6 8.1 %collective-permute-start.5 = (bf16[480,128]{1,0:T(8,128)(2,1)S(1)}, bf16[480,128]{1,0:T(8,128)(2,1)S(1)}, u32[]{:S(2)}, u32[]{:S(2)}) collective-permute-start(bf16[480,128]{1,0:T(8,128)(2,1)S(1)} %get-tuple-element.32), channel_id=1, source_target_pairs={{0,2},{2,0},{1,3},{3,1},{4,6},{6,4},{5,7},{7,5},{8,10},{10,8},{9,1... | collective-permute-start | bytes 368648 | tf_op jit(solution)/shard_map/ppermute | solution.py:481
  48.7 1.0 %collective-permute-done.5 = bf16[480,128]{1,0:T(8,128)(2,1)S(1)} collective-permute-done((bf16[480,128]{1,0:T(8,128)(2,1)S(1)}, bf16[480,128]{1,0:T(8,128)(2,1)S(1)}, u32[]{:S(2)}, u32[]{:S(2)}) %collective-permute-start.5) | collective-permute-done | bytes 122912 | tf_op jit(solution)/shard_map/ppermute | solution.py:481
  49.7 0.1 collective-permute-start.8
  49.8 0.1 collective-permute-start.7
  49.9 1.4 %collective-permute-start.6 = (bf16[120,128]{1,0:T(8,128)(2,1)S(1)}, bf16[120,128]{1,0:T(8,128)(2,1)S(1)}, u32[]{:S(2)}, u32[]{:S(2)}) collective-permute-start(bf16[120,128]{1,0:T(8,128)(2,1)S(1)} %get-tuple-element.41), channel_id=1, source_target_pairs={{0,4},{4,8},{8,12},{12,0},{1,5},{5,9},{9,13},{13,1},{2,6},{6,10},{... | collective-permute-start | bytes 92168 | tf_op jit(solution)/shard_map/ppermute | solution.py:375
  51.3 2.3 %grad_hidden.1 = bf16[256,1536]{1,0:T(8,128)(2,1)} custom-call(s32[8]{0:T(128)S(1)} %copy-done.4, bf16[64,256]{1,0:T(8,128)(2,1)S(1)} %backward.1.gvt, f32[80,256]{1,0:T(8,128)S(1)} %copy-done.3, bf16[80,256]{1,0:T(8,128)(2,1)S(1)} %collective-permute-done.4.stats_far, bf16[256,1536]{1,0:T(8,128)(2,1)S(1)} %copy-done, bf16[16,2,1536]{2,1,0:T(2,128)(2,1)S(1)} %copy-done.2, ...), custom_call_target="tpu_custom_call" | custom-call | flops 100000000 | bytes 2000000 | tf_op jit(solution)/shard_map/grad_hidden/pallas_call | solution.py:472
  53.6 0.1 collective-permute-done.7
  53.7 1.4 %collective-permute-done.6 = bf16[120,128]{1,0:T(8,128)(2,1)S(1)} collective-permute-done((bf16[120,128]{1,0:T(8,128)(2,1)S(1)}, bf16[120,128]{1,0:T(8,128)(2,1)S(1)}, u32[]{:S(2)}, u32[]{:S(2)}) %collective-permute-start.6) | collective-permute-done | bytes 30752 | tf_op jit(solution)/shard_map/ppermute | solution.py:375
  55.1 0.1 broadcast_in_dim.2
  55.1 12.2 %all_to_all.5 = bf16[16,120,128]{2,1,0:T(8,128)(2,1)S(1)} all-to-all(bf16[16,120,128]{2,1,0:T(8,128)(2,1)S(1)} %broadcast_in_dim.2), channel_id=1, replica_groups=mesh['y'=4,'x'=4,'zl'=4,'core'=2,'mp'=2] {'y','x'}, dimensions={0} | all-to-all | bytes 983040 | tf_op jit(solution)/shard_map/all_to_all | solution.py:384
  67.3 0.1 convert_reduce_fusion
  67.4 1.5 %collective-permute-start.10 = (bf16[120,128]{1,0:T(8,128)(2,1)S(1)}, bf16[120,128]{1,0:T(8,128)(2,1)S(1)}, u32[]{:S(2)}, u32[]{:S(2)}) collective-permute-start(bf16[120,128]{1,0:T(8,128)(2,1)S(1)} %convert_reduce_fusion), channel_id=1, source_target_pairs={{0,8},{4,12},{8,0},{12,4},{1,9},{5,13},{9,1},{13,5},{2,10},{6,14},... | collective-permute-start | bytes 92168 | tf_op jit(solution)/shard_map/ppermute | solution.py:387
  68.9 0.7 collective-permute-start.9
  69.5 0.8 %collective-permute-start.11 = (bf16[120,128]{1,0:T(8,128)(2,1)S(1)}, bf16[120,128]{1,0:T(8,128)(2,1)S(1)}, u32[]{:S(2)}, u32[]{:S(2)}) collective-permute-start(bf16[120,128]{1,0:T(8,128)(2,1)S(1)} %convert_reduce_fusion), channel_id=1, source_target_pairs={{0,4},{4,8},{8,12},{12,0},{1,5},{5,9},{9,13},{13,1},{2,6},{6,10},{... | collective-permute-start | bytes 92168 | tf_op jit(solution)/shard_map/ppermute | solution.py:387
  70.4 0.8 collective-permute-done.10
  71.2 0.5 collective-permute-done.9
  71.6 2.6 %collective-permute-done.11 = bf16[120,128]{1,0:T(8,128)(2,1)S(1)} collective-permute-done((bf16[120,128]{1,0:T(8,128)(2,1)S(1)}, bf16[120,128]{1,0:T(8,128)(2,1)S(1)}, u32[]{:S(2)}, u32[]{:S(2)}) %collective-permute-start.11) | collective-permute-done | bytes 30752 | tf_op jit(solution)/shard_map/ppermute | solution.py:387
  74.2 4.2 %collective-permute-start.12 = (bf16[4,120,128]{2,1,0:T(8,128)(2,1)S(1)}, bf16[4,120,128]{2,1,0:T(8,128)(2,1)S(1)}, u32[]{:S(2)}, u32[]{:S(2)}) collective-permute-start(bf16[4,120,128]{2,1,0:T(8,128)(2,1)S(1)} %pad_maximum_fusion.mine), channel_id=1, source_target_pairs={{0,2},{2,0},{1,3},{3,1},{4,6},{6,4},{5,7},{7,5},{8,10},{10,8},{9,1... | collective-permute-start | bytes 368648 | tf_op jit(solution)/shard_map/ppermute | solution.py:483
  78.5 1.0 %collective-permute-done.12.other = bf16[4,120,128]{2,1,0:T(8,128)(2,1)S(1)} collective-permute-done((bf16[4,120,128]{2,1,0:T(8,128)(2,1)S(1)}, bf16[4,120,128]{2,1,0:T(8,128)(2,1)S(1)}, u32[]{:S(2)}, u32[]{:S(2)}) %collective-permute-start.12) | collective-permute-done | bytes 122912 | tf_op jit(solution)/shard_map/ppermute | solution.py:483
  79.5 1.0 %last.1 = (f32[64,1536]{1,0:T(8,128)}, f32[8,2,1536]{2,1,0:T(2,128)}) custom-call(bf16[4,120,128]{2,1,0:T(8,128)(2,1)S(1)} %pad_maximum_fusion.mine, bf16[4,120,128]{2,1,0:T(8,128)(2,1)S(1)} %collective-permute-done.12.other, bf16[64,1536]{1,0:T(8,128)(2,1)S(1)} %bitcast.31), custom_call_target="tpu_custom_call" | custom-call | flops 10000000 | bytes 1000000 | tf_op jit(solution)/shard_map/last/pallas_call | solution.py:485
  (33 shorter events, 0.2 us)
Async XLA Ops:
  0.6 15.3 %copy-start.5 = (bf16[9,512,16]{1,2,0:T(8,128)(2,1)S(1)}, bf16[9,512,16]{1,2,0:T(8,128)(2,1)}, u32[]{:S(2)}) copy-start(bf16[9,512,16]{1,2,0:T(8,128)(2,1)} %param.11) | copy-start | bytes 442372
  1.4 14.5 %collective-permute-start.1 = (bf16[4,16,128]{2,1,0:T(8,128)(2,1)S(1)}, bf16[4,16,128]{2,1,0:T(8,128)(2,1)S(1)}, u32[]{:S(2)}, u32[]{:S(2)}) collective-permute-start(bf16[4,16,128]{2,1,0:T(8,128)(2,1)S(1)} %get-tuple-element.42), channel_id=1, source_target_pairs={{2,0},{4,2},{6,4},{8,6},{10,8},{12,10},{14,12},{16,14},{18,16},{20... | collective-permute-start | bytes 49160 | tf_op jit(solution)/shard_map/ppermute | solution.py:408
  4.8 11.2 %collective-permute-start = (bf16[4,16,128]{2,1,0:T(8,128)(2,1)S(1)}, bf16[4,16,128]{2,1,0:T(8,128)(2,1)S(1)}, u32[]{:S(2)}, u32[]{:S(2)}) collective-permute-start(bf16[4,16,128]{2,1,0:T(8,128)(2,1)S(1)} %get-tuple-element.43), channel_id=1, source_target_pairs={{0,2},{2,4},{4,6},{6,8},{8,10},{10,12},{12,14},{14,16},{16,18},{18... | collective-permute-start | bytes 49160 | tf_op jit(solution)/shard_map/ppermute | solution.py:407
  6.4 25.2 %collective-permute-start.2 = (bf16[2,128,512]{2,1,0:T(8,128)(2,1)S(1)}, bf16[2,128,512]{2,1,0:T(8,128)(2,1)S(1)}, u32[]{:S(2)}, u32[]{:S(2)}) collective-permute-start(bf16[2,128,512]{2,1,0:T(8,128)(2,1)S(1)} %slice.16), channel_id=1, source_target_pairs={{0,2},{2,4},{4,6},{6,8},{8,10},{10,12},{12,14},{14,16},{16,18},{18... | collective-permute-start | bytes 786440 | tf_op jit(solution)/shard_map/ppermute | solution.py:410
  9.1 22.6 %slice-start = ((s8[4718592]{0:T(1024)(128)(4,1)}), s8[4194304]{0:T(1024)(128)(4,1)S(1)}, s32[]{:S(2)}) async-start(s8[4718592]{0:T(1024)(128)(4,1)} %bitcast.37), calls=%async_computation.1 | async-start | bytes 8388608
  9.1 22.5 %collective-permute-start.3 = (bf16[2,128,512]{2,1,0:T(8,128)(2,1)S(1)}, bf16[2,128,512]{2,1,0:T(8,128)(2,1)S(1)}, u32[]{:S(2)}, u32[]{:S(2)}) collective-permute-start(bf16[2,128,512]{2,1,0:T(8,128)(2,1)S(1)} %slice.15), channel_id=1, source_target_pairs={{2,0},{4,2},{6,4},{8,6},{10,8},{12,10},{14,12},{16,14},{18,16},{20... | collective-permute-start | bytes 786440 | tf_op jit(solution)/shard_map/ppermute | solution.py:425
  15.9 11.3 %copy-start.7 = (bf16[80,256]{1,0:T(8,128)(2,1)S(1)}, bf16[80,256]{1,0:T(8,128)(2,1)}, u32[]{:S(2)}) copy-start(bf16[80,256]{1,0:T(8,128)(2,1)} %get-tuple-element.30) | copy-start | bytes 122884
  15.9 15.8 %slice-start.1 = ((s8[4718592]{0:T(1024)(128)(4,1)}), s8[524288]{0:T(1024)(128)(4,1)S(1)}, s32[]{:S(2)}) async-start(s8[4718592]{0:T(1024)(128)(4,1)} %bitcast.37), calls=%async_computation.2 | async-start | bytes 1048576
  16.0 15.7 %copy-start.6 = (f32[8]{0:T(128)S(1)}, f32[8]{0:T(128)}, u32[]{:S(2)}) copy-start(f32[8]{0:T(128)} %steps.1) | copy-start | bytes 100
  27.2 12.1 %collective-permute-start.4 = (bf16[80,256]{1,0:T(8,128)(2,1)S(1)}, bf16[80,256]{1,0:T(8,128)(2,1)S(1)}, u32[]{:S(2)}, u32[]{:S(2)}) collective-permute-start(bf16[80,256]{1,0:T(8,128)(2,1)S(1)} %copy-done.7), channel_id=1, source_target_pairs={{0,1},{1,0},{2,3},{3,2},{4,5},{5,4},{6,7},{7,6},{8,9},{9,8},{10,11... | collective-permute-start | bytes 122888 | tf_op jit(solution)/shard_map/ppermute | solution.py:448
  31.7 7.6 %copy-start = (bf16[256,1536]{1,0:T(8,128)(2,1)S(1)}, bf16[256,1536]{1,0:T(8,128)(2,1)}, u32[]{:S(2)}) copy-start(bf16[256,1536]{1,0:T(8,128)(2,1)} %hidden.5) | copy-start | bytes 2359300
  31.7 7.6 %copy-start.1 = (bf16[1536,64]{0,1:T(8,128)(2,1)S(1)}, bf16[1536,64]{0,1:T(8,128)(2,1)}, u32[]{:S(2)}) copy-start(bf16[1536,64]{0,1:T(8,128)(2,1)} %param.17) | copy-start | bytes 589828
  31.7 7.6 %copy-start.2 = (bf16[16,2,1536]{2,1,0:T(2,128)(2,1)S(1)}, bf16[16,2,1536]{2,1,0:T(2,128)(2,1)}, u32[]{:S(2)}) copy-start(bf16[16,2,1536]{2,1,0:T(2,128)(2,1)} %mod.5) | copy-start | bytes 294916
  31.8 7.6 %copy-start.3 = (f32[80,256]{1,0:T(8,128)S(1)}, f32[80,256]{1,0:T(8,128)}, u32[]{:S(2)}) copy-start(f32[80,256]{1,0:T(8,128)} %get-tuple-element.29.stats) | copy-start | bytes 245764
  31.8 7.6 %copy-start.4 = (s32[8]{0:T(128)S(1)}, s32[8]{0:T(128)}, u32[]{:S(2)}) copy-start(s32[8]{0:T(128)} %prompts.5) | copy-start | bytes 100
  40.6 9.1 %collective-permute-start.5 = (bf16[480,128]{1,0:T(8,128)(2,1)S(1)}, bf16[480,128]{1,0:T(8,128)(2,1)S(1)}, u32[]{:S(2)}, u32[]{:S(2)}) collective-permute-start(bf16[480,128]{1,0:T(8,128)(2,1)S(1)} %get-tuple-element.32), channel_id=1, source_target_pairs={{0,2},{2,0},{1,3},{3,1},{4,6},{6,4},{5,7},{7,5},{8,10},{10,8},{9,1... | collective-permute-start | bytes 368648 | tf_op jit(solution)/shard_map/ppermute | solution.py:481
  49.7 3.9 %collective-permute-start.8 = (bf16[120,128]{1,0:T(8,128)(2,1)S(1)}, bf16[120,128]{1,0:T(8,128)(2,1)S(1)}, u32[]{:S(2)}, u32[]{:S(2)}) collective-permute-start(bf16[120,128]{1,0:T(8,128)(2,1)S(1)} %get-tuple-element.39), channel_id=1, source_target_pairs={{0,12},{4,0},{8,4},{12,8},{1,13},{5,1},{9,5},{13,9},{2,14},{6,2},{... | collective-permute-start | bytes 92168 | tf_op jit(solution)/shard_map/ppermute | solution.py:375
  49.8 3.8 %collective-permute-start.7 = (bf16[120,128]{1,0:T(8,128)(2,1)S(1)}, bf16[120,128]{1,0:T(8,128)(2,1)S(1)}, u32[]{:S(2)}, u32[]{:S(2)}) collective-permute-start(bf16[120,128]{1,0:T(8,128)(2,1)S(1)} %get-tuple-element.40), channel_id=1, source_target_pairs={{0,8},{4,12},{8,0},{12,4},{1,9},{5,13},{9,1},{13,5},{2,10},{6,14},... | collective-permute-start | bytes 92168 | tf_op jit(solution)/shard_map/ppermute | solution.py:375
  49.9 5.1 %collective-permute-start.6 = (bf16[120,128]{1,0:T(8,128)(2,1)S(1)}, bf16[120,128]{1,0:T(8,128)(2,1)S(1)}, u32[]{:S(2)}, u32[]{:S(2)}) collective-permute-start(bf16[120,128]{1,0:T(8,128)(2,1)S(1)} %get-tuple-element.41), channel_id=1, source_target_pairs={{0,4},{4,8},{8,12},{12,0},{1,5},{5,9},{9,13},{13,1},{2,6},{6,10},{... | collective-permute-start | bytes 92168 | tf_op jit(solution)/shard_map/ppermute | solution.py:375
  67.4 3.7 %collective-permute-start.10 = (bf16[120,128]{1,0:T(8,128)(2,1)S(1)}, bf16[120,128]{1,0:T(8,128)(2,1)S(1)}, u32[]{:S(2)}, u32[]{:S(2)}) collective-permute-start(bf16[120,128]{1,0:T(8,128)(2,1)S(1)} %convert_reduce_fusion), channel_id=1, source_target_pairs={{0,8},{4,12},{8,0},{12,4},{1,9},{5,13},{9,1},{13,5},{2,10},{6,14},... | collective-permute-start | bytes 92168 | tf_op jit(solution)/shard_map/ppermute | solution.py:387
  68.9 2.7 %collective-permute-start.9 = (bf16[120,128]{1,0:T(8,128)(2,1)S(1)}, bf16[120,128]{1,0:T(8,128)(2,1)S(1)}, u32[]{:S(2)}, u32[]{:S(2)}) collective-permute-start(bf16[120,128]{1,0:T(8,128)(2,1)S(1)} %convert_reduce_fusion), channel_id=1, source_target_pairs={{0,12},{4,0},{8,4},{12,8},{1,13},{5,1},{9,5},{13,9},{2,14},{6,2},{... | collective-permute-start | bytes 92168 | tf_op jit(solution)/shard_map/ppermute | solution.py:387
  69.5 4.7 %collective-permute-start.11 = (bf16[120,128]{1,0:T(8,128)(2,1)S(1)}, bf16[120,128]{1,0:T(8,128)(2,1)S(1)}, u32[]{:S(2)}, u32[]{:S(2)}) collective-permute-start(bf16[120,128]{1,0:T(8,128)(2,1)S(1)} %convert_reduce_fusion), channel_id=1, source_target_pairs={{0,4},{4,8},{8,12},{12,0},{1,5},{5,9},{9,13},{13,1},{2,6},{6,10},{... | collective-permute-start | bytes 92168 | tf_op jit(solution)/shard_map/ppermute | solution.py:387
  74.2 5.2 %collective-permute-start.12 = (bf16[4,120,128]{2,1,0:T(8,128)(2,1)S(1)}, bf16[4,120,128]{2,1,0:T(8,128)(2,1)S(1)}, u32[]{:S(2)}, u32[]{:S(2)}) collective-permute-start(bf16[4,120,128]{2,1,0:T(8,128)(2,1)S(1)} %pad_maximum_fusion.mine), channel_id=1, source_target_pairs={{0,2},{2,0},{1,3},{3,1},{4,6},{6,4},{5,7},{7,5},{8,10},{10,8},{9,1... | collective-permute-start | bytes 368648 | tf_op jit(solution)/shard_map/ppermute | solution.py:483

commit v7 on v6

--- a/solution.py
+++ b/solution.py
@@ -378,10 +378,15 @@
     came, beside = lax.optimization_barrier((came, beside))
     for block in came:
         total = total + block.astype(F32)
-    plane = ("y", "x")
-    chips = lax.axis_size(plane)
-    copies = jnp.broadcast_to(total.astype(BF)[None], (chips,) + total.shape)
-    total = jnp.sum(lax.all_to_all(copies, plane, 0, 0).astype(F32), axis=0)
+    for axis in ("x", "y"):
+        size = lax.axis_size(axis)
+        out = total.astype(BF)
+        came = [
+            lax.ppermute(out, axis, [(i, (i + d) % size) for i in range(size)])
+            for d in range(1, size)
+        ]
+        for block in came:
+            total = total + block.astype(F32)
     total = lax.optimization_barrier(total).astype(BF)
     came = [
         lax.ppermute(total, "zl", [(i, (i - d) % count) for i in range(count)])

time: 80.6 us -> 80.7 us (level)
  blocking collectives: 12.2 us -> 0 us
  waiting for transfers between devices: 7.27 us -> 14.9 us
  starting transfers between devices: 31.8 us -> 36.5 us
    all_to_all x1 -> x0, blocking collectives: 12.2 us -> none  [sum_over_chips(): total = jnp.sum(lax.all_to_all(copies, plane, 0, 0).astype(F32), axis=0)]
    ppermute x0 -> x6, waiting for transfers between devices: none -> 7.34 us  [sum_over_chips(): lax.ppermute(out, axis, [(i, (i + d) % size) for i in range(size)])]
    ppermute x0 -> x6, starting transfers between devices: none -> 3.06 us  [sum_over_chips(): lax.ppermute(out, axis, [(i, (i + d) % size) for i in range(size)])]
    ppermute x1, starting transfers between devices: 4.23 us -> 6.38 us  [body(): other = lax.ppermute(mine, 'core', swap)]
  transfers between devices with their start and end apart: 13 -> 19, of which waited for: 7 -> 13; matrix products, arithmetic and copies ran while one was open for 2% -> 2% of each run, Pallas kernels for 29% -> 29%
where the time goes in v7:
time: 80.7 us; the launch traced here: 80.5 us
  starting transfers between devices  36.5 us (45%)
  Pallas kernels  25.5 us (32%)
  waiting for transfers between devices  14.9 us (18%)
  local copies, waits for them, and re-layouts  2.55 us (3%)
  between operations  0.92 us (1%)
    pallas_call x1, Pallas kernels, body(): call(functools.partial(forward_kernel, geometry), (jax.ShapeDtypeStruct((...  11.2 us
    ppermute x1, starting transfers between devices, body(): total = keep + lax.ppermute(send, 'core', swap).astype(F32)  8.12 us
    pallas_call x1, Pallas kernels, body(): call(functools.partial(backward_kernel, geometry), jax.ShapeDtypeStruct((...  7.56 us
    ppermute x6, waiting for transfers between devices, sum_over_chips(): lax.ppermute(out, axis, [(i, (i + d) % size) for i in range(size)])  7.34 us
    ppermute x1, starting transfers between devices, body(): cot_high = lax.ppermute(cot_own[:2], TILE, down)  6.78 us
    ppermute x1, starting transfers between devices, body(): other = lax.ppermute(mine, 'core', swap)  6.38 us
    ppermute x1, starting transfers between devices, body(): stats_far = lax.ppermute(stats_send, 'mp', [(0, 1), (1, 0)])  4.46 us
    ppermute x3, waiting for transfers between devices, sum_over_chips(): lax.ppermute(total, 'zl', [(i, (i - d) % count) for i in range(count)])  4.18 us
  transfers between devices with their start and end apart: 19, of which 13 were waited for; matrix products, arithmetic and copies ran while one was open for 2% of the time, Pallas kernels for 29%

profile of v7, /device:TPU:1, one launch (start us, length us, event | category | flops | bytes accessed | tf_op | source)
XLA Modules:
  0.0 80.5 jit_solution(4444629381799644265)
XLA Ops:
  0.6 0.8 copy.15
  1.4 3.3 %collective-permute-start.1 = (bf16[4,16,128]{2,1,0:T(8,128)(2,1)S(1)}, bf16[4,16,128]{2,1,0:T(8,128)(2,1)S(1)}, u32[]{:S(2)}, u32[]{:S(2)}) collective-permute-start(bf16[4,16,128]{2,1,0:T(8,128)(2,1)S(1)} %get-tuple-element.44), channel_id=1, source_target_pairs={{2,0},{4,2},{6,4},{8,6},{10,8},{12,10},{14,12},{16,14},{18,16},{20... | collective-permute-start | bytes 49160 | tf_op jit(solution)/shard_map/ppermute | solution.py:413
  4.8 1.6 %copy.13 = bf16[512,8,128]{0,2,1:T(8,128)(2,1)S(1)} copy(bf16[512,8,128]{2,1,0:T(8,128)(2,1)} %param.9) | data formatting | bytes 2097152 | tf_op jit(solution)/shard_map/optimization_barrier | solution.py:411
  6.4 0.4 collective-permute-start.2
  6.8 2.3 %stats.1 = (f32[80,256]{1,0:T(8,128)}, bf16[80,256]{1,0:T(8,128)(2,1)}) custom-call(s32[8]{0:T(128)} %prompts.5, bf16[256,1536]{1,0:T(8,128)(2,1)} %hidden.5, bf16[16,2,1536]{2,1,0:T(2,128)(2,1)} %mod.5, bf16[64,1536]{1,0:T(8,128)(2,1)} %bitcast.27), custom_call_target="tpu_custom_call" | custom-call | flops 100000000 | bytes 1000000 | tf_op jit(solution)/shard_map/stats/pallas_call | solution.py:418
  9.1 6.8 %collective-permute-start.3 = (bf16[2,128,512]{2,1,0:T(8,128)(2,1)S(1)}, bf16[2,128,512]{2,1,0:T(8,128)(2,1)S(1)}, u32[]{:S(2)}, u32[]{:S(2)}) collective-permute-start(bf16[2,128,512]{2,1,0:T(8,128)(2,1)S(1)} %slice.15), channel_id=1, source_target_pairs={{2,0},{4,2},{6,4},{8,6},{10,8},{12,10},{14,12},{16,14},{18,16},{20... | collective-permute-start | bytes 786440 | tf_op jit(solution)/shard_map/ppermute | solution.py:430
  16.0 11.2 %forward.1 = (f32[1536,512]{1,0:T(8,128)S(1)}, f32[1280,512]{1,0:T(8,128)S(1)}) custom-call(bf16[4,16,128]{2,1,0:T(8,128)(2,1)S(1)} %collective-permute-done.lat_low, bf16[8,16,128]{2,1,0:T(8,128)(2,1)S(1)} %bitcast.35, bf16[4,16,128]{2,1,0:T(8,128)(2,1)S(1)} %collective-permute-done.1.lat_high, bf16[144,512]{1,0:T(8,128)(2,1)S(1)} %bitcast.38, ...), custom_call_target="tpu_custom_call" | custom-call | flops 8000000000 | bytes 8000000 | tf_op jit(solution)/shard_map/forward/pallas_call | solution.py:433
  27.2 4.5 %collective-permute-start.4 = (bf16[80,256]{1,0:T(8,128)(2,1)S(1)}, bf16[80,256]{1,0:T(8,128)(2,1)S(1)}, u32[]{:S(2)}, u32[]{:S(2)}) collective-permute-start(bf16[80,256]{1,0:T(8,128)(2,1)S(1)} %copy-done.7), channel_id=1, source_target_pairs={{0,1},{1,0},{2,3},{3,2},{4,5},{5,4},{6,7},{7,6},{8,9},{9,8},{10,11... | collective-permute-start | bytes 122888 | tf_op jit(solution)/shard_map/ppermute | solution.py:453
  31.8 7.6 %backward.1.gvt = bf16[64,256]{1,0:T(8,128)(2,1)S(1)} custom-call(f32[8]{0:T(128)S(1)} %copy-done.6, f32[1536,512]{1,0:T(8,128)S(1)} %get-tuple-element.24.slope_two, f32[1280,512]{1,0:T(8,128)S(1)} %get-tuple-element.25.slope_one, bf16[2,128,512]{2,1,0:T(8,128)(2,1)S(1)} %collective-permute-done.2.cot_low, bf16[8,128,512]{2,1,0:T(8,128)(2,1)S(1)} %bitcast.33, ...), custom_call_target="tpu_custom_call" | custom-call | flops 7000000000 | bytes 8000000 | tf_op jit(solution)/shard_map/backward/pallas_call | solution.py:454
  39.4 1.2 %sums.1 = (bf16[480,128]{1,0:T(8,128)(2,1)S(1)}, f32[480,128]{1,0:T(8,128)S(1)}) custom-call(s32[8]{0:T(128)S(1)} %copy-done.4, bf16[64,256]{1,0:T(8,128)(2,1)S(1)} %backward.1.gvt, f32[80,256]{1,0:T(8,128)S(1)} %copy-done.3, bf16[80,256]{1,0:T(8,128)(2,1)S(1)} %collective-permute-done.4.stats_far, bf16[256,1536]{1,0:T(8,128)(2,1)S(1)} %copy-done, ...), custom_call_target="tpu_custom_call" | custom-call | flops 100000000 | bytes 2000000 | tf_op jit(solution)/shard_map/sums/pallas_call | solution.py:469
  40.6 8.1 %collective-permute-start.5 = (bf16[480,128]{1,0:T(8,128)(2,1)S(1)}, bf16[480,128]{1,0:T(8,128)(2,1)S(1)}, u32[]{:S(2)}, u32[]{:S(2)}) collective-permute-start(bf16[480,128]{1,0:T(8,128)(2,1)S(1)} %get-tuple-element.32), channel_id=1, source_target_pairs={{0,2},{2,0},{1,3},{3,1},{4,6},{6,4},{5,7},{7,5},{8,10},{10,8},{9,1... | collective-permute-start | bytes 368648 | tf_op jit(solution)/shard_map/ppermute | solution.py:486
  48.7 1.0 %collective-permute-done.5 = bf16[480,128]{1,0:T(8,128)(2,1)S(1)} collective-permute-done((bf16[480,128]{1,0:T(8,128)(2,1)S(1)}, bf16[480,128]{1,0:T(8,128)(2,1)S(1)}, u32[]{:S(2)}, u32[]{:S(2)}) %collective-permute-start.5) | collective-permute-done | bytes 122912 | tf_op jit(solution)/shard_map/ppermute | solution.py:486
  49.9 1.4 %collective-permute-start.6 = (bf16[120,128]{1,0:T(8,128)(2,1)S(1)}, bf16[120,128]{1,0:T(8,128)(2,1)S(1)}, u32[]{:S(2)}, u32[]{:S(2)}) collective-permute-start(bf16[120,128]{1,0:T(8,128)(2,1)S(1)} %get-tuple-element.43), channel_id=1, source_target_pairs={{0,4},{4,8},{8,12},{12,0},{1,5},{5,9},{9,13},{13,1},{2,6},{6,10},{... | collective-permute-start | bytes 92168 | tf_op jit(solution)/shard_map/ppermute | solution.py:375
  51.3 2.3 %grad_hidden.1 = bf16[256,1536]{1,0:T(8,128)(2,1)} custom-call(s32[8]{0:T(128)S(1)} %copy-done.4, bf16[64,256]{1,0:T(8,128)(2,1)S(1)} %backward.1.gvt, f32[80,256]{1,0:T(8,128)S(1)} %copy-done.3, bf16[80,256]{1,0:T(8,128)(2,1)S(1)} %collective-permute-done.4.stats_far, bf16[256,1536]{1,0:T(8,128)(2,1)S(1)} %copy-done, bf16[16,2,1536]{2,1,0:T(2,128)(2,1)S(1)} %copy-done.2, ...), custom_call_target="tpu_custom_call" | custom-call | flops 100000000 | bytes 2000000 | tf_op jit(solution)/shard_map/grad_hidden/pallas_call | solution.py:477
  53.7 1.4 %collective-permute-done.6 = bf16[120,128]{1,0:T(8,128)(2,1)S(1)} collective-permute-done((bf16[120,128]{1,0:T(8,128)(2,1)S(1)}, bf16[120,128]{1,0:T(8,128)(2,1)S(1)}, u32[]{:S(2)}, u32[]{:S(2)}) %collective-permute-start.6) | collective-permute-done | bytes 30752 | tf_op jit(solution)/shard_map/ppermute | solution.py:375
  55.2 1.4 %collective-permute-start.9 = (bf16[120,128]{1,0:T(8,128)(2,1)S(1)}, bf16[120,128]{1,0:T(8,128)(2,1)S(1)}, u32[]{:S(2)}, u32[]{:S(2)}) collective-permute-start(bf16[120,128]{1,0:T(8,128)(2,1)S(1)} %get-tuple-element.39), channel_id=1, source_target_pairs={{0,16},{16,32},{32,48},{48,0},{1,17},{17,33},{33,49},{49,1},{2,18}... | collective-permute-start | bytes 92168 | tf_op jit(solution)/shard_map/ppermute | solution.py:385
  56.6 1.3 %collective-permute-done.11 = bf16[120,128]{1,0:T(8,128)(2,1)S(1)} collective-permute-done((bf16[120,128]{1,0:T(8,128)(2,1)S(1)}, bf16[120,128]{1,0:T(8,128)(2,1)S(1)}, u32[]{:S(2)}, u32[]{:S(2)}) %collective-permute-start.11) | collective-permute-done | bytes 30752 | tf_op jit(solution)/shard_map/ppermute | solution.py:385
  57.9 1.6 %collective-permute-done.10 = bf16[120,128]{1,0:T(8,128)(2,1)S(1)} collective-permute-done((bf16[120,128]{1,0:T(8,128)(2,1)S(1)}, bf16[120,128]{1,0:T(8,128)(2,1)S(1)}, u32[]{:S(2)}, u32[]{:S(2)}) %collective-permute-start.10) | collective-permute-done | bytes 30752 | tf_op jit(solution)/shard_map/ppermute | solution.py:385
  59.5 0.8 collective-permute-done.9
  60.5 1.4 %collective-permute-start.12 = (bf16[120,128]{1,0:T(8,128)(2,1)S(1)}, bf16[120,128]{1,0:T(8,128)(2,1)S(1)}, u32[]{:S(2)}, u32[]{:S(2)}) collective-permute-start(bf16[120,128]{1,0:T(8,128)(2,1)S(1)} %fusion.5), channel_id=1, source_target_pairs={{0,64},{64,128},{128,192},{192,0},{1,65},{65,129},{129,193},{193,1... | collective-permute-start | bytes 92168 | tf_op jit(solution)/shard_map/ppermute | solution.py:385
  61.8 1.3 %collective-permute-done.14 = bf16[120,128]{1,0:T(8,128)(2,1)S(1)} collective-permute-done((bf16[120,128]{1,0:T(8,128)(2,1)S(1)}, bf16[120,128]{1,0:T(8,128)(2,1)S(1)}, u32[]{:S(2)}, u32[]{:S(2)}) %collective-permute-start.14) | collective-permute-done | bytes 30752 | tf_op jit(solution)/shard_map/ppermute | solution.py:385
  63.1 1.6 %collective-permute-done.13 = bf16[120,128]{1,0:T(8,128)(2,1)S(1)} collective-permute-done((bf16[120,128]{1,0:T(8,128)(2,1)S(1)}, bf16[120,128]{1,0:T(8,128)(2,1)S(1)}, u32[]{:S(2)}, u32[]{:S(2)}) %collective-permute-start.13) | collective-permute-done | bytes 30752 | tf_op jit(solution)/shard_map/ppermute | solution.py:385
  64.7 0.8 collective-permute-done.12
  65.5 1.0 %collective-permute-start.16 = (bf16[120,128]{1,0:T(8,128)(2,1)S(1)}, bf16[120,128]{1,0:T(8,128)(2,1)S(1)}, u32[]{:S(2)}, u32[]{:S(2)}) collective-permute-start(bf16[120,128]{1,0:T(8,128)(2,1)S(1)} %convert_add_fusion.1), channel_id=1, source_target_pairs={{0,8},{4,12},{8,0},{12,4},{1,9},{5,13},{9,1},{13,5},{2,10},{6,14},... | collective-permute-start | bytes 92168 | tf_op jit(solution)/shard_map/ppermute | solution.py:392
  66.6 1.1 %collective-permute-start.15 = (bf16[120,128]{1,0:T(8,128)(2,1)S(1)}, bf16[120,128]{1,0:T(8,128)(2,1)S(1)}, u32[]{:S(2)}, u32[]{:S(2)}) collective-permute-start(bf16[120,128]{1,0:T(8,128)(2,1)S(1)} %convert_add_fusion.1), channel_id=1, source_target_pairs={{0,12},{4,0},{8,4},{12,8},{1,13},{5,1},{9,5},{13,9},{2,14},{6,2},{... | collective-permute-start | bytes 92168 | tf_op jit(solution)/shard_map/ppermute | solution.py:392
  67.7 0.4 collective-permute-start.17
  68.0 1.5 %collective-permute-done.16 = bf16[120,128]{1,0:T(8,128)(2,1)S(1)} collective-permute-done((bf16[120,128]{1,0:T(8,128)(2,1)S(1)}, bf16[120,128]{1,0:T(8,128)(2,1)S(1)}, u32[]{:S(2)}, u32[]{:S(2)}) %collective-permute-start.16) | collective-permute-done | bytes 30752 | tf_op jit(solution)/shard_map/ppermute | solution.py:392
  69.6 0.1 collective-permute-done.15
  69.7 2.5 %collective-permute-done.17 = bf16[120,128]{1,0:T(8,128)(2,1)S(1)} collective-permute-done((bf16[120,128]{1,0:T(8,128)(2,1)S(1)}, bf16[120,128]{1,0:T(8,128)(2,1)S(1)}, u32[]{:S(2)}, u32[]{:S(2)}) %collective-permute-start.17) | collective-permute-done | bytes 30752 | tf_op jit(solution)/shard_map/ppermute | solution.py:392
  72.2 6.4 %collective-permute-start.18 = (bf16[4,120,128]{2,1,0:T(8,128)(2,1)S(1)}, bf16[4,120,128]{2,1,0:T(8,128)(2,1)S(1)}, u32[]{:S(2)}, u32[]{:S(2)}) collective-permute-start(bf16[4,120,128]{2,1,0:T(8,128)(2,1)S(1)} %pad_maximum_fusion.mine), channel_id=1, source_target_pairs={{0,2},{2,0},{1,3},{3,1},{4,6},{6,4},{5,7},{7,5},{8,10},{10,8},{9,1... | collective-permute-start | bytes 368648 | tf_op jit(solution)/shard_map/ppermute | solution.py:488
  78.6 1.0 %collective-permute-done.18.other = bf16[4,120,128]{2,1,0:T(8,128)(2,1)S(1)} collective-permute-done((bf16[4,120,128]{2,1,0:T(8,128)(2,1)S(1)}, bf16[4,120,128]{2,1,0:T(8,128)(2,1)S(1)}, u32[]{:S(2)}, u32[]{:S(2)}) %collective-permute-start.18) | collective-permute-done | bytes 122912 | tf_op jit(solution)/shard_map/ppermute | solution.py:488
  79.6 1.0 %last.1 = (f32[64,1536]{1,0:T(8,128)}, f32[8,2,1536]{2,1,0:T(2,128)}) custom-call(bf16[4,120,128]{2,1,0:T(8,128)(2,1)S(1)} %pad_maximum_fusion.mine, bf16[4,120,128]{2,1,0:T(8,128)(2,1)S(1)} %collective-permute-done.18.other, bf16[64,1536]{1,0:T(8,128)(2,1)S(1)} %bitcast.30), custom_call_target="tpu_custom_call" | custom-call | flops 10000000 | bytes 1000000 | tf_op jit(solution)/shard_map/last/pallas_call | solution.py:490
  (44 shorter events, 0.9 us)
Async XLA Ops:
  0.6 15.3 %copy-start.5 = (bf16[9,512,16]{1,2,0:T(8,128)(2,1)S(1)}, bf16[9,512,16]{1,2,0:T(8,128)(2,1)}, u32[]{:S(2)}) copy-start(bf16[9,512,16]{1,2,0:T(8,128)(2,1)} %param.11) | copy-start | bytes 442372
  1.4 14.5 %collective-permute-start.1 = (bf16[4,16,128]{2,1,0:T(8,128)(2,1)S(1)}, bf16[4,16,128]{2,1,0:T(8,128)(2,1)S(1)}, u32[]{:S(2)}, u32[]{:S(2)}) collective-permute-start(bf16[4,16,128]{2,1,0:T(8,128)(2,1)S(1)} %get-tuple-element.44), channel_id=1, source_target_pairs={{2,0},{4,2},{6,4},{8,6},{10,8},{12,10},{14,12},{16,14},{18,16},{20... | collective-permute-start | bytes 49160 | tf_op jit(solution)/shard_map/ppermute | solution.py:413
  4.8 11.2 %collective-permute-start = (bf16[4,16,128]{2,1,0:T(8,128)(2,1)S(1)}, bf16[4,16,128]{2,1,0:T(8,128)(2,1)S(1)}, u32[]{:S(2)}, u32[]{:S(2)}) collective-permute-start(bf16[4,16,128]{2,1,0:T(8,128)(2,1)S(1)} %get-tuple-element.45), channel_id=1, source_target_pairs={{0,2},{2,4},{4,6},{6,8},{8,10},{10,12},{12,14},{14,16},{16,18},{18... | collective-permute-start | bytes 49160 | tf_op jit(solution)/shard_map/ppermute | solution.py:412
  6.4 25.2 %collective-permute-start.2 = (bf16[2,128,512]{2,1,0:T(8,128)(2,1)S(1)}, bf16[2,128,512]{2,1,0:T(8,128)(2,1)S(1)}, u32[]{:S(2)}, u32[]{:S(2)}) collective-permute-start(bf16[2,128,512]{2,1,0:T(8,128)(2,1)S(1)} %slice.16), channel_id=1, source_target_pairs={{0,2},{2,4},{4,6},{6,8},{8,10},{10,12},{12,14},{14,16},{16,18},{18... | collective-permute-start | bytes 786440 | tf_op jit(solution)/shard_map/ppermute | solution.py:415
  9.1 22.6 %slice-start = ((s8[4718592]{0:T(1024)(128)(4,1)}), s8[4194304]{0:T(1024)(128)(4,1)S(1)}, s32[]{:S(2)}) async-start(s8[4718592]{0:T(1024)(128)(4,1)} %bitcast.36), calls=%async_computation | async-start | bytes 8388608
  9.1 22.5 %collective-permute-start.3 = (bf16[2,128,512]{2,1,0:T(8,128)(2,1)S(1)}, bf16[2,128,512]{2,1,0:T(8,128)(2,1)S(1)}, u32[]{:S(2)}, u32[]{:S(2)}) collective-permute-start(bf16[2,128,512]{2,1,0:T(8,128)(2,1)S(1)} %slice.15), channel_id=1, source_target_pairs={{2,0},{4,2},{6,4},{8,6},{10,8},{12,10},{14,12},{16,14},{18,16},{20... | collective-permute-start | bytes 786440 | tf_op jit(solution)/shard_map/ppermute | solution.py:430
  15.9 11.3 %copy-start.7 = (bf16[80,256]{1,0:T(8,128)(2,1)S(1)}, bf16[80,256]{1,0:T(8,128)(2,1)}, u32[]{:S(2)}) copy-start(bf16[80,256]{1,0:T(8,128)(2,1)} %get-tuple-element.30) | copy-start | bytes 122884
  15.9 15.8 %slice-start.1 = ((s8[4718592]{0:T(1024)(128)(4,1)}), s8[524288]{0:T(1024)(128)(4,1)S(1)}, s32[]{:S(2)}) async-start(s8[4718592]{0:T(1024)(128)(4,1)} %bitcast.36), calls=%async_computation.1 | async-start | bytes 1048576
  16.0 15.7 %copy-start.6 = (f32[8]{0:T(128)S(1)}, f32[8]{0:T(128)}, u32[]{:S(2)}) copy-start(f32[8]{0:T(128)} %steps.1) | copy-start | bytes 100
  27.2 12.1 %collective-permute-start.4 = (bf16[80,256]{1,0:T(8,128)(2,1)S(1)}, bf16[80,256]{1,0:T(8,128)(2,1)S(1)}, u32[]{:S(2)}, u32[]{:S(2)}) collective-permute-start(bf16[80,256]{1,0:T(8,128)(2,1)S(1)} %copy-done.7), channel_id=1, source_target_pairs={{0,1},{1,0},{2,3},{3,2},{4,5},{5,4},{6,7},{7,6},{8,9},{9,8},{10,11... | collective-permute-start | bytes 122888 | tf_op jit(solution)/shard_map/ppermute | solution.py:453
  31.7 7.6 %copy-start = (bf16[256,1536]{1,0:T(8,128)(2,1)S(1)}, bf16[256,1536]{1,0:T(8,128)(2,1)}, u32[]{:S(2)}) copy-start(bf16[256,1536]{1,0:T(8,128)(2,1)} %hidden.5) | copy-start | bytes 2359300
  31.7 7.6 %copy-start.1 = (bf16[1536,64]{0,1:T(8,128)(2,1)S(1)}, bf16[1536,64]{0,1:T(8,128)(2,1)}, u32[]{:S(2)}) copy-start(bf16[1536,64]{0,1:T(8,128)(2,1)} %param.17) | copy-start | bytes 589828
  31.7 7.6 %copy-start.2 = (bf16[16,2,1536]{2,1,0:T(2,128)(2,1)S(1)}, bf16[16,2,1536]{2,1,0:T(2,128)(2,1)}, u32[]{:S(2)}) copy-start(bf16[16,2,1536]{2,1,0:T(2,128)(2,1)} %mod.5) | copy-start | bytes 294916
  31.8 7.6 %copy-start.3 = (f32[80,256]{1,0:T(8,128)S(1)}, f32[80,256]{1,0:T(8,128)}, u32[]{:S(2)}) copy-start(f32[80,256]{1,0:T(8,128)} %get-tuple-element.29.stats) | copy-start | bytes 245764
  31.8 7.6 %copy-start.4 = (s32[8]{0:T(128)S(1)}, s32[8]{0:T(128)}, u32[]{:S(2)}) copy-start(s32[8]{0:T(128)} %prompts.5) | copy-start | bytes 100
  40.6 9.1 %collective-permute-start.5 = (bf16[480,128]{1,0:T(8,128)(2,1)S(1)}, bf16[480,128]{1,0:T(8,128)(2,1)S(1)}, u32[]{:S(2)}, u32[]{:S(2)}) collective-permute-start(bf16[480,128]{1,0:T(8,128)(2,1)S(1)} %get-tuple-element.32), channel_id=1, source_target_pairs={{0,2},{2,0},{1,3},{3,1},{4,6},{6,4},{5,7},{7,5},{8,10},{10,8},{9,1... | collective-permute-start | bytes 368648 | tf_op jit(solution)/shard_map/ppermute | solution.py:486
  49.7 3.9 %collective-permute-start.8 = (bf16[120,128]{1,0:T(8,128)(2,1)S(1)}, bf16[120,128]{1,0:T(8,128)(2,1)S(1)}, u32[]{:S(2)}, u32[]{:S(2)}) collective-permute-start(bf16[120,128]{1,0:T(8,128)(2,1)S(1)} %get-tuple-element.41), channel_id=1, source_target_pairs={{0,12},{4,0},{8,4},{12,8},{1,13},{5,1},{9,5},{13,9},{2,14},{6,2},{... | collective-permute-start | bytes 92168 | tf_op jit(solution)/shard_map/ppermute | solution.py:375
  49.8 3.8 %collective-permute-start.7 = (bf16[120,128]{1,0:T(8,128)(2,1)S(1)}, bf16[120,128]{1,0:T(8,128)(2,1)S(1)}, u32[]{:S(2)}, u32[]{:S(2)}) collective-permute-start(bf16[120,128]{1,0:T(8,128)(2,1)S(1)} %get-tuple-element.42), channel_id=1, source_target_pairs={{0,8},{4,12},{8,0},{12,4},{1,9},{5,13},{9,1},{13,5},{2,10},{6,14},... | collective-permute-start | bytes 92168 | tf_op jit(solution)/shard_map/ppermute | solution.py:375
  49.9 5.1 %collective-permute-start.6 = (bf16[120,128]{1,0:T(8,128)(2,1)S(1)}, bf16[120,128]{1,0:T(8,128)(2,1)S(1)}, u32[]{:S(2)}, u32[]{:S(2)}) collective-permute-start(bf16[120,128]{1,0:T(8,128)(2,1)S(1)} %get-tuple-element.43), channel_id=1, source_target_pairs={{0,4},{4,8},{8,12},{12,0},{1,5},{5,9},{9,13},{13,1},{2,6},{6,10},{... | collective-permute-start | bytes 92168 | tf_op jit(solution)/shard_map/ppermute | solution.py:375
  55.1 2.8 %collective-permute-start.11 = (bf16[120,128]{1,0:T(8,128)(2,1)S(1)}, bf16[120,128]{1,0:T(8,128)(2,1)S(1)}, u32[]{:S(2)}, u32[]{:S(2)}) collective-permute-start(bf16[120,128]{1,0:T(8,128)(2,1)S(1)} %get-tuple-element.39), channel_id=1, source_target_pairs={{0,48},{16,0},{32,16},{48,32},{1,49},{17,1},{33,17},{49,33},{2,50}... | collective-permute-start | bytes 92168 | tf_op jit(solution)/shard_map/ppermute | solution.py:385
  55.1 4.3 %collective-permute-start.10 = (bf16[120,128]{1,0:T(8,128)(2,1)S(1)}, bf16[120,128]{1,0:T(8,128)(2,1)S(1)}, u32[]{:S(2)}, u32[]{:S(2)}) collective-permute-start(bf16[120,128]{1,0:T(8,128)(2,1)S(1)} %get-tuple-element.39), channel_id=1, source_target_pairs={{0,32},{16,48},{32,0},{48,16},{1,33},{17,49},{33,1},{49,17},{2,34}... | collective-permute-start | bytes 92168 | tf_op jit(solution)/shard_map/ppermute | solution.py:385
  55.2 5.0 %collective-permute-start.9 = (bf16[120,128]{1,0:T(8,128)(2,1)S(1)}, bf16[120,128]{1,0:T(8,128)(2,1)S(1)}, u32[]{:S(2)}, u32[]{:S(2)}) collective-permute-start(bf16[120,128]{1,0:T(8,128)(2,1)S(1)} %get-tuple-element.39), channel_id=1, source_target_pairs={{0,16},{16,32},{32,48},{48,0},{1,17},{17,33},{33,49},{49,1},{2,18}... | collective-permute-start | bytes 92168 | tf_op jit(solution)/shard_map/ppermute | solution.py:385
  60.3 2.8 %collective-permute-start.14 = (bf16[120,128]{1,0:T(8,128)(2,1)S(1)}, bf16[120,128]{1,0:T(8,128)(2,1)S(1)}, u32[]{:S(2)}, u32[]{:S(2)}) collective-permute-start(bf16[120,128]{1,0:T(8,128)(2,1)S(1)} %fusion.5), channel_id=1, source_target_pairs={{0,192},{64,0},{128,64},{192,128},{1,193},{65,1},{129,65},{193,129... | collective-permute-start | bytes 92168 | tf_op jit(solution)/shard_map/ppermute | solution.py:385
  60.4 4.3 %collective-permute-start.13 = (bf16[120,128]{1,0:T(8,128)(2,1)S(1)}, bf16[120,128]{1,0:T(8,128)(2,1)S(1)}, u32[]{:S(2)}, u32[]{:S(2)}) collective-permute-start(bf16[120,128]{1,0:T(8,128)(2,1)S(1)} %fusion.5), channel_id=1, source_target_pairs={{0,128},{64,192},{128,0},{192,64},{1,129},{65,193},{129,1},{193,65... | collective-permute-start | bytes 92168 | tf_op jit(solution)/shard_map/ppermute | solution.py:385
  60.5 5.0 %collective-permute-start.12 = (bf16[120,128]{1,0:T(8,128)(2,1)S(1)}, bf16[120,128]{1,0:T(8,128)(2,1)S(1)}, u32[]{:S(2)}, u32[]{:S(2)}) collective-permute-start(bf16[120,128]{1,0:T(8,128)(2,1)S(1)} %fusion.5), channel_id=1, source_target_pairs={{0,64},{64,128},{128,192},{192,0},{1,65},{65,129},{129,193},{193,1... | collective-permute-start | bytes 92168 | tf_op jit(solution)/shard_map/ppermute | solution.py:385
  65.5 4.0 %collective-permute-start.16 = (bf16[120,128]{1,0:T(8,128)(2,1)S(1)}, bf16[120,128]{1,0:T(8,128)(2,1)S(1)}, u32[]{:S(2)}, u32[]{:S(2)}) collective-permute-start(bf16[120,128]{1,0:T(8,128)(2,1)S(1)} %convert_add_fusion.1), channel_id=1, source_target_pairs={{0,8},{4,12},{8,0},{12,4},{1,9},{5,13},{9,1},{13,5},{2,10},{6,14},... | collective-permute-start | bytes 92168 | tf_op jit(solution)/shard_map/ppermute | solution.py:392
  66.6 3.1 %collective-permute-start.15 = (bf16[120,128]{1,0:T(8,128)(2,1)S(1)}, bf16[120,128]{1,0:T(8,128)(2,1)S(1)}, u32[]{:S(2)}, u32[]{:S(2)}) collective-permute-start(bf16[120,128]{1,0:T(8,128)(2,1)S(1)} %convert_add_fusion.1), channel_id=1, source_target_pairs={{0,12},{4,0},{8,4},{12,8},{1,13},{5,1},{9,5},{13,9},{2,14},{6,2},{... | collective-permute-start | bytes 92168 | tf_op jit(solution)/shard_map/ppermute | solution.py:392
  67.7 4.5 %collective-permute-start.17 = (bf16[120,128]{1,0:T(8,128)(2,1)S(1)}, bf16[120,128]{1,0:T(8,128)(2,1)S(1)}, u32[]{:S(2)}, u32[]{:S(2)}) collective-permute-start(bf16[120,128]{1,0:T(8,128)(2,1)S(1)} %convert_add_fusion.1), channel_id=1, source_target_pairs={{0,4},{4,8},{8,12},{12,0},{1,5},{5,9},{9,13},{13,1},{2,6},{6,10},{... | collective-permute-start | bytes 92168 | tf_op jit(solution)/shard_map/ppermute | solution.py:392
  72.2 7.4 %collective-permute-start.18 = (bf16[4,120,128]{2,1,0:T(8,128)(2,1)S(1)}, bf16[4,120,128]{2,1,0:T(8,128)(2,1)S(1)}, u32[]{:S(2)}, u32[]{:S(2)}) collective-permute-start(bf16[4,120,128]{2,1,0:T(8,128)(2,1)S(1)} %pad_maximum_fusion.mine), channel_id=1, source_target_pairs={{0,2},{2,0},{1,3},{3,1},{4,6},{6,4},{5,7},{7,5},{8,10},{10,8},{9,1... | collective-permute-start | bytes 368648 | tf_op jit(solution)/shard_map/ppermute | solution.py:488
